TPU v7x, 32 devices: a whole 2x2x4 slice. The times are simulated.
32 devices in a mesh: space: 4 (over y, core), band: 8 (over z, x).
Axes of the slice: x: 2, y: 2, z: 4, core: 2. Of those that a mesh axis runs over, the one named last changes fastest.
Arguments:
- orbitals: float32 [64, 48, 16, 128], P('band', 'space'), may hold values from -12 to 12
- potential: float32 [48, 16, 128], P('space'), may hold values from -2 to 2
Outputs:
- filtered: float32 [64, 48, 16, 128], P('band', 'space')
- intersection: float32 [64, 64], P('band')
- projected: float32 [64, 64], P('band')
All inputs are finite; a program needn't handle non-finite values.
Results may differ from a plain program's by a relative error of at most 0.0003.
Values may be sent and summed in bfloat16 or wider, within the bound.
No kernel may reach another device: no remote copies, remote signals or barrier semaphores. Data moves between devices by JAX's collectives and lax.ppermute only.
A program may use at most 128 MiB of HBM per device.

v0:
```python
import jax
import jax.numpy as jnp
from jax import lax
from jax.sharding import PartitionSpec as P

STENCIL = (
    -5369.0 / 1800.0,
    12.0 / 7.0,
    -15.0 / 56.0,
    10.0 / 189.0,
    -1.0 / 112.0,
    2.0 / 1925.0,
    -1.0 / 16632.0,
)


def padded_2(cells, sides, width):
    for axis, dim in sides:
        count = lax.axis_size(axis)
        head = lax.slice_in_dim(cells, 0, width, axis=dim)
        tail = lax.slice_in_dim(cells, cells.shape[dim] - width, cells.shape[dim], axis=dim)
        cells = jnp.concatenate(
            [
                lax.ppermute(tail, axis, [(i, (i + 1) % count) for i in range(count)]),
                cells,
                lax.ppermute(head, axis, [((i + 1) % count, i) for i in range(count)]),
            ],
            axis=dim,
        )
    return cells


def padded_laplace(padded):
    interior = padded.shape[1] - 12
    center = padded[:, 6 : 6 + interior]
    summed = 3.0 * STENCIL[0] * center
    for offset in range(1, 7):
        factor = STENCIL[offset]
        summed = summed + factor * (jnp.roll(center, offset, 2) + jnp.roll(center, -offset, 2))
        summed = summed + factor * (jnp.roll(center, offset, 3) + jnp.roll(center, -offset, 3))
        summed = summed + factor * (
            padded[:, 6 + offset : 6 + offset + interior]
            + padded[:, 6 - offset : 6 - offset + interior]
        )
    return (summed, center)


def hamiltonian(padded, potential):
    summed, center = padded_laplace(padded)
    return (-0.5 * summed + potential * center, center)


def filter_step(padded, potential):
    applied, center = hamiltonian(padded, potential)
    return (applied - 9.0 * center) * 0.125


def planes(field):
    return padded_2(field, (("space", 1),), 6)


def local(orbitals, potential):
    first = filter_step(planes(orbitals), potential)
    second = 2.0 * filter_step(planes(first), potential) - orbitals
    beside_all = padded_2(second.astype(jnp.bfloat16), (("space", 1),), 6).astype(second.dtype)
    applied, unused_center = hamiltonian(beside_all, potential)
    count = second.shape[0]
    narrow = second.astype(jnp.bfloat16).reshape(count, -1)
    narrow_applied = applied.astype(jnp.bfloat16).reshape(count, -1)
    contract = (((1,), (1,)), ((), ()))
    piece = lax.all_gather(narrow, "band", axis=0, tiled=True)
    intersection_part = lax.dot_general(narrow, piece, contract, preferred_element_type=jnp.float32)
    project_part = lax.dot_general(
        narrow_applied, piece, contract, preferred_element_type=jnp.float32
    )
    intersection_rows = intersection_part
    project_rows = project_part
    intersection_rows, project_rows = (intersection_rows, project_rows)
    intersection_rows, project_rows = lax.psum((intersection_rows, project_rows), "space")
    inverse = 1.0 / (narrow.shape[1] * lax.axis_size("space"))
    return (second, intersection_rows * inverse, project_rows * inverse)


def solution(mesh):
    return jax.shard_map(
        local,
        mesh=mesh,
        in_specs=(P("band", "space", None, None), P("space", None, None)),
        out_specs=(P("band", "space", None, None), P("band", None), P("band", None)),
        check_vma=False,
    )
```

profile of v0, /device:TPU:0, one launch (start us, length us, event | category | flops | bytes accessed | tf_op | source)
XLA Modules:
  0.0 180.2 jit_solution(10736552041778930613)
XLA Ops:
  7.2 1.2 fusion.215
  9.0 2.0 %collective-permute-start = (f32[8,6,16,128]{3,2,1,0:T(8,128)S(1)}, f32[8,6,16,128]{3,2,1,0:T(8,128)S(1)}, u32[]{:S(2)}, u32[]{:S(2)}) collective-permute-start(f32[8,6,16,128]{3,2,1,0:T(8,128)S(1)} %get-tuple-element.155), channel_id=1, source_target_pairs={{8,0},{16,8},{24,16},{0,24},{9,1},{17,9},{25,17},{1,25},{10,2},{18... | collective-permute-start | bytes 1179656 | tf_op jit(solution)/shard_map/ppermute | solution.py:26
  11.8 1.2 fusion.197
  13.0 1.4 fusion.198
  14.4 1.3 fusion.200
  15.7 1.4 fusion.201
  17.1 1.4 fusion.202
  18.5 1.3 fusion.204
  19.8 1.4 fusion.205
  21.2 1.5 fusion.206
  22.7 1.3 fusion.208
  24.0 1.4 fusion.209
  25.4 1.5 fusion.210
  26.8 1.3 fusion.212
  28.1 1.4 fusion.213
  29.5 1.4 fusion.214
  31.7 0.9 fusion.211
  33.5 0.8 fusion.203
  36.6 11.7 %broadcast_multiply_fusion = (f32[8,12,16,128]{3,2,1,0:T(8,128)S(1)}, f32[8,12,16,128]{3,2,1,0:T(8,128)}) fusion(f32[8,12,16,128]{3,2,1,0:T(8,128)S(1)} %copy-done, f32[12,16,128]{2,1,0:T(8,128)} %param.3, f32[8,18,16,128]{3,2,1,0:T(8,128)S(1)} %get-tuple-element.158, f32[8,18,16,128]{3,2,1,0:T(8,128)S(1)} %constant_dynamic-update-slice_fusion, ...), kind=kLoop, calls=%fused_computation.210 | loop fusion | flops 16711680 | bytes 30769152 | tf_op jit(solution)/shard_map/mul | solution.py:55
  49.1 1.4 fusion.167
  50.5 1.4 fusion.168
  51.8 1.4 fusion.169
  53.3 1.3 fusion.171
  54.5 1.4 fusion.172
  55.9 1.4 fusion.173
  57.4 1.3 fusion.175
  58.7 1.4 fusion.176
  60.1 1.4 fusion.177
  61.5 1.3 fusion.179
  62.8 1.4 fusion.180
  64.2 1.4 fusion.181
  65.6 1.3 fusion.183
  67.0 1.4 fusion.184
  68.4 1.0 fusion.182
  69.4 1.0 fusion.186
  70.3 0.8 fusion.174
  74.1 1.4 fusion.185
  75.5 6.4 %collective-permute-done.2 = f32[8,6,16,128]{3,2,1,0:T(8,128)S(1)} collective-permute-done((f32[8,6,16,128]{3,2,1,0:T(8,128)S(1)}, f32[8,6,16,128]{3,2,1,0:T(8,128)S(1)}, u32[]{:S(2)}, u32[]{:S(2)}) %collective-permute-start.2) | collective-permute-done | bytes 393248 | tf_op jit(solution)/shard_map/ppermute | solution.py:26
  81.9 2.8 %collective-permute-done.3 = f32[8,6,16,128]{3,2,1,0:T(8,128)S(1)} collective-permute-done((f32[8,6,16,128]{3,2,1,0:T(8,128)S(1)}, f32[8,6,16,128]{3,2,1,0:T(8,128)S(1)}, u32[]{:S(2)}, u32[]{:S(2)}) %collective-permute-start.3) | collective-permute-done | bytes 393248 | tf_op jit(solution)/shard_map/ppermute | solution.py:24
  85.5 13.5 %fusion.139 = (bf16[8,12,16,128]{3,2,1,0:T(8,128)(2,1)S(1)}, f32[8,12,16,128]{3,2,1,0:T(8,128)}) fusion(f32[8,12,16,128]{3,2,1,0:T(8,128)S(1)} %copy-done, f32[8,12,16,128]{3,2,1,0:T(8,128)} %get-tuple-element.8, f32[12,16,128]{2,1,0:T(8,128)} %broadcast_multiply_fusion.1, f32[8,12,16,128]{3,2,1,0:T(8,128)S(1)} %get-tuple-element.7, ...), kind=kLoop, calls=%fused_computation.219 | loop fusion | flops 19464192 | bytes 23298048 | tf_op jit(solution)/shard_map/convert_element_type | solution.py:68
  99.4 1.5 collective-permute-start.5
  100.9 1.0 copy.13
  101.9 3.4 %collective-permute-done.4 = bf16[8,6,16,128]{3,2,1,0:T(8,128)(2,1)S(1)} collective-permute-done((bf16[8,6,16,128]{3,2,1,0:T(8,128)(2,1)S(1)}, bf16[8,6,16,128]{3,2,1,0:T(8,128)(2,1)S(1)}, u32[]{:S(2)}, u32[]{:S(2)}) %collective-permute-start.4) | collective-permute-done | bytes 196640 | tf_op jit(solution)/shard_map/ppermute | solution.py:24
  106.0 1.0 fusion.145
  107.0 1.0 fusion.149
  108.0 0.8 fusion.153
  108.8 0.8 fusion.157
  112.0 1.4 fusion.150
  113.4 1.4 fusion.151
  114.8 1.3 fusion.152
  116.1 1.4 fusion.154
  117.6 1.4 fusion.155
  119.0 1.3 fusion.156
  120.3 1.4 fusion.158
  121.7 1.5 fusion.159
  123.1 1.3 fusion.160
  124.4 1.4 fusion.162
  125.8 1.5 fusion.163
  127.3 1.3 fusion.164
  128.6 11.3 %fusion.45 = bf16[8,12,16,128]{3,2,1,0:T(8,128)(2,1)} fusion(f32[8,24,16,128]{3,2,1,0:T(8,128)S(1)} %maximum_convert_fusion, f32[8,12,15,128]{3,2,1,0:T(8,128)} %get-tuple-element.54, f32[8,12,1,128]{3,2,1,0:T(1,128)} %get-tuple-element.56, f32[8,12,1,128]{3,2,1,0:T(1,128)S(1)} %get-tuple-element.55, f32[8,12,15,128]{3,2,1,0:T(8,128)} %get-tuple-element.53, ...), kind=kLoop, calls=%fused_computation.66 | loop fusion | flops 16318464 | bytes 29589504 | tf_op jit(solution)/shard_map/convert_element_type | solution.py:69
  139.8 23.1 %all-gather.2.cloned.1.call-done = bf16[64,24576]{1,0:T(8,128)(2,1)} async-done(((bf16[8,24576]{1,0:T(8,128)(2,1)}), bf16[64,24576]{1,0:T(8,128)(2,1)}) %all-gather.2.cloned.1.call-update) | async-done | bytes 3145744 | tf_op jit(solution)/shard_map/all_gather | solution.py:71
  163.0 2.9 %fusion.138 = f32[8,64]{1,0:T(8,128)S(1)} fusion(bf16[64,24576]{1,0:T(8,128)(2,1)} %all-gather.2.cloned.1.call-done, bf16[1,8,192,128]{3,2,1,0:T(8,128)(2,1)S(1)} %bitcast.14), kind=kOutput, calls=%fused_computation.218 | convolution fusion | flops 25165824 | bytes 3540992 | tf_op jit(solution)/shard_map/dot_general | solution.py:72
  165.9 1.0 fusion.135
  166.9 5.8 %all-reduce = (f32[8,64]{1,0:T(8,128)S(1)}, f32[8,64]{1,0:T(8,128)S(1)}) all-reduce(f32[8,64]{1,0:T(8,128)S(1)} %fusion.138, f32[8,64]{1,0:T(8,128)S(1)} %fusion.135), channel_id=1, replica_groups=mesh['space'=4,'band'=8] {'space'}, use_global_device_ids=true, to_apply=%region_0.1 | all-reduce | flops 1024 | bytes 8192 | tf_op jit(solution)/shard_map/psum | solution.py:79
  (51 shorter events, 13.7 us)
Async XLA Ops:
  7.2 3.8 %copy-start = (f32[8,12,16,128]{3,2,1,0:T(8,128)S(1)}, f32[8,12,16,128]{3,2,1,0:T(8,128)}, u32[]{:S(2)}) copy-start(f32[8,12,16,128]{3,2,1,0:T(8,128)} %param.2) | copy-start | bytes 2359300
  7.2 155.8 %all-gather.2.cloned.1.call-start = ((), (), s32[]{:S(2)}) async-start(), calls=%async_computation | async-start | bytes 3538944 | tf_op jit(solution)/shard_map/all_gather | solution.py:71
  8.5 27.9 %collective-permute-start.1 = (f32[8,6,16,128]{3,2,1,0:T(8,128)S(1)}, f32[8,6,16,128]{3,2,1,0:T(8,128)S(1)}, u32[]{:S(2)}, u32[]{:S(2)}) collective-permute-start(f32[8,6,16,128]{3,2,1,0:T(8,128)S(1)} %get-tuple-element.156), channel_id=1, source_target_pairs={{0,8},{8,16},{16,24},{24,0},{1,9},{9,17},{17,25},{25,1},{2,10},{10... | collective-permute-start | bytes 1179656 | tf_op jit(solution)/shard_map/ppermute | solution.py:24
  9.0 27.6 %collective-permute-start = (f32[8,6,16,128]{3,2,1,0:T(8,128)S(1)}, f32[8,6,16,128]{3,2,1,0:T(8,128)S(1)}, u32[]{:S(2)}, u32[]{:S(2)}) collective-permute-start(f32[8,6,16,128]{3,2,1,0:T(8,128)S(1)} %get-tuple-element.155), channel_id=1, source_target_pairs={{8,0},{16,8},{24,16},{0,24},{9,1},{17,9},{25,17},{1,25},{10,2},{18... | collective-permute-start | bytes 1179656 | tf_op jit(solution)/shard_map/ppermute | solution.py:26
  31.7 4.0 %copy-start.3 = (f32[12,16,128]{2,1,0:T(8,128)S(1)}, f32[12,16,128]{2,1,0:T(8,128)}, u32[]{:S(2)}) copy-start(f32[12,16,128]{2,1,0:T(8,128)} %param.3) | copy-start | bytes 294916
  72.8 9.2 %collective-permute-start.2 = (f32[8,6,16,128]{3,2,1,0:T(8,128)S(1)}, f32[8,6,16,128]{3,2,1,0:T(8,128)S(1)}, u32[]{:S(2)}, u32[]{:S(2)}) collective-permute-start(f32[8,6,16,128]{3,2,1,0:T(8,128)S(1)} %get-tuple-element.105), channel_id=1, source_target_pairs={{8,0},{16,8},{24,16},{0,24},{9,1},{17,9},{25,17},{1,25},{10,2},{18... | collective-permute-start | bytes 1179656 | tf_op jit(solution)/shard_map/ppermute | solution.py:26
  73.4 11.3 %collective-permute-start.3 = (f32[8,6,16,128]{3,2,1,0:T(8,128)S(1)}, f32[8,6,16,128]{3,2,1,0:T(8,128)S(1)}, u32[]{:S(2)}, u32[]{:S(2)}) collective-permute-start(f32[8,6,16,128]{3,2,1,0:T(8,128)S(1)} %get-tuple-element.106), channel_id=1, source_target_pairs={{0,8},{8,16},{16,24},{24,0},{1,9},{9,17},{17,25},{25,1},{2,10},{10... | collective-permute-start | bytes 1179656 | tf_op jit(solution)/shard_map/ppermute | solution.py:24
  81.9 2.8 %copy-start.4 = (f32[8,6,16,128]{3,2,1,0:T(8,128)}, f32[8,6,16,128]{3,2,1,0:T(8,128)S(1)}, u32[]{:S(2)}) copy-start(f32[8,6,16,128]{3,2,1,0:T(8,128)S(1)} %collective-permute-done.2) | copy-start | bytes 1179652
  84.7 0.8 copy-start.5
  99.1 6.3 %collective-permute-start.4 = (bf16[8,6,16,128]{3,2,1,0:T(8,128)(2,1)S(1)}, bf16[8,6,16,128]{3,2,1,0:T(8,128)(2,1)S(1)}, u32[]{:S(2)}, u32[]{:S(2)}) collective-permute-start(bf16[8,6,16,128]{3,2,1,0:T(8,128)(2,1)S(1)} %get-tuple-element.159), channel_id=1, source_target_pairs={{0,8},{8,16},{16,24},{24,0},{1,9},{9,17},{17,25},{25,1},{2,10},{10... | collective-permute-start | bytes 589832 | tf_op jit(solution)/shard_map/ppermute | solution.py:24
  99.4 6.0 %collective-permute-start.5 = (bf16[8,6,16,128]{3,2,1,0:T(8,128)(2,1)S(1)}, bf16[8,6,16,128]{3,2,1,0:T(8,128)(2,1)S(1)}, u32[]{:S(2)}, u32[]{:S(2)}) collective-permute-start(bf16[8,6,16,128]{3,2,1,0:T(8,128)(2,1)S(1)} %get-tuple-element.160), channel_id=1, source_target_pairs={{8,0},{16,8},{24,16},{0,24},{9,1},{17,9},{25,17},{1,25},{10,2},{18... | collective-permute-start | bytes 589832 | tf_op jit(solution)/shard_map/ppermute | solution.py:26
  139.8 26.1 %copy-start.2 = (bf16[8,12,16,128]{3,2,1,0:T(8,128)(2,1)S(1)}, bf16[8,12,16,128]{3,2,1,0:T(8,128)(2,1)}, u32[]{:S(2)}) copy-start(bf16[8,12,16,128]{3,2,1,0:T(8,128)(2,1)} %fusion.45) | copy-start | bytes 1179652
  163.0 3.0 %copy-start.1 = (bf16[64,24576]{1,0:T(8,128)(2,1)S(1)}, bf16[64,24576]{1,0:T(8,128)(2,1)}, u32[]{:S(2)}) copy-start(bf16[64,24576]{1,0:T(8,128)(2,1)} %all-gather.2.cloned.1.call-done) | copy-start | bytes 9437188
Sparse Core Ops, SparseCore 0:
  102.0 60.9 all-gather.1
where the time goes:
time: 180 us
  local copies, waits for them, and re-layouts  77.5 us (43%)
  other arithmetic  37.9 us (21%)
  waiting for transfers between devices  35.8 us (20%)
  between operations  14.2 us (8%)
  blocking collectives  5.83 us (3%)
  starting transfers between devices  5.04 us (3%)
  matrix products  3.9 us (2%)
    slice x24, local copies, waits for them, and re-layouts, padded_laplace(): jnp.roll(center, offset, 3) + jnp.roll(center, -offset, 3)  29.1 us
    all_gather x1, waiting for transfers between devices, local(): piece = lax.all_gather(narrow, 'band', axis=0, tiled=True)  23.1 us
    slice x24, local copies, waits for them, and re-layouts, padded_laplace(): jnp.roll(center, offset, 2) + jnp.roll(center, -offset, 2)  22 us
    convert_element_type x1, other arithmetic, local(): narrow = second.astype(jnp.bfloat16).reshape(count, -1)  13.5 us
    slice x12, local copies, waits for them, and re-layouts, padded_laplace(): jnp.roll(center, -offset, 3)  12.6 us
    mul x1, other arithmetic, filter_step(): return (applied - 9.0 * center) * 0.125  11.7 us
    convert_element_type x1, other arithmetic, local(): narrow_applied = applied.astype(jnp.bfloat16).reshape(count, -1)  11.3 us
    slice x12, local copies, waits for them, and re-layouts, padded_laplace(): jnp.roll(center, -offset, 2)  10.5 us
  transfers between devices with their start and end apart: 7, of which 4 were waited for; matrix products, arithmetic and copies ran while one was open for 35% of the time, Pallas kernels for 0%

commit v1 on v0

v1 whole, which is shorter than its diff:
```python
import functools

import jax
import jax.numpy as jnp
from jax import lax
from jax.experimental import pallas as pl
from jax.experimental.pallas import tpu as pltpu
from jax.sharding import PartitionSpec as P

STENCIL = (
    -5369.0 / 1800.0,
    12.0 / 7.0,
    -15.0 / 56.0,
    10.0 / 189.0,
    -1.0 / 112.0,
    2.0 / 1925.0,
    -1.0 / 16632.0,
)
WIDTH = 6
BF16 = jnp.bfloat16
F32 = jnp.float32
VMEM = pl.BlockSpec(memory_space=pltpu.VMEM)
PARAMS = pltpu.CompilerParams(vmem_limit_bytes=40 * 1024 * 1024)

GROUP = 8


def apply_row(load, center, where, nx, plane_rows, factors, diagonal):
    results = []
    for x in range(nx):
        here = center[x]
        total = diagonal(x) * here
        for k in range(1, WIDTH + 1):
            near = load(where + k * plane_rows + x * GROUP) + load(where - k * plane_rows + x * GROUP)
            near = near + (center[(x + k) % nx] + center[(x - k) % nx])
            near = near + (pltpu.roll(here, k, 1) + pltpu.roll(here, here.shape[1] - k, 1))
            total = total + factors[k - 1] * near
        results.append(total)
    return results


def loader(ref):
    def load(row):
        return ref[pl.ds(pl.multiple_of(row, GROUP), GROUP), :]

    return load


L_FACTORS = tuple(-0.0625 * c for c in STENCIL[1:])
L_CENTER = (-1.5 * STENCIL[0] - 9.0) / 8.0
H_FACTORS = tuple(-0.5 * c for c in STENCIL[1:])
H_CENTER = -1.5 * STENCIL[0]


def prepare_kernel(planes, nx, orbitals_ref, potential_ref, own_ref, left_ref, right_ref):
    rows = planes * nx
    plane_rows = nx * GROUP

    @pl.loop(0, rows // 2, unroll=8)
    def _(pair):
        row = pair * 2
        both = jnp.concatenate(
            [
                orbitals_ref[pl.ds(row, GROUP, stride=rows), :],
                orbitals_ref[pl.ds(row + 1, GROUP, stride=rows), :],
            ],
            axis=0,
        )
        at = pl.ds(pl.multiple_of(row * GROUP, 2 * GROUP), 2 * GROUP)
        own_ref[at, :] = both
        high = both.astype(BF16)
        left_ref[at, :] = high
        right_ref[at, :] = high

    extra = planes * plane_rows
    for out_ref, plane in ((left_ref, 0), (right_ref, planes - 1)):
        for x in range(0, nx, 2):
            block = own_ref[pl.ds(plane * plane_rows + x * GROUP, 2 * GROUP), :]
            low = block - block.astype(BF16).astype(F32)
            out_ref[pl.ds(extra + x * GROUP, 2 * GROUP), :] = low.astype(BF16)
    extra += plane_rows
    for out_ref, first, nearest in ((left_ref, 0, 0), (right_ref, planes - WIDTH, planes - 2)):
        for i in range(WIDTH):
            block = potential_ref[pl.ds((first + i) * nx, nx), :]
            out_ref[pl.ds(extra + i * nx, nx), :] = block.astype(BF16)
        for i in range(2):
            block = potential_ref[pl.ds((nearest + i) * nx, nx), :]
            low = block - block.astype(BF16).astype(F32)
            out_ref[pl.ds(extra + (WIDTH + i) * nx, nx), :] = low.astype(BF16)


def two_steps_kernel(
    planes, nx, own_ref, potential_ref, from_left_ref, from_right_ref,
    second_ref, filtered_ref, to_left_ref, to_right_ref, field, first, levels,
):
    plane_rows = nx * GROUP
    rows = planes * nx
    size = planes * plane_rows
    field[pl.ds(size, size), :] = own_ref[...]
    field[pl.ds(0, size), :] = from_left_ref[pl.ds(0, size), :].astype(F32)
    field[pl.ds(2 * size, size), :] = from_right_ref[pl.ds(0, size), :].astype(F32)
    for plane, ref in ((planes - 1, from_left_ref), (2 * planes, from_right_ref)):
        at = pl.ds(plane * plane_rows, plane_rows)
        field[at, :] = field[at, :] + ref[pl.ds(size, plane_rows), :].astype(F32)
    extra = size + plane_rows
    side = WIDTH * nx
    levels[pl.ds(side, rows), :] = potential_ref[...]
    for plane, nearest, ref in ((0, WIDTH - 2, from_left_ref), (WIDTH + planes, WIDTH + planes, from_right_ref)):
        levels[pl.ds(plane * nx, side), :] = ref[pl.ds(extra, side), :].astype(F32)
        at = pl.ds(nearest * nx, 2 * nx)
        levels[at, :] = levels[at, :] + ref[pl.ds(extra + side, 2 * nx), :].astype(F32)

    def diagonal(plane):
        def at(x):
            row = levels[pl.ds(plane * nx + x, 1), :]
            return jnp.broadcast_to(0.125 * row + L_CENTER, (GROUP, row.shape[1]))

        return at

    load = loader(field)

    @pl.loop(0, planes + 2 * WIDTH)
    def _(plane):
        where = (plane + planes - WIDTH) * plane_rows
        center = [load(where + x * GROUP) for x in range(nx)]
        total = apply_row(load, center, where, nx, plane_rows, L_FACTORS, diagonal(plane))
        for x in range(nx):
            first[pl.ds(pl.multiple_of(plane * plane_rows + x * GROUP, GROUP), GROUP), :] = total[x]

    load_first = loader(first)

    def second_step(plane, halo_ref, halo_plane):
        where = (plane + WIDTH) * plane_rows
        center = [load_first(where + x * GROUP) for x in range(nx)]
        total = apply_row(load_first, center, where, nx, plane_rows, L_FACTORS, diagonal(plane + WIDTH))
        base = plane * plane_rows
        values = []
        for x in range(nx):
            value = 2.0 * total[x] - load(size + base + x * GROUP)
            second_ref[pl.ds(pl.multiple_of(base + x * GROUP, GROUP), GROUP), :] = value
            filtered_ref[pl.ds(plane * nx + x, GROUP, stride=rows), :] = value
            values.append(value)
        for x in range(0, nx, 2):
            at = pl.ds(pl.multiple_of(halo_plane * plane_rows + x * GROUP, 2 * GROUP), 2 * GROUP)
            halo_ref[at, :] = jnp.concatenate(values[x : x + 2], axis=0).astype(BF16)

    @pl.loop(0, WIDTH)
    def _(plane):
        second_step(plane, to_left_ref, plane)

    @pl.loop(0, WIDTH)
    def _(plane):
        second_step(plane + planes - WIDTH, to_right_ref, plane)


def applied_kernel(planes, nx, second_ref, potential_ref, from_left_ref, from_right_ref, out_ref, field):
    plane_rows = nx * GROUP
    size = planes * plane_rows
    side = WIDTH * plane_rows
    field[pl.ds(side, size), :] = second_ref[...]
    field[pl.ds(0, side), :] = from_left_ref[...].astype(F32)
    field[pl.ds(side + size, side), :] = from_right_ref[...].astype(F32)
    load = loader(field)

    @pl.loop(0, planes)
    def _(plane):
        where = (plane + WIDTH) * plane_rows

        def diagonal(x):
            row = potential_ref[pl.ds(plane * nx + x, 1), :]
            return jnp.broadcast_to(row + H_CENTER, (GROUP, row.shape[1]))

        center = [load(where + x * GROUP) for x in range(nx)]
        total = apply_row(load, center, where, nx, plane_rows, H_FACTORS, diagonal)
        for x in range(nx):
            at = pl.multiple_of((plane * nx + x) * 2 * GROUP, 2 * GROUP)
            out_ref[pl.ds(at, 2 * GROUP), :] = jnp.concatenate([center[x], total[x]], axis=0).astype(BF16)


def gram_kernel(band, space, steps, in_ref, out_ref):
    width = 2 * GROUP
    total = jnp.zeros((band * width, band * width), F32)
    for step in range(0, steps, 2):
        block = jnp.concatenate(
            [in_ref[:, pl.ds((step + i) * width, width), :].reshape(band * width, -1) for i in range(2)],
            axis=1,
        )
        total = total + lax.dot_general(
            block, block, (((1,), (1,)), ((), ())), preferred_element_type=F32
        )
    lanes = lax.broadcasted_iota(jnp.int32, (GROUP, band * width), 1)
    for b in range(band):
        narrow = total[b * width : b * width + GROUP]
        applied = pltpu.roll(total[b * width + GROUP : (b + 1) * width], GROUP, 1)
        piece = jnp.where(lanes % width < GROUP, narrow, applied)
        for s in range(space):
            out_ref[s * band + b] = piece


def sum_kernel(scale, in_ref, intersection_ref, projected_ref):
    total = in_ref[0]
    for i in range(1, in_ref.shape[0]):
        total = total + in_ref[i]
    total = total * scale
    lanes, columns = total.shape[1], intersection_ref.shape[1]
    source = lax.broadcasted_iota(jnp.int32, (lanes, columns), 0)
    target = lax.broadcasted_iota(jnp.int32, (lanes, columns), 1)
    place = (target // GROUP) * (2 * GROUP) + target % GROUP
    for offset, ref in ((0, intersection_ref), (GROUP, projected_ref)):
        pick = jnp.where(source == place + offset, 1.0, 0.0).astype(F32)
        ref[...] = jnp.dot(total, pick, precision=lax.Precision.HIGHEST, preferred_element_type=F32)


def call(kernel, outs, *args, scratch=(), flops=1000000):
    return pl.pallas_call(
        kernel,
        out_shape=outs,
        in_specs=[VMEM] * len(args),
        out_specs=jax.tree.map(lambda _: VMEM, outs),
        scratch_shapes=list(scratch),
        compiler_params=PARAMS,
        cost_estimate=pl.CostEstimate(flops=flops, bytes_accessed=1000000, transcendentals=0),
    )(*args)


def shifts(axis):
    count = lax.axis_size(axis)
    up = [(i, (i + 1) % count) for i in range(count)]
    return up, [(j, i) for i, j in up]


def local_kernels(orbitals, potential):
    count, planes, nx, ny = orbitals.shape
    space, band = lax.axis_size("space"), lax.axis_size("band")
    rows = planes * nx
    plane_rows = nx * GROUP
    size = planes * plane_rows
    struct = jax.ShapeDtypeStruct
    levels = potential.reshape(rows, ny)
    up, down = shifts("space")

    message = struct((size + 2 * plane_rows, ny), BF16)
    own, to_left, to_right = call(
        functools.partial(prepare_kernel, planes, nx),
        (struct((size, ny), F32), message, message),
        orbitals.reshape(count * rows, ny), levels,
    )
    from_left = lax.ppermute(to_right, "space", up)
    from_right = lax.ppermute(to_left, "space", down)
    halo = struct((WIDTH * plane_rows, ny), BF16)
    second, filtered, to_left, to_right = call(
        functools.partial(two_steps_kernel, planes, nx),
        (struct((size, ny), F32), struct((count * rows, ny), F32), halo, halo),
        own, levels, from_left, from_right,
        scratch=[
            pltpu.VMEM((3 * size, ny), F32),
            pltpu.VMEM(((planes + 2 * WIDTH) * plane_rows, ny), F32),
            pltpu.VMEM(((planes + 2 * WIDTH) * nx, ny), F32),
        ],
    )
    from_left = lax.ppermute(to_right, "space", up)
    from_right = lax.ppermute(to_left, "space", down)
    pairs = call(
        functools.partial(applied_kernel, planes, nx),
        struct((rows * 2 * GROUP, ny), BF16),
        second, levels, from_left, from_right,
        scratch=[pltpu.VMEM(((planes + 2 * WIDTH) * plane_rows, ny), F32)],
    )
    steps = rows // band
    pairs = lax.all_to_all(pairs.reshape(band, steps * 2 * GROUP, ny), "band", 0, 0, tiled=True)
    pieces = call(
        functools.partial(gram_kernel, band, space, steps),
        struct((space * band, GROUP, band * 2 * GROUP), F32),
        pairs,
    )
    pieces = lax.all_to_all(pieces, ("space", "band"), 0, 0, tiled=True)
    total = count * band
    rows_out = struct((count, total), F32)
    intersection, projected = call(
        functools.partial(sum_kernel, 1.0 / (rows * ny * space)), (rows_out, rows_out), pieces
    )
    return filtered.reshape(orbitals.shape), intersection, projected


def padded(cells, width):
    up, down = shifts("space")
    head, tail = cells[:, :width], cells[:, cells.shape[1] - width :]
    return jnp.concatenate(
        [lax.ppermute(tail, "space", up), cells, lax.ppermute(head, "space", down)], axis=1
    )


def hamiltonian(beside, potential):
    planes = beside.shape[1] - 2 * WIDTH
    center = beside[:, WIDTH : WIDTH + planes]
    summed = 3.0 * STENCIL[0] * center
    for k in range(1, WIDTH + 1):
        near = beside[:, WIDTH + k : WIDTH + k + planes] + beside[:, WIDTH - k : WIDTH - k + planes]
        for dim in (2, 3):
            near = near + (jnp.roll(center, k, dim) + jnp.roll(center, -k, dim))
        summed = summed + STENCIL[k] * near
    return -0.5 * summed + potential * center


def local_plain(orbitals, potential):
    def step(field):
        return (hamiltonian(padded(field, WIDTH), potential) - 9.0 * field) * 0.125

    filtered = 2.0 * step(step(orbitals)) - orbitals
    beside = padded(filtered.astype(BF16), WIDTH).astype(F32)
    applied = hamiltonian(beside, potential).astype(BF16)
    count = orbitals.shape[0]
    narrow = filtered.astype(BF16).reshape(count, -1)
    applied = applied.reshape(count, -1)
    everyone = lax.all_gather(narrow, "band", axis=0, tiled=True)
    contract = (((1,), (1,)), ((), ()))
    parts = [
        lax.dot_general(rows, everyone, contract, preferred_element_type=F32)
        for rows in (narrow, applied)
    ]
    scale = 1.0 / (narrow.shape[1] * lax.axis_size("space"))
    intersection, projected = lax.psum(tuple(parts), "space")
    return filtered, intersection * scale, projected * scale


def local(orbitals, potential):
    count, planes, nx, ny = orbitals.shape
    band = lax.axis_size("band")
    fits = (
        count == GROUP
        and planes >= 2 * WIDTH
        and nx == 16
        and ny == 128
        and band * 2 * GROUP == 128
        and (planes * nx) % (2 * band) == 0
    )
    return (local_kernels if fits else local_plain)(orbitals, potential)


def solution(mesh):
    return jax.shard_map(
        local,
        mesh=mesh,
        in_specs=(P("band", "space", None, None), P("space", None, None)),
        out_specs=(P("band", "space", None, None), P("band", None), P("band", None)),
        check_vma=False,
    )
```

time: 180 us -> 77 us (0.43)
  local copies, waits for them, and re-layouts: 77.5 us -> 2.02 us
  other arithmetic: 37.9 us -> 0 us
  blocking collectives: 5.83 us -> 37.2 us
  waiting for transfers between devices: 35.8 us -> 15.8 us
  Pallas kernels: 0 us -> 16.4 us
  between operations: 14.2 us -> 0.66 us
  matrix products: 3.9 us -> 0 us
    slice x75 -> x0, local copies, waits for them, and re-layouts: 75.5 us -> none  [the longest x24 29.1 us: padded_laplace(): jnp.roll(center, offset, 3) + jnp.roll(center, -offset, 3)]
    all_to_all x0 -> x2, blocking collectives: none -> 37.2 us  [the longest x1 25.9 us: local_kernels(): lax.all_to_all(pairs.reshape(band, steps * 2 * GROUP, ny), 'band', 0, 0,...]
    convert_element_type x3 -> x0, other arithmetic: 24.9 us -> none  [the longest x1 13.5 us: local(): narrow = second.astype(jnp.bfloat16).reshape(count, -1)]
    all_gather x1 -> x0, waiting for transfers between devices: 23.1 us -> none  [local(): piece = lax.all_gather(narrow, 'band', axis=0, tiled=True)]
    pallas_call x0 -> x5, Pallas kernels: none -> 16.4 us  [call(): pl.pallas_call(kernel, out_shape=outs, in_specs=[VMEM] * len(args), out_s...]
    mul x3 -> x0, other arithmetic: 13 us -> none  [the longest x1 11.7 us: filter_step(): return (applied - 9.0 * center) * 0.125]
    psum x1 -> x0, blocking collectives: 5.83 us -> none  [local(): lax.psum((intersection_rows, project_rows), 'space')]
    dot_general x2 -> x0, matrix products: 3.9 us -> none  [the longest x1 2.95 us: local(): lax.dot_general(narrow, piece, contract, preferred_element_type=jnp.float32)]
  transfers between devices with their start and end apart: 7 -> 4, of which waited for: 4 -> 4; matrix products, arithmetic and copies ran while one was open for 35% -> 0% of each run, Pallas kernels for 0% -> 0%
where the time goes in v1:
time: 77 us; the launch traced here: 76.7 us
  blocking collectives  37.2 us (48%)
  Pallas kernels  16.4 us (21%)
  waiting for transfers between devices  15.8 us (21%)
  starting transfers between devices  4.65 us (6%)
  local copies, waits for them, and re-layouts  2.02 us (3%)
    all_to_all x1, blocking collectives, local_kernels(): lax.all_to_all(pairs.reshape(band, steps * 2 * GROUP, ny), 'band', 0, 0,...  25.9 us
    pallas_call x5, Pallas kernels, call(): pl.pallas_call(kernel, out_shape=outs, in_specs=[VMEM] * len(args), out_s...  16.4 us
    ppermute x2, waiting for transfers between devices, local_kernels(): from_left = lax.ppermute(to_right, 'space', up)  11.7 us
    all_to_all x1, blocking collectives, local_kernels(): pieces = lax.all_to_all(pieces, ('space', 'band'), 0, 0, tiled=True)  11.3 us
    ppermute x2, waiting for transfers between devices, local_kernels(): from_right = lax.ppermute(to_left, 'space', down)  4.14 us
    ppermute x2, starting transfers between devices, local_kernels(): from_right = lax.ppermute(to_left, 'space', down)  4.1 us
    unnamed x6, local copies, waits for them, and re-layouts  2.02 us
  transfers between devices with their start and end apart: 4, of which 4 were waited for; matrix products, arithmetic and copies ran while one was open for 0% of the time, Pallas kernels for 0%

profile of v1, /device:TPU:0, one launch (start us, length us, event | category | flops | bytes accessed | tf_op | source)
XLA Modules:
  0.0 76.7 jit_solution(6642072783681868767)
XLA Ops:
  0.6 0.0 copy-start
  0.6 0.9 %copy-done = f32[12,16,128]{2,1,0:T(8,128)S(1)} copy-done((f32[12,16,128]{2,1,0:T(8,128)S(1)}, f32[12,16,128]{2,1,0:T(8,128)}, u32[]{:S(2)}) %copy-start) | copy-done | bytes 98328
  1.5 0.0 copy-start.2
  1.5 1.1 %copy-done.2 = f32[8,12,16,128]{3,2,1,0:T(8,128)S(1)} copy-done((f32[8,12,16,128]{3,2,1,0:T(8,128)S(1)}, f32[8,12,16,128]{3,2,1,0:T(8,128)}, u32[]{:S(2)}) %copy-start.2) | copy-done | bytes 786456
  2.7 0.0 copy-start.1
  2.7 0.5 shard_map.49
  3.2 0.5 collective-permute-start
  3.7 2.0 %collective-permute-start.1 = (bf16[1792,128]{1,0:T(8,128)(2,1)S(1)}, bf16[1792,128]{1,0:T(8,128)(2,1)S(1)}, u32[]{:S(2)}, u32[]{:S(2)}) collective-permute-start(bf16[1792,128]{1,0:T(8,128)(2,1)S(1)} %get-tuple-element.14), channel_id=1, source_target_pairs={{8,0},{16,8},{24,16},{0,24},{9,1},{17,9},{25,17},{1,25},{10,2},{18... | collective-permute-start | bytes 1376264 | tf_op jit(solution)/shard_map/ppermute | solution.py:249
  5.7 8.3 %collective-permute-done.from_left_ref = bf16[1792,128]{1,0:T(8,128)(2,1)S(1)} collective-permute-done((bf16[1792,128]{1,0:T(8,128)(2,1)S(1)}, bf16[1792,128]{1,0:T(8,128)(2,1)S(1)}, u32[]{:S(2)}, u32[]{:S(2)}) %collective-permute-start) | collective-permute-done | bytes 458784 | tf_op jit(solution)/shard_map/ppermute | solution.py:248
  14.1 2.5 %collective-permute-done.1.from_right_ref = bf16[1792,128]{1,0:T(8,128)(2,1)S(1)} collective-permute-done((bf16[1792,128]{1,0:T(8,128)(2,1)S(1)}, bf16[1792,128]{1,0:T(8,128)(2,1)S(1)}, u32[]{:S(2)}, u32[]{:S(2)}) %collective-permute-start.1) | collective-permute-done | bytes 458784 | tf_op jit(solution)/shard_map/ppermute | solution.py:249
  16.6 0.0 copy-done.1
  16.6 11.1 %shard_map.50 = (f32[1536,128]{1,0:T(8,128)S(1)}, f32[1536,128]{1,0:T(8,128)}, bf16[768,128]{1,0:T(8,128)(2,1)S(1)}, bf16[768,128]{1,0:T(8,128)(2,1)S(1)}) custom-call(f32[1536,128]{1,0:T(8,128)S(1)} %get-tuple-element.12.own_ref, f32[192,128]{1,0:T(8,128)S(1)} %bitcast.6, bf16[1792,128]{1,0:T(8,128)(2,1)S(1)} %collective-permute-done.from_left_ref, ...), custom_call_target="tpu_custom_call" | custom-call | flops 1000000 | bytes 1000000 | tf_op jit(solution)/shard_map/pallas_call | solution.py:215
  27.7 0.0 collective-permute-start.2
  27.8 2.1 %collective-permute-start.3 = (bf16[768,128]{1,0:T(8,128)(2,1)S(1)}, bf16[768,128]{1,0:T(8,128)(2,1)S(1)}, u32[]{:S(2)}, u32[]{:S(2)}) collective-permute-start(bf16[768,128]{1,0:T(8,128)(2,1)S(1)} %get-tuple-element.18), channel_id=1, source_target_pairs={{8,0},{16,8},{24,16},{0,24},{9,1},{17,9},{25,17},{1,25},{10,2},{18... | collective-permute-start | bytes 589832 | tf_op jit(solution)/shard_map/ppermute | solution.py:262
  29.8 3.3 %collective-permute-done.2.from_left_ref = bf16[768,128]{1,0:T(8,128)(2,1)S(1)} collective-permute-done((bf16[768,128]{1,0:T(8,128)(2,1)S(1)}, bf16[768,128]{1,0:T(8,128)(2,1)S(1)}, u32[]{:S(2)}, u32[]{:S(2)}) %collective-permute-start.2) | collective-permute-done | bytes 196640 | tf_op jit(solution)/shard_map/ppermute | solution.py:261
  33.2 1.7 %collective-permute-done.3.from_right_ref = bf16[768,128]{1,0:T(8,128)(2,1)S(1)} collective-permute-done((bf16[768,128]{1,0:T(8,128)(2,1)S(1)}, bf16[768,128]{1,0:T(8,128)(2,1)S(1)}, u32[]{:S(2)}, u32[]{:S(2)}) %collective-permute-start.3) | collective-permute-done | bytes 196640 | tf_op jit(solution)/shard_map/ppermute | solution.py:262
  34.8 3.4 %shard_map.51 = bf16[3072,128]{1,0:T(8,128)(2,1)S(1)} custom-call(f32[1536,128]{1,0:T(8,128)S(1)} %get-tuple-element.16.second_ref, f32[192,128]{1,0:T(8,128)S(1)} %bitcast.7, bf16[768,128]{1,0:T(8,128)(2,1)S(1)} %collective-permute-done.2.from_left_ref, bf16[768,128]{1,0:T(8,128)(2,1)S(1)} %collective-permute-done.3.from_right_ref), custom_call_target="tpu_custom_call" | custom-call | flops 1000000 | bytes 1000000 | tf_op jit(solution)/shard_map/pallas_call | solution.py:215
  38.3 25.9 %all_to_all.10.in_ref = bf16[8,384,128]{2,1,0:T(8,128)(2,1)S(1)} all-to-all(bf16[8,384,128]{2,1,0:T(8,128)(2,1)S(1)} %bitcast.4), channel_id=1, replica_groups=mesh['space'=4,'band'=8] {'band'}, dimensions={0} | all-to-all | bytes 1572864 | tf_op jit(solution)/shard_map/all_to_all | solution.py:270
  64.2 0.4 shard_map.52
  64.6 11.3 %all_to_all.11.in_ref = f32[32,8,128]{2,1,0:T(8,128)S(1)} all-to-all(f32[32,8,128]{2,1,0:T(8,128)S(1)} %shard_map.52), channel_id=1, replica_groups=mesh['space'=4,'band'=8] {'space','band'}, dimensions={0} | all-to-all | bytes 262144 | tf_op jit(solution)/shard_map/all_to_all | solution.py:276
  75.9 0.9 %shard_map.53 = (f32[8,64]{1,0:T(8,128)}, f32[8,64]{1,0:T(8,128)}) custom-call(f32[32,8,128]{2,1,0:T(8,128)S(1)} %all_to_all.11.in_ref), custom_call_target="tpu_custom_call" | custom-call | flops 1000000 | bytes 1000000 | tf_op jit(solution)/shard_map/pallas_call | solution.py:215
Async XLA Ops:
  0.6 0.9 %copy-start = (f32[12,16,128]{2,1,0:T(8,128)S(1)}, f32[12,16,128]{2,1,0:T(8,128)}, u32[]{:S(2)}) copy-start(f32[12,16,128]{2,1,0:T(8,128)} %param.3) | copy-start | bytes 294916
  1.5 1.1 %copy-start.2 = (f32[8,12,16,128]{3,2,1,0:T(8,128)S(1)}, f32[8,12,16,128]{3,2,1,0:T(8,128)}, u32[]{:S(2)}) copy-start(f32[8,12,16,128]{3,2,1,0:T(8,128)} %param.2) | copy-start | bytes 2359300
  2.7 13.9 %copy-start.1 = (f32[12,16,128]{2,1,0:T(8,128)S(1)}, f32[12,16,128]{2,1,0:T(8,128)}, u32[]{:S(2)}) copy-start(f32[12,16,128]{2,1,0:T(8,128)} %param.3) | copy-start | bytes 294916
  3.2 10.9 %collective-permute-start = (bf16[1792,128]{1,0:T(8,128)(2,1)S(1)}, bf16[1792,128]{1,0:T(8,128)(2,1)S(1)}, u32[]{:S(2)}, u32[]{:S(2)}) collective-permute-start(bf16[1792,128]{1,0:T(8,128)(2,1)S(1)} %get-tuple-element.13), channel_id=1, source_target_pairs={{0,8},{8,16},{16,24},{24,0},{1,9},{9,17},{17,25},{25,1},{2,10},{10... | collective-permute-start | bytes 1376264 | tf_op jit(solution)/shard_map/ppermute | solution.py:248
  3.7 12.9 %collective-permute-start.1 = (bf16[1792,128]{1,0:T(8,128)(2,1)S(1)}, bf16[1792,128]{1,0:T(8,128)(2,1)S(1)}, u32[]{:S(2)}, u32[]{:S(2)}) collective-permute-start(bf16[1792,128]{1,0:T(8,128)(2,1)S(1)} %get-tuple-element.14), channel_id=1, source_target_pairs={{8,0},{16,8},{24,16},{0,24},{9,1},{17,9},{25,17},{1,25},{10,2},{18... | collective-permute-start | bytes 1376264 | tf_op jit(solution)/shard_map/ppermute | solution.py:249
  27.7 5.5 %collective-permute-start.2 = (bf16[768,128]{1,0:T(8,128)(2,1)S(1)}, bf16[768,128]{1,0:T(8,128)(2,1)S(1)}, u32[]{:S(2)}, u32[]{:S(2)}) collective-permute-start(bf16[768,128]{1,0:T(8,128)(2,1)S(1)} %get-tuple-element.17), channel_id=1, source_target_pairs={{0,8},{8,16},{16,24},{24,0},{1,9},{9,17},{17,25},{25,1},{2,10},{10... | collective-permute-start | bytes 589832 | tf_op jit(solution)/shard_map/ppermute | solution.py:261
  27.8 7.1 %collective-permute-start.3 = (bf16[768,128]{1,0:T(8,128)(2,1)S(1)}, bf16[768,128]{1,0:T(8,128)(2,1)S(1)}, u32[]{:S(2)}, u32[]{:S(2)}) collective-permute-start(bf16[768,128]{1,0:T(8,128)(2,1)S(1)} %get-tuple-element.18), channel_id=1, source_target_pairs={{8,0},{16,8},{24,16},{0,24},{9,1},{17,9},{25,17},{1,25},{10,2},{18... | collective-permute-start | bytes 589832 | tf_op jit(solution)/shard_map/ppermute | solution.py:262

commit v2 on v1

v2 whole, which is shorter than its diff:
```python
import functools

import jax
import jax.numpy as jnp
from jax import lax
from jax.experimental import pallas as pl
from jax.experimental.pallas import tpu as pltpu
from jax.sharding import PartitionSpec as P

STENCIL = (
    -5369.0 / 1800.0,
    12.0 / 7.0,
    -15.0 / 56.0,
    10.0 / 189.0,
    -1.0 / 112.0,
    2.0 / 1925.0,
    -1.0 / 16632.0,
)
WIDTH = 6
BF16 = jnp.bfloat16
F32 = jnp.float32
VMEM = pl.BlockSpec(memory_space=pltpu.VMEM)
PARAMS = pltpu.CompilerParams(vmem_limit_bytes=40 * 1024 * 1024)

GROUP = 8

H_FACTORS = tuple(-0.5 * c for c in STENCIL[1:])
H_CENTER = -1.5 * STENCIL[0]
L_FACTORS = tuple(0.125 * c for c in H_FACTORS)
L_CENTER = (H_CENTER - 9.0) / 8.0


def aligned(start, size):
    return pl.ds(pl.multiple_of(start, size), size)


def low_part(block):
    return block - block.astype(BF16).astype(F32)


def circulant(ny):
    row = lax.broadcasted_iota(jnp.int32, (ny, ny), 0)
    column = lax.broadcasted_iota(jnp.int32, (ny, ny), 1)
    apart = jnp.abs(row - column)
    apart = jnp.minimum(apart, ny - apart)
    matrix = jnp.zeros((ny, ny), F32)
    for k in range(1, WIDTH + 1):
        matrix = jnp.where(apart == k, H_FACTORS[k - 1], matrix)
    high = matrix.astype(BF16)
    return jnp.concatenate([high, low_part(matrix).astype(BF16), high], axis=0)


def along_y(matrix, source, start, count, y_ref, plane_rows):
    step = min(count, WIDTH)
    for i in range(0, count, step):
        block = source[pl.ds((start + i) * plane_rows, step * plane_rows), :]
        high = block.astype(BF16)
        parts = jnp.concatenate([high, high, low_part(block).astype(BF16)], axis=1)
        y_ref[pl.ds(i * plane_rows, step * plane_rows), :] = jnp.dot(
            parts, matrix, preferred_element_type=F32
        )


def apply_planes(matrix, source, start, count, nx, y_ref, levels, level, linear, emit):
    plane_rows = nx * GROUP
    along_y(matrix, source, start, count, y_ref, plane_rows)
    factors, scale = (L_FACTORS, 0.125) if linear else (H_FACTORS, 1.0)

    def load(row):
        return source[aligned(row, GROUP), :]

    @pl.loop(0, count)
    def _(i):
        where = (start + i) * plane_rows
        center = [load(where + x * GROUP) for x in range(nx)]
        values = []
        for x in range(nx):
            row = levels[pl.ds((level + i) * nx + x, 1), :]
            row = 0.125 * row + L_CENTER if linear else row + H_CENTER
            total = jnp.broadcast_to(row, center[x].shape) * center[x]
            total = total + scale * y_ref[aligned(i * plane_rows + x * GROUP, GROUP), :]
            for k in range(1, WIDTH + 1):
                near = load(where + k * plane_rows + x * GROUP) + load(where - k * plane_rows + x * GROUP)
                near = near + (center[(x + k) % nx] + center[(x - k) % nx])
                total = total + factors[k - 1] * near
            values.append(total)
        emit(i, values, center)


def prepare_kernel(
    planes, nx, orbitals_hbm, potential_hbm, own_ref, level_ref, chip_ref, core_ref,
    orbitals, potential, semaphores,
):
    plane_rows = nx * GROUP
    rows = planes * nx
    parts = semaphores.shape[0] - 1
    each = planes // parts
    odd = lax.rem(lax.axis_index("space"), 2)

    def fetch(i):
        at = pl.ds(i * each, each)
        return pltpu.make_async_copy(orbitals_hbm.at[:, at], orbitals.at[:, at], semaphores.at[i])

    fetch_levels = pltpu.make_async_copy(potential_hbm, potential, semaphores.at[parts])
    for i in range(parts):
        fetch(i).start()
    fetch_levels.start()
    cells = orbitals.reshape(GROUP * rows, orbitals.shape[-1])
    for i in range(parts):
        fetch(i).wait()

        @pl.loop(i * each, (i + 1) * each)
        def _(plane):
            target = lax.select(odd == 1, planes - 1 - plane, plane) * plane_rows
            for x in range(0, nx, 2):
                row = plane * nx + x
                both = jnp.concatenate(
                    [cells[pl.ds(row + j, GROUP, stride=rows), :] for j in range(2)], axis=0
                )
                at = aligned(target + x * GROUP, 2 * GROUP)
                own_ref[at, :] = both
                high = both.astype(BF16)
                chip_ref[at, :] = high
                core_ref[at, :] = high

    fetch_levels.wait()
    extra = planes * plane_rows
    for out_ref, plane in ((chip_ref, 0), (core_ref, planes - 1)):
        block = own_ref[pl.ds(plane * plane_rows, plane_rows), :]
        out_ref[pl.ds(extra, plane_rows), :] = low_part(block).astype(BF16)
    extra += plane_rows
    for plane in range(planes):
        source = lax.select(odd == 1, planes - 1 - plane, plane) * nx
        block = potential[aligned(source, nx), :]
        level_ref[pl.ds(plane * nx, nx), :] = block
        for out_ref, first in ((chip_ref, 0), (core_ref, planes - NEAR)):
            out_ref[pl.ds(extra + plane * nx, nx), :] = block.astype(BF16)
            if first <= plane < first + NEAR:
                at = extra + (planes + plane - first) * nx
                out_ref[pl.ds(at, nx), :] = low_part(block).astype(BF16)


NEAR = 4


def place_planes(message, count, field, where, step, plane_rows):
    for i in range(count):
        block = message[pl.ds(i * plane_rows, plane_rows), :]
        field[pl.ds((where + step * i) * plane_rows, plane_rows), :] = block.astype(F32)


def add_low(message, planes, field, where, plane_rows):
    at = pl.ds(where * plane_rows, plane_rows)
    field[at, :] = field[at, :] + message[pl.ds(planes * plane_rows, plane_rows), :].astype(F32)


def place_levels(message, planes, nx, levels, where, step, near):
    extra = (planes + 1) * nx * GROUP
    for i in range(planes):
        block = message[pl.ds(extra + i * nx, nx), :].astype(F32)
        if near <= i < near + NEAR:
            block = block + message[pl.ds(extra + (planes + i - near) * nx, nx), :].astype(F32)
        levels[pl.ds((where + step * i) * nx, nx), :] = block


def store_planes(ref, first, nx):
    def emit(i, values, center):
        for x in range(nx):
            ref[aligned(((first + i) * nx + x) * GROUP, GROUP), :] = values[x]

    return emit


def early_kernel(planes, nx, own_ref, level_ref, core_ref, first_ref, field, levels, y_ref):
    plane_rows = nx * GROUP
    field[pl.ds(0, planes * plane_rows), :] = own_ref[...]
    place_planes(core_ref, planes, field, 2 * planes - 1, -1, plane_rows)
    add_low(core_ref, planes, field, planes, plane_rows)
    levels[pl.ds(0, planes * nx), :] = level_ref[...]
    place_levels(core_ref, planes, nx, levels, 2 * planes - 1, -1, planes - NEAR)
    matrix = circulant(y_ref.shape[1])
    apply_planes(
        matrix, field, WIDTH, 2 * planes - 2 * WIDTH, nx, y_ref, levels, WIDTH, True,
        store_planes(first_ref, 0, nx),
    )


def middle_kernel(
    planes, nx, own_ref, level_ref, chip_ref, early_ref, first_ref, second_ref, core_ref,
    field, levels, first, y_ref,
):
    plane_rows = nx * GROUP
    size = planes * plane_rows
    side = WIDTH * plane_rows
    place_planes(chip_ref, planes, field, planes - 1, -1, plane_rows)
    add_low(chip_ref, planes, field, planes - 1, plane_rows)
    field[pl.ds(size, size), :] = own_ref[...]
    place_levels(chip_ref, planes, nx, levels, planes - 1, -1, 0)
    levels[pl.ds(planes * nx, planes * nx), :] = level_ref[...]
    matrix = circulant(y_ref.shape[1])

    def emit_first(i, values, center):
        for x in range(nx):
            at = aligned((i * nx + x) * GROUP, GROUP)
            first_ref[at, :] = values[x]
            first[at, :] = values[x]

    begin = planes - WIDTH
    apply_planes(matrix, field, begin, planes, nx, y_ref, levels, begin, True, emit_first)
    first[pl.ds(planes * plane_rows, planes * plane_rows), :] = early_ref[...]

    def emit_second(i, values, center):
        for x in range(nx):
            at = aligned((i * nx + x) * GROUP, GROUP)
            second_ref[at, :] = 2.0 * values[x] - own_ref[at, :]

    apply_planes(matrix, first, WIDTH, planes, nx, y_ref, levels, planes, True, emit_second)
    core_ref[...] = second_ref[pl.ds(size - side, side), :].astype(BF16)


def forward_kernel(begin, early_ref, chip_ref, far_ref):
    del early_ref
    far_ref[...] = chip_ref[pl.ds(begin, far_ref.shape[0]), :]


def left_kernel(
    planes, nx, level_ref, chip_ref, far_ref, middle_ref, second_ref,
    pairs_ref, filtered_hbm, field, levels, first, second, y_ref, filtered, semaphore,
):
    plane_rows = nx * GROUP
    rows = planes * nx
    size = planes * plane_rows
    side = WIDTH * plane_rows
    odd = lax.rem(lax.axis_index("space"), 2)

    @pl.loop(0, planes)
    def _(plane):
        target = lax.select(odd == 1, planes - 1 - plane, plane) * nx
        for x in range(nx):
            value = second_ref[aligned((plane * nx + x) * GROUP, GROUP), :]
            filtered[pl.ds(target + x, GROUP, stride=rows), :] = value

    write = pltpu.make_async_copy(filtered, filtered_hbm, semaphore)
    write.start()
    matrix = circulant(y_ref.shape[1])

    field[pl.ds(0, side), :] = far_ref[...].astype(F32)
    place_planes(chip_ref, planes, field, WIDTH + planes - 1, -1, plane_rows)
    add_low(chip_ref, planes, field, WIDTH + planes - 1, plane_rows)
    place_levels(chip_ref, planes, nx, levels, planes - 1, -1, 0)
    first[pl.ds(side, size), :] = middle_ref[...]
    second[pl.ds(side, size), :] = second_ref[...]
    apply_planes(
        matrix, field, WIDTH, WIDTH, nx, y_ref, levels, 0, True, store_planes(first, 0, nx)
    )

    def emit_second(i, values, center):
        for x in range(nx):
            row = (i * nx + x) * GROUP
            before = field[aligned(planes * plane_rows + row, GROUP), :]
            second[aligned(row, GROUP), :] = 2.0 * values[x] - before

    apply_planes(
        matrix, first, WIDTH, WIDTH, nx, y_ref, levels, planes - WIDTH, True, emit_second
    )
    apply_planes(
        matrix, second, WIDTH, WIDTH, nx, y_ref, level_ref, 0, False, store_pairs(pairs_ref, nx)
    )
    write.wait()


def store_pairs(ref, nx):
    def emit(i, values, center):
        for x in range(nx):
            pair = jnp.concatenate([center[x], values[x]], axis=0).astype(BF16)
            ref[aligned((i * nx + x) * 2 * GROUP, 2 * GROUP), :] = pair

    return emit


def right_kernel(
    planes, nx, level_ref, core_ref, second_ref, left_ref, out_ref, second, y_ref, pairs,
):
    plane_rows = nx * GROUP
    size = planes * plane_rows
    band, height, _ = out_ref.shape
    me = lax.axis_index("band")
    second[pl.ds(0, size), :] = second_ref[...]
    place_planes(core_ref, WIDTH, second, planes + WIDTH - 1, -1, plane_rows)
    matrix = circulant(y_ref.shape[1])
    half = planes - WIDTH
    apply_planes(
        matrix, second, WIDTH, half, nx, y_ref, level_ref, WIDTH, False, store_pairs(pairs, nx)
    )
    for i in range(band // 2):
        at = pl.ds(i * height, height)
        out_ref[i ^ me] = left_ref[at, :]
        out_ref[(band // 2 + i) ^ me] = pairs[at, :]


def gram_kernel(space, steps, *refs):
    *blocks, out_ref, held = refs
    band = len(blocks)
    width = 2 * GROUP
    me = lax.axis_index("band")
    for k in range(band):
        held[k ^ me] = blocks[k][...]
    total = jnp.zeros((band * width, band * width), F32)
    for step in range(0, steps, 2):
        block = jnp.concatenate(
            [held[:, pl.ds((step + i) * width, width), :].reshape(band * width, -1) for i in range(2)],
            axis=1,
        )
        total = total + lax.dot_general(
            block, block, (((1,), (1,)), ((), ())), preferred_element_type=F32
        )
    lanes = lax.broadcasted_iota(jnp.int32, (GROUP, band * width), 1)
    for b in range(band):
        narrow = total[b * width : b * width + GROUP]
        applied = pltpu.roll(total[b * width + GROUP : (b + 1) * width], GROUP, 1)
        piece = jnp.where(lanes % width < GROUP, narrow, applied)
        for s in range(space):
            out_ref[s * band + b] = piece


def sum_kernel(scale, in_ref, intersection_ref, projected_ref):
    total = in_ref[0]
    for i in range(1, in_ref.shape[0]):
        total = total + in_ref[i]
    total = total * scale
    lanes, columns = total.shape[1], intersection_ref.shape[1]
    source = lax.broadcasted_iota(jnp.int32, (lanes, columns), 0)
    target = lax.broadcasted_iota(jnp.int32, (lanes, columns), 1)
    place = (target // GROUP) * (2 * GROUP) + target % GROUP
    for offset, ref in ((0, intersection_ref), (GROUP, projected_ref)):
        pick = jnp.where(source == place + offset, 1.0, 0.0).astype(F32)
        ref[...] = jnp.dot(total, pick, precision=lax.Precision.HIGHEST, preferred_element_type=F32)


def call(kernel, outs, *args, scratch=(), hbm_in=0, hbm_out=(), space=pl.ANY, flops=1000000):
    anywhere = pl.BlockSpec(memory_space=space)
    return pl.pallas_call(
        kernel,
        out_shape=outs,
        in_specs=[anywhere] * hbm_in + [VMEM] * (len(args) - hbm_in),
        out_specs=tuple(anywhere if i in hbm_out else VMEM for i in range(len(outs))),
        scratch_shapes=list(scratch),
        compiler_params=PARAMS,
        cost_estimate=pl.CostEstimate(flops=flops, bytes_accessed=1000000, transcendentals=0),
    )(*args)


def shifts(axis):
    count = lax.axis_size(axis)
    up = [(i, (i + 1) % count) for i in range(count)]
    return up, [(j, i) for i, j in up]


def local_kernels(orbitals, potential):
    count, planes, nx, ny = orbitals.shape
    space, band = lax.axis_size("space"), lax.axis_size("band")
    rows = planes * nx
    plane_rows = nx * GROUP
    size = planes * plane_rows
    struct = jax.ShapeDtypeStruct
    other_core = [(i, i ^ 1) for i in range(space)]
    other_chip = [(i, i ^ 3) for i in range(space)]

    def f32_planes(many, height=plane_rows):
        return pltpu.VMEM((many * height, ny), F32)

    message = struct((size + plane_rows + (planes + NEAR) * nx, ny), BF16)
    slab = struct((size, ny), F32)
    parts = 4
    own, levels, to_chip, to_core = call(
        functools.partial(prepare_kernel, planes, nx),
        (slab, struct((rows, ny), F32), message, message),
        orbitals, potential.reshape(rows, ny),
        hbm_in=2, space=pltpu.HBM,
        scratch=[
            pltpu.VMEM(orbitals.shape, F32),
            pltpu.VMEM((rows, ny), F32),
            pltpu.SemaphoreType.DMA((parts + 1,)),
        ],
    )
    chip = lax.ppermute(to_chip, "space", other_chip)
    core = lax.ppermute(to_core, "space", other_core)
    (early,) = call(
        functools.partial(early_kernel, planes, nx),
        (slab,),
        own, levels, core,
        scratch=[f32_planes(2 * planes), f32_planes(2 * planes, nx), f32_planes(planes)],
    )
    side = struct((WIDTH * plane_rows, ny), BF16)
    (far,) = call(
        functools.partial(forward_kernel, (planes - WIDTH) * plane_rows), (side,), early, chip, hbm_in=1
    )
    far = lax.ppermute(far, "space", other_core)
    middle, second, to_core = call(
        functools.partial(middle_kernel, planes, nx),
        (slab, slab, side),
        own, levels, chip, early,
        scratch=[
            f32_planes(2 * planes), f32_planes(2 * planes, nx), f32_planes(2 * planes), f32_planes(planes),
        ],
    )
    beside = lax.ppermute(to_core, "space", other_core)
    left, filtered = call(
        functools.partial(left_kernel, planes, nx),
        (struct((WIDTH * nx * 2 * GROUP, ny), BF16), struct((count * rows, ny), F32)),
        levels, chip, far, middle, second,
        hbm_out=(1,),
        scratch=[
            f32_planes(planes + WIDTH),
            f32_planes(planes, nx),
            f32_planes(planes + WIDTH),
            f32_planes(planes + WIDTH),
            f32_planes(WIDTH),
            pltpu.VMEM((count * rows, ny), F32),
            pltpu.SemaphoreType.DMA,
        ],
    )
    steps = rows // band
    block = (steps * 2 * GROUP, ny)
    (pairs,) = call(
        functools.partial(right_kernel, planes, nx),
        (struct((band, *block), BF16),),
        levels, beside, second, left,
        scratch=[
            f32_planes(planes + WIDTH),
            f32_planes(planes - WIDTH),
            pltpu.VMEM(((planes - WIDTH) * nx * 2 * GROUP, ny), BF16),
        ],
    )
    blocks = [pairs[0]]
    for k in range(1, band):
        blocks.append(lax.ppermute(pairs[k], "band", [(i, i ^ k) for i in range(band)]))
    (pieces,) = call(
        functools.partial(gram_kernel, space, steps),
        (struct((space * band, GROUP, band * 2 * GROUP), F32),),
        *blocks,
        scratch=[pltpu.VMEM((band, *block), BF16)],
    )
    pieces = lax.all_to_all(pieces, ("space", "band"), 0, 0, tiled=True)
    rows_out = struct((count, count * band), F32)
    intersection, projected = call(
        functools.partial(sum_kernel, 1.0 / (rows * ny * space)), (rows_out, rows_out), pieces
    )
    return filtered.reshape(orbitals.shape), intersection, projected


def padded(cells, width):
    up, down = shifts("space")
    head, tail = cells[:, :width], cells[:, cells.shape[1] - width :]
    return jnp.concatenate(
        [lax.ppermute(tail, "space", up), cells, lax.ppermute(head, "space", down)], axis=1
    )


def hamiltonian(beside, potential):
    planes = beside.shape[1] - 2 * WIDTH
    center = beside[:, WIDTH : WIDTH + planes]
    summed = 3.0 * STENCIL[0] * center
    for k in range(1, WIDTH + 1):
        near = beside[:, WIDTH + k : WIDTH + k + planes] + beside[:, WIDTH - k : WIDTH - k + planes]
        for dim in (2, 3):
            near = near + (jnp.roll(center, k, dim) + jnp.roll(center, -k, dim))
        summed = summed + STENCIL[k] * near
    return -0.5 * summed + potential * center


def local_plain(orbitals, potential):
    def step(field):
        return (hamiltonian(padded(field, WIDTH), potential) - 9.0 * field) * 0.125

    filtered = 2.0 * step(step(orbitals)) - orbitals
    beside = padded(filtered.astype(BF16), WIDTH).astype(F32)
    applied = hamiltonian(beside, potential).astype(BF16)
    count = orbitals.shape[0]
    narrow = filtered.astype(BF16).reshape(count, -1)
    applied = applied.reshape(count, -1)
    everyone = lax.all_gather(narrow, "band", axis=0, tiled=True)
    contract = (((1,), (1,)), ((), ()))
    parts = [
        lax.dot_general(rows, everyone, contract, preferred_element_type=F32)
        for rows in (narrow, applied)
    ]
    scale = 1.0 / (narrow.shape[1] * lax.axis_size("space"))
    intersection, projected = lax.psum(tuple(parts), "space")
    return filtered, intersection * scale, projected * scale


def local(orbitals, potential):
    count, planes, nx, ny = orbitals.shape
    band = lax.axis_size("band")
    fits = (
        count == GROUP
        and lax.axis_size("space") == 4
        and planes == 2 * WIDTH
        and nx == 16
        and ny == 128
        and band * 2 * GROUP == 128
        and (planes * nx) % (2 * band) == 0
    )
    return (local_kernels if fits else local_plain)(orbitals, potential)


def solution(mesh):
    return jax.shard_map(
        local,
        mesh=mesh,
        in_specs=(P("band", "space", None, None), P("space", None, None)),
        out_specs=(P("band", "space", None, None), P("band", None), P("band", None)),
        check_vma=False,
    )
```

time: 77 us -> 61.8 us (0.80)
  blocking collectives: 37.2 us -> 11.7 us
  starting transfers between devices: 4.65 us -> 16.2 us
  Pallas kernels: 16.4 us -> 11.1 us
  waiting for transfers between devices: 15.8 us -> 19.8 us
    all_to_all x1 -> x0, blocking collectives: 25.9 us -> none  [local_kernels(): lax.all_to_all(pairs.reshape(band, steps * 2 * GROUP, ny), 'band', 0, 0,...]
    ppermute x4 -> x11, starting transfers between devices: 4.65 us -> 16.2 us  [the longest x7 12.4 us: local_kernels(): lax.ppermute(pairs[k], 'band', [(i, i ^ k) for i in range(band)])]
    pallas_call x5 -> x8, Pallas kernels: 16.4 us -> 11.1 us  [call(): pl.pallas_call(kernel, out_shape=outs, in_specs=[anywhere] * hbm_in + [VM...]
    ppermute x4 -> x11, waiting for transfers between devices: 15.8 us -> 19.8 us  [the longest x1 9.96 us: local_kernels(): chip = lax.ppermute(to_chip, 'space', other_chip)]
    unnamed x6 -> x4, local copies, waits for them, and re-layouts: 2.02 us -> 2.02 us
  transfers between devices with their start and end apart: 4 -> 11, of which waited for: 4 -> 5; matrix products, arithmetic and copies ran while one was open for 0% -> 0% of each run, Pallas kernels for 0% -> 13%
where the time goes in v2:
time: 61.8 us; the launch traced here: 61.6 us
  waiting for transfers between devices  19.8 us (32%)
  starting transfers between devices  16.2 us (26%)
  blocking collectives  11.7 us (19%)
  Pallas kernels  11.1 us (18%)
  local copies, waits for them, and re-layouts  2.07 us (3%)
  between operations  0.71 us (1%)
    ppermute x7, starting transfers between devices, local_kernels(): lax.ppermute(pairs[k], 'band', [(i, i ^ k) for i in range(band)])  12.4 us
    all_to_all x1, blocking collectives, local_kernels(): pieces = lax.all_to_all(pieces, ('space', 'band'), 0, 0, tiled=True)  11.7 us
    pallas_call x8, Pallas kernels, call(): pl.pallas_call(kernel, out_shape=outs, in_specs=[anywhere] * hbm_in + [VM...  11.1 us
    ppermute x1, waiting for transfers between devices, local_kernels(): chip = lax.ppermute(to_chip, 'space', other_chip)  9.96 us
    ppermute x7, waiting for transfers between devices, local_kernels(): lax.ppermute(pairs[k], 'band', [(i, i ^ k) for i in range(band)])  9.84 us
    ppermute x1, starting transfers between devices, local_kernels(): chip = lax.ppermute(to_chip, 'space', other_chip)  2.64 us
    unnamed x4, local copies, waits for them, and re-layouts  2.02 us
  transfers between devices with their start and end apart: 11, of which 5 were waited for; matrix products, arithmetic and copies ran while one was open for 0% of the time, Pallas kernels for 13%

profile of v2, /device:TPU:0, one launch (start us, length us, event | category | flops | bytes accessed | tf_op | source)
XLA Modules:
  0.0 61.6 jit_solution(13024691517532725099)
XLA Ops:
  0.6 0.0 copy-start
  0.6 1.1 %copy-done = f32[8,12,16,128]{3,2,1,0:T(8,128)S(1)} copy-done((f32[8,12,16,128]{3,2,1,0:T(8,128)S(1)}, f32[8,12,16,128]{3,2,1,0:T(8,128)}, u32[]{:S(2)}) %copy-start) | copy-done | bytes 786456
  1.8 0.0 copy-start.1
  1.8 0.9 %copy-done.1 = f32[12,16,128]{2,1,0:T(8,128)S(1)} copy-done((f32[12,16,128]{2,1,0:T(8,128)S(1)}, f32[12,16,128]{2,1,0:T(8,128)}, u32[]{:S(2)}) %copy-start.1) | copy-done | bytes 98328
  2.7 0.9 %shard_map.49 = (f32[1536,128]{1,0:T(8,128)S(1)}, f32[192,128]{1,0:T(8,128)S(1)}, bf16[1920,128]{1,0:T(8,128)(2,1)S(1)}, bf16[1920,128]{1,0:T(8,128)(2,1)S(1)}) custom-call(f32[8,12,16,128]{3,2,1,0:T(8,128)S(1)} %copy-done, f32[192,128]{1,0:T(8,128)S(1)} %bitcast.18), custom_call_target="tpu_custom_call" | custom-call | flops 1000000 | bytes 1000000 | tf_op jit(solution)/shard_map/pallas_call | solution.py:342
  3.5 0.5 collective-permute-start.1
  4.0 2.6 %collective-permute-start = (bf16[1920,128]{1,0:T(8,128)(2,1)S(1)}, bf16[1920,128]{1,0:T(8,128)(2,1)S(1)}, u32[]{:S(2)}, u32[]{:S(2)}) collective-permute-start(bf16[1920,128]{1,0:T(8,128)(2,1)S(1)} %get-tuple-element.15), channel_id=1, source_target_pairs={{0,24},{8,16},{16,8},{24,0},{1,25},{9,17},{17,9},{25,1},{2,26},{10... | collective-permute-start | bytes 1474568 | tf_op jit(solution)/shard_map/ppermute | solution.py:386
  6.7 0.0 collective-permute-done.1.core_ref
  6.7 1.5 %shard_map.50.early_ref = f32[1536,128]{1,0:T(8,128)S(1)} custom-call(f32[1536,128]{1,0:T(8,128)S(1)} %get-tuple-element.16.own_ref, f32[192,128]{1,0:T(8,128)S(1)} %get-tuple-element.14.level_ref, bf16[1920,128]{1,0:T(8,128)(2,1)S(1)} %collective-permute-done.1.core_ref), custom_call_target="tpu_custom_call" | custom-call | flops 1000000 | bytes 1000000 | tf_op jit(solution)/shard_map/pallas_call | solution.py:342
  8.2 10.0 %collective-permute-done.chip_ref = bf16[1920,128]{1,0:T(8,128)(2,1)S(1)} collective-permute-done((bf16[1920,128]{1,0:T(8,128)(2,1)S(1)}, bf16[1920,128]{1,0:T(8,128)(2,1)S(1)}, u32[]{:S(2)}, u32[]{:S(2)}) %collective-permute-start) | collective-permute-done | bytes 491552 | tf_op jit(solution)/shard_map/ppermute | solution.py:386
  18.2 0.2 collective-permute-start.2
  18.4 3.1 %shard_map.52 = (f32[1536,128]{1,0:T(8,128)S(1)}, f32[1536,128]{1,0:T(8,128)S(1)}, bf16[768,128]{1,0:T(8,128)(2,1)S(1)}) custom-call(f32[1536,128]{1,0:T(8,128)S(1)} %get-tuple-element.16.own_ref, f32[192,128]{1,0:T(8,128)S(1)} %get-tuple-element.14.level_ref, bf16[1920,128]{1,0:T(8,128)(2,1)S(1)} %collective-permute-done.chip_ref, ...), custom_call_target="tpu_custom_call" | custom-call | flops 1000000 | bytes 1000000 | tf_op jit(solution)/shard_map/pallas_call | solution.py:342
  21.5 0.5 collective-permute-start.3
  21.9 0.0 collective-permute-done.2.far_ref
  21.9 3.3 %shard_map.53 = (bf16[1536,128]{1,0:T(8,128)(2,1)S(1)}, f32[1536,128]{1,0:T(8,128)}) custom-call(f32[192,128]{1,0:T(8,128)S(1)} %get-tuple-element.14.level_ref, bf16[1920,128]{1,0:T(8,128)(2,1)S(1)} %collective-permute-done.chip_ref, bf16[768,128]{1,0:T(8,128)(2,1)S(1)} %collective-permute-done.2.far_ref, f32[1536,128]{1,0:T(8,128)S(1)} %get-tuple-element.18.middle_ref, ...), custom_call_target="tpu_custom_call" | custom-call | flops 1000000 | bytes 1000000 | tf_op jit(solution)/shard_map/pallas_call | solution.py:342
  25.2 0.0 collective-permute-done.3.core_ref
  25.2 1.0 %shard_map.54 = bf16[8,384,128]{2,1,0:T(8,128)(2,1)S(1)} custom-call(f32[192,128]{1,0:T(8,128)S(1)} %get-tuple-element.14.level_ref, bf16[768,128]{1,0:T(8,128)(2,1)S(1)} %collective-permute-done.3.core_ref, f32[1536,128]{1,0:T(8,128)S(1)} %get-tuple-element.19.second_ref, bf16[1536,128]{1,0:T(8,128)(2,1)S(1)} %get-tuple-element.22.left_ref), custom_call_target="tpu_custom_call" | custom-call | flops 1000000 | bytes 1000000 | tf_op jit(solution)/shard_map/pallas_call | solution.py:342
  26.2 0.1 slice_bitcast_fusion
  26.3 4.5 %collective-permute-start.10 = (bf16[384,128]{1,0:T(8,128)(2,1)S(1)}, bf16[384,128]{1,0:T(8,128)(2,1)S(1)}, u32[]{:S(2)}, u32[]{:S(2)}) collective-permute-start(bf16[384,128]{1,0:T(8,128)(2,1)S(1)} %get-tuple-element.25), channel_id=1, source_target_pairs={{0,7},{1,6},{2,5},{3,4},{4,3},{5,2},{6,1},{7,0},{8,15},{9,14},{10,... | collective-permute-start | bytes 294920 | tf_op jit(solution)/shard_map/ppermute | solution.py:437
  30.7 0.6 collective-permute-start.4
  31.3 0.0 collective-permute-start.5
  31.3 2.9 %collective-permute-start.6 = (bf16[384,128]{1,0:T(8,128)(2,1)S(1)}, bf16[384,128]{1,0:T(8,128)(2,1)S(1)}, u32[]{:S(2)}, u32[]{:S(2)}) collective-permute-start(bf16[384,128]{1,0:T(8,128)(2,1)S(1)} %get-tuple-element.29), channel_id=1, source_target_pairs={{0,3},{1,2},{2,1},{3,0},{4,7},{5,6},{6,5},{7,4},{8,11},{9,10},{10,... | collective-permute-start | bytes 294920 | tf_op jit(solution)/shard_map/ppermute | solution.py:437
  34.2 0.0 collective-permute-start.7
  34.2 0.5 collective-permute-done.10.refs_7_
  34.7 2.9 %collective-permute-start.8 = (bf16[384,128]{1,0:T(8,128)(2,1)S(1)}, bf16[384,128]{1,0:T(8,128)(2,1)S(1)}, u32[]{:S(2)}, u32[]{:S(2)}) collective-permute-start(bf16[384,128]{1,0:T(8,128)(2,1)S(1)} %get-tuple-element.27), channel_id=1, source_target_pairs={{0,5},{1,4},{2,7},{3,6},{4,1},{5,0},{6,3},{7,2},{8,13},{9,12},{10,... | collective-permute-start | bytes 294920 | tf_op jit(solution)/shard_map/ppermute | solution.py:437
  37.6 0.0 collective-permute-done.4.refs_1_
  37.6 1.5 %collective-permute-start.9 = (bf16[384,128]{1,0:T(8,128)(2,1)S(1)}, bf16[384,128]{1,0:T(8,128)(2,1)S(1)}, u32[]{:S(2)}, u32[]{:S(2)}) collective-permute-start(bf16[384,128]{1,0:T(8,128)(2,1)S(1)} %get-tuple-element.26), channel_id=1, source_target_pairs={{0,6},{1,7},{2,4},{3,5},{4,2},{5,3},{6,0},{7,1},{8,14},{9,15},{10,... | collective-permute-start | bytes 294920 | tf_op jit(solution)/shard_map/ppermute | solution.py:437
  39.2 0.0 collective-permute-done.5.refs_2_
  39.2 1.2 %collective-permute-done.6.refs_3_ = bf16[384,128]{1,0:T(8,128)(2,1)S(1)} collective-permute-done((bf16[384,128]{1,0:T(8,128)(2,1)S(1)}, bf16[384,128]{1,0:T(8,128)(2,1)S(1)}, u32[]{:S(2)}, u32[]{:S(2)}) %collective-permute-start.6) | collective-permute-done | bytes 98336 | tf_op jit(solution)/shard_map/ppermute | solution.py:437
  40.4 6.3 %collective-permute-done.7.refs_4_ = bf16[384,128]{1,0:T(8,128)(2,1)S(1)} collective-permute-done((bf16[384,128]{1,0:T(8,128)(2,1)S(1)}, bf16[384,128]{1,0:T(8,128)(2,1)S(1)}, u32[]{:S(2)}, u32[]{:S(2)}) %collective-permute-start.7) | collective-permute-done | bytes 98336 | tf_op jit(solution)/shard_map/ppermute | solution.py:437
  46.7 1.9 %collective-permute-done.8.refs_5_ = bf16[384,128]{1,0:T(8,128)(2,1)S(1)} collective-permute-done((bf16[384,128]{1,0:T(8,128)(2,1)S(1)}, bf16[384,128]{1,0:T(8,128)(2,1)S(1)}, u32[]{:S(2)}, u32[]{:S(2)}) %collective-permute-start.8) | collective-permute-done | bytes 98336 | tf_op jit(solution)/shard_map/ppermute | solution.py:437
  48.6 0.0 collective-permute-done.9.refs_6_
  48.6 0.5 shard_map.55
  49.1 11.7 %all_to_all.5.in_ref = f32[32,8,128]{2,1,0:T(8,128)S(1)} all-to-all(f32[32,8,128]{2,1,0:T(8,128)S(1)} %shard_map.55), channel_id=1, replica_groups=mesh['space'=4,'band'=8] {'space','band'}, dimensions={0} | all-to-all | bytes 262144 | tf_op jit(solution)/shard_map/all_to_all | solution.py:444
  60.7 0.9 %shard_map.56 = (f32[8,64]{1,0:T(8,128)}, f32[8,64]{1,0:T(8,128)}) custom-call(f32[32,8,128]{2,1,0:T(8,128)S(1)} %all_to_all.5.in_ref), custom_call_target="tpu_custom_call" | custom-call | flops 1000000 | bytes 1000000 | tf_op jit(solution)/shard_map/pallas_call | solution.py:342
  (1 shorter events, 0.0 us)
Async XLA Ops:
  0.6 1.1 %copy-start = (f32[8,12,16,128]{3,2,1,0:T(8,128)S(1)}, f32[8,12,16,128]{3,2,1,0:T(8,128)}, u32[]{:S(2)}) copy-start(f32[8,12,16,128]{3,2,1,0:T(8,128)} %orbitals_hbm.1) | copy-start | bytes 2359300
  1.8 0.9 %copy-start.1 = (f32[12,16,128]{2,1,0:T(8,128)S(1)}, f32[12,16,128]{2,1,0:T(8,128)}, u32[]{:S(2)}) copy-start(f32[12,16,128]{2,1,0:T(8,128)} %param.3) | copy-start | bytes 294916
  3.5 3.2 %collective-permute-start.1 = (bf16[1920,128]{1,0:T(8,128)(2,1)S(1)}, bf16[1920,128]{1,0:T(8,128)(2,1)S(1)}, u32[]{:S(2)}, u32[]{:S(2)}) collective-permute-start(bf16[1920,128]{1,0:T(8,128)(2,1)S(1)} %get-tuple-element.17), channel_id=1, source_target_pairs={{0,8},{8,0},{16,24},{24,16},{1,9},{9,1},{17,25},{25,17},{2,10},{10... | collective-permute-start | bytes 1474568 | tf_op jit(solution)/shard_map/ppermute | solution.py:387
  4.0 14.1 %collective-permute-start = (bf16[1920,128]{1,0:T(8,128)(2,1)S(1)}, bf16[1920,128]{1,0:T(8,128)(2,1)S(1)}, u32[]{:S(2)}, u32[]{:S(2)}) collective-permute-start(bf16[1920,128]{1,0:T(8,128)(2,1)S(1)} %get-tuple-element.15), channel_id=1, source_target_pairs={{0,24},{8,16},{16,8},{24,0},{1,25},{9,17},{17,9},{25,1},{2,26},{10... | collective-permute-start | bytes 1474568 | tf_op jit(solution)/shard_map/ppermute | solution.py:386
  18.2 3.7 %collective-permute-start.2 = (bf16[768,128]{1,0:T(8,128)(2,1)S(1)}, bf16[768,128]{1,0:T(8,128)(2,1)S(1)}, u32[]{:S(2)}, u32[]{:S(2)}) collective-permute-start(bf16[768,128]{1,0:T(8,128)(2,1)S(1)} %shard_map.51), channel_id=1, source_target_pairs={{0,8},{8,0},{16,24},{24,16},{1,9},{9,1},{17,25},{25,17},{2,10},{10... | collective-permute-start | bytes 589832 | tf_op jit(solution)/shard_map/ppermute | solution.py:398
  21.5 3.8 %collective-permute-start.3 = (bf16[768,128]{1,0:T(8,128)(2,1)S(1)}, bf16[768,128]{1,0:T(8,128)(2,1)S(1)}, u32[]{:S(2)}, u32[]{:S(2)}) collective-permute-start(bf16[768,128]{1,0:T(8,128)(2,1)S(1)} %get-tuple-element.21), channel_id=1, source_target_pairs={{0,8},{8,0},{16,24},{24,16},{1,9},{9,1},{17,25},{25,17},{2,10},{10... | collective-permute-start | bytes 589832 | tf_op jit(solution)/shard_map/ppermute | solution.py:407
  26.3 8.4 %collective-permute-start.10 = (bf16[384,128]{1,0:T(8,128)(2,1)S(1)}, bf16[384,128]{1,0:T(8,128)(2,1)S(1)}, u32[]{:S(2)}, u32[]{:S(2)}) collective-permute-start(bf16[384,128]{1,0:T(8,128)(2,1)S(1)} %get-tuple-element.25), channel_id=1, source_target_pairs={{0,7},{1,6},{2,5},{3,4},{4,3},{5,2},{6,1},{7,0},{8,15},{9,14},{10,... | collective-permute-start | bytes 294920 | tf_op jit(solution)/shard_map/ppermute | solution.py:437
  30.7 6.9 %collective-permute-start.4 = (bf16[384,128]{1,0:T(8,128)(2,1)S(1)}, bf16[384,128]{1,0:T(8,128)(2,1)S(1)}, u32[]{:S(2)}, u32[]{:S(2)}) collective-permute-start(bf16[384,128]{1,0:T(8,128)(2,1)S(1)} %get-tuple-element.31), channel_id=1, source_target_pairs={{0,1},{1,0},{2,3},{3,2},{4,5},{5,4},{6,7},{7,6},{8,9},{9,8},{10,11... | collective-permute-start | bytes 294920 | tf_op jit(solution)/shard_map/ppermute | solution.py:437
  31.3 7.9 %collective-permute-start.5 = (bf16[384,128]{1,0:T(8,128)(2,1)S(1)}, bf16[384,128]{1,0:T(8,128)(2,1)S(1)}, u32[]{:S(2)}, u32[]{:S(2)}) collective-permute-start(bf16[384,128]{1,0:T(8,128)(2,1)S(1)} %get-tuple-element.30), channel_id=1, source_target_pairs={{0,2},{1,3},{2,0},{3,1},{4,6},{5,7},{6,4},{7,5},{8,10},{9,11},{10,... | collective-permute-start | bytes 294920 | tf_op jit(solution)/shard_map/ppermute | solution.py:437
  31.3 9.1 %collective-permute-start.6 = (bf16[384,128]{1,0:T(8,128)(2,1)S(1)}, bf16[384,128]{1,0:T(8,128)(2,1)S(1)}, u32[]{:S(2)}, u32[]{:S(2)}) collective-permute-start(bf16[384,128]{1,0:T(8,128)(2,1)S(1)} %get-tuple-element.29), channel_id=1, source_target_pairs={{0,3},{1,2},{2,1},{3,0},{4,7},{5,6},{6,5},{7,4},{8,11},{9,10},{10,... | collective-permute-start | bytes 294920 | tf_op jit(solution)/shard_map/ppermute | solution.py:437
  34.2 12.5 %collective-permute-start.7 = (bf16[384,128]{1,0:T(8,128)(2,1)S(1)}, bf16[384,128]{1,0:T(8,128)(2,1)S(1)}, u32[]{:S(2)}, u32[]{:S(2)}) collective-permute-start(bf16[384,128]{1,0:T(8,128)(2,1)S(1)} %get-tuple-element.28), channel_id=1, source_target_pairs={{0,4},{1,5},{2,6},{3,7},{4,0},{5,1},{6,2},{7,3},{8,12},{9,13},{10,... | collective-permute-start | bytes 294920 | tf_op jit(solution)/shard_map/ppermute | solution.py:437
  34.7 13.9 %collective-permute-start.8 = (bf16[384,128]{1,0:T(8,128)(2,1)S(1)}, bf16[384,128]{1,0:T(8,128)(2,1)S(1)}, u32[]{:S(2)}, u32[]{:S(2)}) collective-permute-start(bf16[384,128]{1,0:T(8,128)(2,1)S(1)} %get-tuple-element.27), channel_id=1, source_target_pairs={{0,5},{1,4},{2,7},{3,6},{4,1},{5,0},{6,3},{7,2},{8,13},{9,12},{10,... | collective-permute-start | bytes 294920 | tf_op jit(solution)/shard_map/ppermute | solution.py:437
  37.6 10.9 %collective-permute-start.9 = (bf16[384,128]{1,0:T(8,128)(2,1)S(1)}, bf16[384,128]{1,0:T(8,128)(2,1)S(1)}, u32[]{:S(2)}, u32[]{:S(2)}) collective-permute-start(bf16[384,128]{1,0:T(8,128)(2,1)S(1)} %get-tuple-element.26), channel_id=1, source_target_pairs={{0,6},{1,7},{2,4},{3,5},{4,2},{5,3},{6,0},{7,1},{8,14},{9,15},{10,... | collective-permute-start | bytes 294920 | tf_op jit(solution)/shard_map/ppermute | solution.py:437

commit v3 on v2

v3 whole, which is shorter than its diff:
```python
import functools

import jax
import jax.numpy as jnp
from jax import lax
from jax.experimental import pallas as pl
from jax.experimental.pallas import tpu as pltpu
from jax.sharding import PartitionSpec as P

STENCIL = (
    -5369.0 / 1800.0,
    12.0 / 7.0,
    -15.0 / 56.0,
    10.0 / 189.0,
    -1.0 / 112.0,
    2.0 / 1925.0,
    -1.0 / 16632.0,
)
WIDTH = 6
BF16 = jnp.bfloat16
F32 = jnp.float32
VMEM = pl.BlockSpec(memory_space=pltpu.VMEM)

GROUP = 8

H_FACTORS = tuple(-0.5 * c for c in STENCIL[1:])
H_CENTER = -1.5 * STENCIL[0]
L_FACTORS = tuple(0.125 * c for c in H_FACTORS)
L_CENTER = (H_CENTER - 9.0) / 8.0


def aligned(start, size):
    return pl.ds(pl.multiple_of(start, size), size)


def low_part(block):
    return block - block.astype(BF16).astype(F32)


def circulant(ny):
    row = lax.broadcasted_iota(jnp.int32, (ny, ny), 0)
    column = lax.broadcasted_iota(jnp.int32, (ny, ny), 1)
    apart = jnp.abs(row - column)
    apart = jnp.minimum(apart, ny - apart)
    matrix = jnp.zeros((ny, ny), F32)
    for k in range(1, WIDTH + 1):
        matrix = jnp.where(apart == k, H_FACTORS[k - 1] / H_FACTORS[0], matrix)
    matrix = matrix.astype(BF16)
    return jnp.concatenate([matrix, matrix], axis=0)


def along_y(matrix, source, start, count, y_ref, plane_rows):
    step = min(count, WIDTH)
    for i in range(0, count, step):
        block = source[pl.ds((start + i) * plane_rows, step * plane_rows), :]
        parts = jnp.concatenate([block.astype(BF16), low_part(block).astype(BF16)], axis=1)
        y_ref[pl.ds(i * plane_rows, step * plane_rows), :] = jnp.dot(
            parts, matrix, preferred_element_type=F32
        )


def apply_planes(matrix, source, start, count, nx, y_ref, levels, level, linear, emit):
    plane_rows = nx * GROUP
    along_y(matrix, source, start, count, y_ref, plane_rows)
    factors = L_FACTORS if linear else H_FACTORS

    def load(row):
        return source[aligned(row, GROUP), :]

    @pl.loop(0, count)
    def _(i):
        where = (start + i) * plane_rows
        center = [load(where + x * GROUP) for x in range(nx)]
        values = []
        for x in range(nx):
            row = levels[pl.ds((level + i) * nx + x, 1), :]
            row = 0.125 * row + L_CENTER if linear else row + H_CENTER
            total = jnp.broadcast_to(row, center[x].shape) * center[x]
            total = total + factors[0] * y_ref[aligned(i * plane_rows + x * GROUP, GROUP), :]
            for k in range(1, WIDTH + 1):
                near = load(where + k * plane_rows + x * GROUP) + load(where - k * plane_rows + x * GROUP)
                near = near + (center[(x + k) % nx] + center[(x - k) % nx])
                total = total + factors[k - 1] * near
            values.append(total)
        emit(i, values, center)


def prepare_kernel(
    planes, nx, orbitals_hbm, potential_hbm, own_ref, level_ref, near_ref, far_ref, core_ref,
    orbitals, potential, semaphores,
):
    plane_rows = nx * GROUP
    rows = planes * nx
    side = WIDTH * plane_rows
    parts = semaphores.shape[0] - 1
    each = planes // parts
    odd = lax.rem(lax.axis_index("space"), 2)

    def fetch(i):
        at = pl.ds(i * each, each)
        return pltpu.make_async_copy(orbitals_hbm.at[:, at], orbitals.at[:, at], semaphores.at[i])

    fetch_levels = pltpu.make_async_copy(potential_hbm, potential, semaphores.at[parts])
    for i in range(parts):
        fetch(i).start()
    fetch_levels.start()
    cells = orbitals.reshape(GROUP * rows, orbitals.shape[-1])
    for i in range(parts):
        fetch(i).wait()

        @pl.loop(i * each, (i + 1) * each)
        def _(plane):
            target = lax.select(odd == 1, planes - 1 - plane, plane) * plane_rows
            for x in range(0, nx, 2):
                row = plane * nx + x
                both = jnp.concatenate(
                    [cells[pl.ds(row + j, GROUP, stride=rows), :] for j in range(2)], axis=0
                )
                at = aligned(target + x * GROUP, 2 * GROUP)
                own_ref[at, :] = both
                core_ref[at, :] = both.astype(BF16)

    near_ref[pl.ds(0, side), :] = core_ref[pl.ds(0, side), :]
    far_ref[pl.ds(0, side), :] = core_ref[pl.ds(side, side), :]
    size = planes * plane_rows
    for out_ref, plane, at in ((near_ref, 0, side), (core_ref, planes - 1, size)):
        block = own_ref[pl.ds(plane * plane_rows, plane_rows), :]
        out_ref[pl.ds(at, plane_rows), :] = low_part(block).astype(BF16)
    fetch_levels.wait()
    for plane in range(planes):
        source = lax.select(odd == 1, planes - 1 - plane, plane) * nx
        block = potential[aligned(source, nx), :]
        level_ref[pl.ds(plane * nx, nx), :] = block
        core_ref[pl.ds(size + plane_rows + plane * nx, nx), :] = block.astype(BF16)
        if plane < WIDTH:
            near_ref[pl.ds(side + plane_rows + plane * nx, nx), :] = block.astype(BF16)
        else:
            far_ref[pl.ds(side + (plane - WIDTH) * nx, nx), :] = block.astype(BF16)
        if plane < NEAR:
            at = side + plane_rows + (WIDTH + plane) * nx
            near_ref[pl.ds(at, nx), :] = low_part(block).astype(BF16)
        if plane >= planes - NEAR:
            at = size + plane_rows + (planes + plane - (planes - NEAR)) * nx
            core_ref[pl.ds(at, nx), :] = low_part(block).astype(BF16)


NEAR = 2


def place_planes(message, count, field, where, step, plane_rows):
    for i in range(count):
        block = message[pl.ds(i * plane_rows, plane_rows), :]
        field[pl.ds((where + step * i) * plane_rows, plane_rows), :] = block.astype(F32)


def add_low(message, planes, field, where, plane_rows):
    at = pl.ds(where * plane_rows, plane_rows)
    field[at, :] = field[at, :] + message[pl.ds(planes * plane_rows, plane_rows), :].astype(F32)


def place_levels(message, extra, count, nx, levels, where, near):
    for i in range(count):
        block = message[pl.ds(extra + i * nx, nx), :].astype(F32)
        if near <= i < near + NEAR:
            block = block + message[pl.ds(extra + (count + i - near) * nx, nx), :].astype(F32)
        levels[pl.ds((where - i) * nx, nx), :] = block


def store_planes(nx, *refs):
    def emit(i, values, center):
        for x in range(nx):
            for ref, first in refs:
                ref[aligned(((first + i) * nx + x) * GROUP, GROUP), :] = values[x]

    return emit


def store_second(nx, before, start, *refs):
    def emit(i, values, center):
        for x in range(nx):
            row = (i * nx + x) * GROUP
            value = 2.0 * values[x] - before[aligned(start * nx * GROUP + row, GROUP), :]
            for ref, first in refs:
                ref[aligned(first * nx * GROUP + row, GROUP), :] = value

    return emit


def early_kernel(planes, nx, own_ref, level_ref, core_ref, first_ref, field, levels, y_ref):
    plane_rows = nx * GROUP
    field[pl.ds(0, planes * plane_rows), :] = own_ref[...]
    place_planes(core_ref, planes, field, 2 * planes - 1, -1, plane_rows)
    add_low(core_ref, planes, field, planes, plane_rows)
    levels[pl.ds(0, planes * nx), :] = level_ref[...]
    extra = (planes + 1) * plane_rows
    place_levels(core_ref, extra, planes, nx, levels, 2 * planes - 1, planes - NEAR)
    matrix = circulant(y_ref.shape[1])
    apply_planes(
        matrix, field, WIDTH, 2 * planes - 2 * WIDTH, nx, y_ref, levels, WIDTH, True,
        store_planes(nx, (first_ref, 0)),
    )


def pass_kernel(after_ref, in_ref, out_ref):
    del after_ref
    out_ref[...] = in_ref[...]


def near_kernel(
    planes, nx, own_ref, level_ref, near_ref, early_ref, first_ref, second_ref, core_ref,
    field, first, y_ref,
):
    plane_rows = nx * GROUP
    side = WIDTH * plane_rows
    place_planes(near_ref, WIDTH, field, WIDTH - 1, -1, plane_rows)
    add_low(near_ref, WIDTH, field, WIDTH - 1, plane_rows)
    field[pl.ds(side, 2 * side), :] = own_ref[...]
    first[pl.ds(side, 2 * side), :] = early_ref[...]
    matrix = circulant(y_ref.shape[1])
    apply_planes(
        matrix, field, WIDTH, WIDTH, nx, y_ref, level_ref, 0, True,
        store_planes(nx, (first_ref, 0), (first, 0)),
    )
    apply_planes(
        matrix, first, WIDTH, WIDTH, nx, y_ref, level_ref, WIDTH, True,
        store_second(nx, own_ref, WIDTH, (second_ref, 0)),
    )
    core_ref[...] = second_ref[...].astype(BF16)


def middle_kernel(
    planes, nx, own_ref, level_ref, near_ref, far_ref, early_ref, beside_first_ref,
    first_ref, second_ref, field, levels, first, y_ref,
):
    plane_rows = nx * GROUP
    side = WIDTH * plane_rows
    place_planes(far_ref, WIDTH, field, WIDTH - 1, -1, plane_rows)
    place_planes(near_ref, WIDTH, field, planes - 1, -1, plane_rows)
    add_low(near_ref, WIDTH, field, planes - 1, plane_rows)
    field[pl.ds(2 * side, side), :] = own_ref[pl.ds(0, side), :]
    place_levels(near_ref, side + plane_rows, WIDTH, nx, levels, WIDTH - 1, 0)
    first[pl.ds(side, side), :] = beside_first_ref[...]
    first[pl.ds(2 * side, side), :] = early_ref[pl.ds(0, side), :]
    matrix = circulant(y_ref.shape[1])
    apply_planes(
        matrix, field, WIDTH, WIDTH, nx, y_ref, levels, 0, True,
        store_planes(nx, (first_ref, 0), (first, 0)),
    )
    apply_planes(
        matrix, first, WIDTH, WIDTH, nx, y_ref, level_ref, 0, True,
        store_second(nx, own_ref, 0, (second_ref, 0)),
    )


def right_kernel(
    planes, nx, level_ref, beside_ref, second_ref, beyond_ref, pairs_ref, second, y_ref,
):
    plane_rows = nx * GROUP
    side = WIDTH * plane_rows
    second[pl.ds(0, side), :] = second_ref[...]
    second[pl.ds(side, side), :] = beyond_ref[...]
    place_planes(beside_ref, WIDTH, second, 3 * WIDTH - 1, -1, plane_rows)
    matrix = circulant(y_ref.shape[1])
    apply_planes(
        matrix, second, WIDTH, WIDTH, nx, y_ref, level_ref, WIDTH, False, store_pairs(pairs_ref, 0, nx)
    )


def left_kernel(
    planes, nx, level_ref, near_ref, far_ref, relay_ref, first_low_ref, first_ref, second_ref,
    beyond_ref, right_ref, out_ref, field, levels, first, second, y_ref, pairs,
):
    plane_rows = nx * GROUP
    side = WIDTH * plane_rows
    place_planes(relay_ref, WIDTH, field, 0, 1, plane_rows)
    place_planes(far_ref, WIDTH, field, 2 * WIDTH - 1, -1, plane_rows)
    place_planes(near_ref, WIDTH, field, 3 * WIDTH - 1, -1, plane_rows)
    add_low(near_ref, WIDTH, field, 3 * WIDTH - 1, plane_rows)
    place_levels(far_ref, side, WIDTH, nx, levels, WIDTH - 1, WIDTH)
    place_levels(near_ref, side + plane_rows, WIDTH, nx, levels, 2 * WIDTH - 1, 0)
    first[pl.ds(side, side), :] = first_low_ref[...]
    first[pl.ds(2 * side, side), :] = first_ref[...]
    second[pl.ds(side, side), :] = second_ref[...]
    second[pl.ds(2 * side, side), :] = beyond_ref[...]
    matrix = circulant(y_ref.shape[1])
    apply_planes(
        matrix, field, WIDTH, WIDTH, nx, y_ref, levels, 0, True, store_planes(nx, (first, 0))
    )
    apply_planes(
        matrix, first, WIDTH, WIDTH, nx, y_ref, levels, WIDTH, True,
        store_second(nx, field, 2 * WIDTH, (second, 0)),
    )
    apply_planes(
        matrix, second, WIDTH, WIDTH, nx, y_ref, level_ref, 0, False, store_pairs(pairs, 0, nx)
    )
    band, height, _ = out_ref.shape
    me = lax.axis_index("band")
    for i in range(band // 2):
        at = pl.ds(i * height, height)
        out_ref[i ^ me] = pairs[at, :]
        out_ref[(band // 2 + i) ^ me] = right_ref[at, :]


def write_kernel(planes, nx, second_ref, beyond_ref, filtered_ref, done_ref):
    done_ref[...] = jnp.zeros_like(done_ref)
    rows = planes * nx
    odd = lax.rem(lax.axis_index("space"), 2)
    for ref, first in ((second_ref, 0), (beyond_ref, WIDTH)):

        @pl.loop(0, WIDTH)
        def _(i):
            plane = first + i
            target = lax.select(odd == 1, planes - 1 - plane, plane) * nx
            for x in range(nx):
                value = ref[aligned((i * nx + x) * GROUP, GROUP), :]
                filtered_ref[pl.ds(target + x, GROUP, stride=rows), :] = value


def store_pairs(ref, first, nx):
    def emit(i, values, center):
        for x in range(nx):
            pair = jnp.concatenate([center[x], values[x]], axis=0).astype(BF16)
            ref[aligned(((first + i) * nx + x) * 2 * GROUP, 2 * GROUP), :] = pair

    return emit


def gram_kernel(space, steps, order, *refs):
    after_ref, *blocks, out_ref, held = refs
    del after_ref
    band = len(blocks)
    width = 2 * GROUP
    me = lax.axis_index("band")
    for k, block in zip(order, blocks):
        held[k ^ me] = block[...]
    total = jnp.zeros((band * width, band * width), F32)
    for step in range(0, steps, 2):
        block = jnp.concatenate(
            [held[:, pl.ds((step + i) * width, width), :].reshape(band * width, -1) for i in range(2)],
            axis=1,
        )
        total = total + lax.dot_general(
            block, block, (((1,), (1,)), ((), ())), preferred_element_type=F32
        )
    lanes = lax.broadcasted_iota(jnp.int32, (GROUP, band * width), 1)
    for b in range(band):
        narrow = total[b * width : b * width + GROUP]
        applied = pltpu.roll(total[b * width + GROUP : (b + 1) * width], GROUP, 1)
        piece = jnp.where(lanes % width < GROUP, narrow, applied)
        for s in range(space):
            out_ref[s * band + b] = piece


def sum_kernel(scale, in_ref, intersection_ref, projected_ref):
    total = in_ref[0]
    for i in range(1, in_ref.shape[0]):
        total = total + in_ref[i]
    total = total * scale
    lanes, columns = total.shape[1], intersection_ref.shape[1]
    source = lax.broadcasted_iota(jnp.int32, (lanes, columns), 0)
    target = lax.broadcasted_iota(jnp.int32, (lanes, columns), 1)
    place = (target // GROUP) * (2 * GROUP) + target % GROUP
    for offset, ref in ((0, intersection_ref), (GROUP, projected_ref)):
        pick = jnp.where(source == place + offset, 1.0, 0.0).astype(F32)
        ref[...] = jnp.dot(total, pick, precision=lax.Precision.HIGHEST, preferred_element_type=F32)


ORDER = (1, 2, 4, 6, 5, 7, 3)


def call(kernel, outs, *args, scratch=(), hbm_in=0, hbm_out=(), vmem=40, flops=1000000):
    anywhere = pl.BlockSpec(memory_space=pl.ANY)
    return pl.pallas_call(
        kernel,
        out_shape=outs,
        in_specs=[anywhere] * hbm_in + [VMEM] * (len(args) - hbm_in),
        out_specs=tuple(anywhere if i in hbm_out else VMEM for i in range(len(outs))),
        scratch_shapes=list(scratch),
        compiler_params=pltpu.CompilerParams(vmem_limit_bytes=int(vmem * 2**20)),
        cost_estimate=pl.CostEstimate(flops=flops, bytes_accessed=1000000, transcendentals=0),
    )(*args)


def shifts(axis):
    count = lax.axis_size(axis)
    up = [(i, (i + 1) % count) for i in range(count)]
    return up, [(j, i) for i, j in up]


def local_kernels(orbitals, potential):
    count, planes, nx, ny = orbitals.shape
    space, band = lax.axis_size("space"), lax.axis_size("band")
    rows = planes * nx
    plane_rows = nx * GROUP
    size = planes * plane_rows
    struct = jax.ShapeDtypeStruct
    other_core = [(i, i ^ 1) for i in range(space)]
    other_chip = [(i, i ^ 3) for i in range(space)]

    def f32_planes(many, height=plane_rows):
        return pltpu.VMEM((many * height, ny), F32)

    def bf16_rows(height):
        return struct((height, ny), BF16)

    half = WIDTH * plane_rows
    slab, half_slab = struct((size, ny), F32), struct((half, ny), F32)
    parts = 4
    own, levels, to_near, to_far, to_core = call(
        functools.partial(prepare_kernel, planes, nx),
        (
            slab,
            struct((rows, ny), F32),
            bf16_rows(half + plane_rows + (WIDTH + NEAR) * nx),
            bf16_rows(half + WIDTH * nx),
            bf16_rows(size + plane_rows + (planes + NEAR) * nx),
        ),
        orbitals, potential.reshape(rows, ny),
        hbm_in=2, vmem=52,
        scratch=[
            pltpu.VMEM(orbitals.shape, F32),
            pltpu.VMEM((rows, ny), F32),
            pltpu.SemaphoreType.DMA((parts + 1,)),
        ],
    )
    near = lax.ppermute(to_near, "space", other_chip)
    core = lax.ppermute(to_core, "space", other_core)
    far = lax.ppermute(to_far, "space", other_chip)
    (early,) = call(
        functools.partial(early_kernel, planes, nx),
        (slab,),
        own, levels, core,
        scratch=[f32_planes(2 * planes), f32_planes(2 * planes, nx), f32_planes(planes)],
    )
    wide = planes + WIDTH
    first, beyond, to_beside = call(
        functools.partial(near_kernel, planes, nx),
        (half_slab, half_slab, bf16_rows(half)),
        own, levels, near, early,
        scratch=[f32_planes(wide), f32_planes(wide), f32_planes(WIDTH)],
    )
    beside = lax.ppermute(to_beside, "space", other_core)
    (relay,) = call(pass_kernel, (bf16_rows(half + WIDTH * nx),), first, far, hbm_in=1)
    relay = lax.ppermute(relay, "space", other_core)
    first_low, second = call(
        functools.partial(middle_kernel, planes, nx),
        (half_slab, half_slab),
        own, levels, near, far, early, first,
        scratch=[f32_planes(wide), f32_planes(WIDTH, nx), f32_planes(wide), f32_planes(WIDTH)],
    )
    (right,) = call(
        functools.partial(right_kernel, planes, nx),
        (bf16_rows(WIDTH * nx * 2 * GROUP),),
        levels, beside, second, beyond,
        scratch=[f32_planes(wide), f32_planes(WIDTH)],
    )
    steps = rows // band
    block = (steps * 2 * GROUP, ny)
    (pairs,) = call(
        functools.partial(left_kernel, planes, nx),
        (struct((band, *block), BF16),),
        levels, near, far, relay, first_low, first, second, beyond, right,
        scratch=[
            f32_planes(wide),
            f32_planes(planes, nx),
            f32_planes(wide),
            f32_planes(wide),
            f32_planes(WIDTH),
            pltpu.VMEM((WIDTH * nx * 2 * GROUP, ny), BF16),
        ],
    )
    filtered, written = call(
        functools.partial(write_kernel, planes, nx),
        (struct((count * rows, ny), F32), struct((GROUP, ny), F32)),
        second, beyond,
    )
    order = (0,) + ORDER[::-1]
    blocks = [
        lax.ppermute(pairs[k], "band", [(i, i ^ k) for i in range(band)]) if k else pairs[k]
        for k in order
    ]
    (pieces,) = call(
        functools.partial(gram_kernel, space, steps, order),
        (struct((space * band, GROUP, band * 2 * GROUP), F32),),
        written, *blocks,
        hbm_in=1,
        scratch=[pltpu.VMEM((band, *block), BF16)],
    )
    pieces = lax.all_to_all(pieces, ("space", "band"), 0, 0, tiled=True)
    rows_out = struct((count, count * band), F32)
    intersection, projected = call(
        functools.partial(sum_kernel, 1.0 / (rows * ny * space)), (rows_out, rows_out), pieces
    )
    return filtered.reshape(orbitals.shape), intersection, projected


def padded(cells, width):
    up, down = shifts("space")
    head, tail = cells[:, :width], cells[:, cells.shape[1] - width :]
    return jnp.concatenate(
        [lax.ppermute(tail, "space", up), cells, lax.ppermute(head, "space", down)], axis=1
    )


def hamiltonian(beside, potential):
    planes = beside.shape[1] - 2 * WIDTH
    center = beside[:, WIDTH : WIDTH + planes]
    summed = 3.0 * STENCIL[0] * center
    for k in range(1, WIDTH + 1):
        near = beside[:, WIDTH + k : WIDTH + k + planes] + beside[:, WIDTH - k : WIDTH - k + planes]
        for dim in (2, 3):
            near = near + (jnp.roll(center, k, dim) + jnp.roll(center, -k, dim))
        summed = summed + STENCIL[k] * near
    return -0.5 * summed + potential * center


def local_plain(orbitals, potential):
    def step(field):
        return (hamiltonian(padded(field, WIDTH), potential) - 9.0 * field) * 0.125

    filtered = 2.0 * step(step(orbitals)) - orbitals
    beside = padded(filtered.astype(BF16), WIDTH).astype(F32)
    applied = hamiltonian(beside, potential).astype(BF16)
    count = orbitals.shape[0]
    narrow = filtered.astype(BF16).reshape(count, -1)
    applied = applied.reshape(count, -1)
    everyone = lax.all_gather(narrow, "band", axis=0, tiled=True)
    contract = (((1,), (1,)), ((), ()))
    parts = [
        lax.dot_general(rows, everyone, contract, preferred_element_type=F32)
        for rows in (narrow, applied)
    ]
    scale = 1.0 / (narrow.shape[1] * lax.axis_size("space"))
    intersection, projected = lax.psum(tuple(parts), "space")
    return filtered, intersection * scale, projected * scale


def local(orbitals, potential):
    count, planes, nx, ny = orbitals.shape
    band = lax.axis_size("band")
    fits = (
        count == GROUP
        and lax.axis_size("space") == 4
        and planes == 2 * WIDTH
        and nx == 16
        and ny == 128
        and band * 2 * GROUP == 128
        and (planes * nx) % (2 * band) == 0
    )
    return (local_kernels if fits else local_plain)(orbitals, potential)


def solution(mesh):
    return jax.shard_map(
        local,
        mesh=mesh,
        in_specs=(P("band", "space", None, None), P("space", None, None)),
        out_specs=(P("band", "space", None, None), P("band", None), P("band", None)),
        check_vma=False,
    )
```

time: 61.8 us -> 59.8 us (0.968)
  waiting for transfers between devices: 19.8 us -> 17.8 us
  Pallas kernels: 11.1 us -> 12.9 us
  starting transfers between devices: 16.2 us -> 14.7 us
  local copies, waits for them, and re-layouts: 2.07 us -> 0.94 us
  blocking collectives: 11.7 us -> 12.5 us
    ppermute x3 -> x4, waiting for transfers between devices: 9.96 us -> 8.04 us  [the longest x1 5.19 us: local_kernels(): near = lax.ppermute(to_near, 'space', other_chip)]
    pallas_call x8 -> x10, Pallas kernels: 11.1 us -> 12.9 us  [call(): pl.pallas_call(kernel, out_shape=outs, in_specs=[anywhere] * hbm_in + [VM...]
    ppermute x7, starting transfers between devices: 12.4 us -> 11 us  [local_kernels(): lax.ppermute(pairs[k], 'band', [(i, i ^ k) for i in range(band)])]
    unnamed x4 -> x2, local copies, waits for them, and re-layouts: 2.02 us -> 0.89 us
    all_to_all x1, blocking collectives: 11.7 us -> 12.5 us  [local_kernels(): pieces = lax.all_to_all(pieces, ('space', 'band'), 0, 0, tiled=True)]
    ppermute x3 -> x4, starting transfers between devices: 3.29 us -> 3.24 us  [the longest x1 2.64 us: local_kernels(): near = lax.ppermute(to_near, 'space', other_chip)]
  transfers between devices with their start and end apart: 11 -> 12, of which waited for: 5 -> 4; matrix products, arithmetic and copies ran while one was open for 0% -> 0% of each run, Pallas kernels for 13% -> 12%
where the time goes in v3:
time: 59.8 us; the launch traced here: 59.6 us
  waiting for transfers between devices  17.8 us (30%)
  starting transfers between devices  14.7 us (25%)
  Pallas kernels  12.9 us (22%)
  blocking collectives  12.5 us (21%)
  local copies, waits for them, and re-layouts  0.94 us (2%)
  between operations  0.72 us (1%)
    pallas_call x10, Pallas kernels, call(): pl.pallas_call(kernel, out_shape=outs, in_specs=[anywhere] * hbm_in + [VM...  12.9 us
    all_to_all x1, blocking collectives, local_kernels(): pieces = lax.all_to_all(pieces, ('space', 'band'), 0, 0, tiled=True)  12.5 us
    ppermute x7, starting transfers between devices, local_kernels(): lax.ppermute(pairs[k], 'band', [(i, i ^ k) for i in range(band)])  11 us
    ppermute x7, waiting for transfers between devices, local_kernels(): lax.ppermute(pairs[k], 'band', [(i, i ^ k) for i in range(band)])  9.77 us
    ppermute x1, waiting for transfers between devices, local_kernels(): near = lax.ppermute(to_near, 'space', other_chip)  5.19 us
    ppermute x1, waiting for transfers between devices, local_kernels(): far = lax.ppermute(to_far, 'space', other_chip)  2.85 us
    ppermute x1, starting transfers between devices, local_kernels(): near = lax.ppermute(to_near, 'space', other_chip)  2.64 us
  transfers between devices with their start and end apart: 12, of which 4 were waited for; matrix products, arithmetic and copies ran while one was open for 0% of the time, Pallas kernels for 12%

profile of v3, /device:TPU:0, one launch (start us, length us, event | category | flops | bytes accessed | tf_op | source)
XLA Modules:
  0.0 59.6 jit_solution(3263983761266266059)
XLA Ops:
  0.6 0.0 copy-start
  0.6 0.9 %copy-done = f32[12,16,128]{2,1,0:T(8,128)S(1)} copy-done((f32[12,16,128]{2,1,0:T(8,128)S(1)}, f32[12,16,128]{2,1,0:T(8,128)}, u32[]{:S(2)}) %copy-start) | copy-done | bytes 98328
  1.5 1.6 %shard_map.49 = (f32[1536,128]{1,0:T(8,128)S(1)}, f32[192,128]{1,0:T(8,128)S(1)}, bf16[1024,128]{1,0:T(8,128)(2,1)S(1)}, bf16[864,128]{1,0:T(8,128)(2,1)S(1)}, bf16[1888,128]{1,0:T(8,128)(2,1)S(1)}) custom-call(f32[8,12,16,128]{3,2,1,0:T(8,128)} %orbitals_hbm.1, f32[192,128]{1,0:T(8,128)S(1)} %bitcast.18), custom_call_target="tpu_custom_call" | custom-call | flops 1000000 | bytes 1000000 | tf_op jit(solution)/shard_map/pallas_call | solution.py:373
  3.1 0.5 collective-permute-start.2
  3.6 2.6 %collective-permute-start = (bf16[1024,128]{1,0:T(8,128)(2,1)S(1)}, bf16[1024,128]{1,0:T(8,128)(2,1)S(1)}, u32[]{:S(2)}, u32[]{:S(2)}) collective-permute-start(bf16[1024,128]{1,0:T(8,128)(2,1)S(1)} %get-tuple-element.19), channel_id=1, source_target_pairs={{0,24},{8,16},{16,8},{24,0},{1,25},{9,17},{17,9},{25,1},{2,26},{10... | collective-permute-start | bytes 786440 | tf_op jit(solution)/shard_map/ppermute | solution.py:426
  6.3 0.0 collective-permute-start.1
  6.3 0.0 collective-permute-done.2.core_ref
  6.3 1.4 %shard_map.50.early_ref = f32[1536,128]{1,0:T(8,128)S(1)} custom-call(f32[1536,128]{1,0:T(8,128)S(1)} %get-tuple-element.17.own_ref, f32[192,128]{1,0:T(8,128)S(1)} %get-tuple-element.18.level_ref, bf16[1888,128]{1,0:T(8,128)(2,1)S(1)} %collective-permute-done.2.core_ref), custom_call_target="tpu_custom_call" | custom-call | flops 1000000 | bytes 1000000 | tf_op jit(solution)/shard_map/pallas_call | solution.py:373
  7.7 5.2 %collective-permute-done.near_ref = bf16[1024,128]{1,0:T(8,128)(2,1)S(1)} collective-permute-done((bf16[1024,128]{1,0:T(8,128)(2,1)S(1)}, bf16[1024,128]{1,0:T(8,128)(2,1)S(1)}, u32[]{:S(2)}, u32[]{:S(2)}) %collective-permute-start) | collective-permute-done | bytes 262176 | tf_op jit(solution)/shard_map/ppermute | solution.py:426
  12.9 1.8 %shard_map.51 = (f32[768,128]{1,0:T(8,128)S(1)}, f32[768,128]{1,0:T(8,128)S(1)}, bf16[768,128]{1,0:T(8,128)(2,1)S(1)}) custom-call(f32[1536,128]{1,0:T(8,128)S(1)} %get-tuple-element.17.own_ref, f32[192,128]{1,0:T(8,128)S(1)} %get-tuple-element.18.level_ref, bf16[1024,128]{1,0:T(8,128)(2,1)S(1)} %collective-permute-done.near_ref, ...), custom_call_target="tpu_custom_call" | custom-call | flops 1000000 | bytes 1000000 | tf_op jit(solution)/shard_map/pallas_call | solution.py:373
  14.7 2.8 %collective-permute-done.1.far_ref.in_ref = bf16[864,128]{1,0:T(8,128)(2,1)S(1)} collective-permute-done((bf16[864,128]{1,0:T(8,128)(2,1)S(1)}, bf16[864,128]{1,0:T(8,128)(2,1)S(1)}, u32[]{:S(2)}, u32[]{:S(2)}) %collective-permute-start.1) | collective-permute-done | bytes 221216 | tf_op jit(solution)/shard_map/ppermute | solution.py:428
  17.6 0.2 collective-permute-start.3
  17.8 0.4 collective-permute-start.4
  18.2 1.8 %shard_map.52 = (f32[768,128]{1,0:T(8,128)S(1)}, f32[768,128]{1,0:T(8,128)S(1)}) custom-call(f32[1536,128]{1,0:T(8,128)S(1)} %get-tuple-element.17.own_ref, f32[192,128]{1,0:T(8,128)S(1)} %get-tuple-element.18.level_ref, bf16[1024,128]{1,0:T(8,128)(2,1)S(1)} %collective-permute-done.near_ref, bf16[864,128]{1,0:T(8,128)(2,1)S(1)} %collective-permute-done.1.far_ref.in_ref, ...), custom_call_target="tpu_custom_call" | custom-call | flops 1000000 | bytes 1000000 | tf_op jit(solution)/shard_map/pallas_call | solution.py:373
  20.0 0.0 collective-permute-done.4.beside_ref
  20.0 0.9 %shard_map.55.right_ref = bf16[1536,128]{1,0:T(8,128)(2,1)S(1)} custom-call(f32[192,128]{1,0:T(8,128)S(1)} %get-tuple-element.18.level_ref, bf16[768,128]{1,0:T(8,128)(2,1)S(1)} %collective-permute-done.4.beside_ref, f32[768,128]{1,0:T(8,128)S(1)} %get-tuple-element.23.second_ref, f32[768,128]{1,0:T(8,128)S(1)} %get-tuple-element.24.beyond_ref), custom_call_target="tpu_custom_call" | custom-call | flops 1000000 | bytes 1000000 | tf_op jit(solution)/shard_map/pallas_call | solution.py:373
  20.9 0.0 collective-permute-done.3.relay_ref
  20.9 2.7 %shard_map.56 = bf16[8,384,128]{2,1,0:T(8,128)(2,1)S(1)} custom-call(f32[192,128]{1,0:T(8,128)S(1)} %get-tuple-element.18.level_ref, bf16[1024,128]{1,0:T(8,128)(2,1)S(1)} %collective-permute-done.near_ref, bf16[864,128]{1,0:T(8,128)(2,1)S(1)} %collective-permute-done.1.far_ref.in_ref, bf16[864,128]{1,0:T(8,128)(2,1)S(1)} %collective-permute-done.3.relay_ref, ...), custom_call_target="tpu_custom_call" | custom-call | flops 1000000 | bytes 1000000 | tf_op jit(solution)/shard_map/pallas_call | solution.py:373
  23.6 0.1 slice_bitcast_fusion
  23.7 1.5 %collective-permute-start.11 = (bf16[384,128]{1,0:T(8,128)(2,1)S(1)}, bf16[384,128]{1,0:T(8,128)(2,1)S(1)}, u32[]{:S(2)}, u32[]{:S(2)}) collective-permute-start(bf16[384,128]{1,0:T(8,128)(2,1)S(1)} %get-tuple-element.31), channel_id=1, source_target_pairs={{0,1},{1,0},{2,3},{3,2},{4,5},{5,4},{6,7},{7,6},{8,9},{9,8},{10,11... | collective-permute-start | bytes 294920 | tf_op jit(solution)/shard_map/ppermute | solution.py:479
  25.1 1.6 %collective-permute-start.10 = (bf16[384,128]{1,0:T(8,128)(2,1)S(1)}, bf16[384,128]{1,0:T(8,128)(2,1)S(1)}, u32[]{:S(2)}, u32[]{:S(2)}) collective-permute-start(bf16[384,128]{1,0:T(8,128)(2,1)S(1)} %get-tuple-element.32), channel_id=1, source_target_pairs={{0,2},{1,3},{2,0},{3,1},{4,6},{5,7},{6,4},{7,5},{8,10},{9,11},{10,... | collective-permute-start | bytes 294920 | tf_op jit(solution)/shard_map/ppermute | solution.py:479
  26.7 2.6 %collective-permute-start.9 = (bf16[384,128]{1,0:T(8,128)(2,1)S(1)}, bf16[384,128]{1,0:T(8,128)(2,1)S(1)}, u32[]{:S(2)}, u32[]{:S(2)}) collective-permute-start(bf16[384,128]{1,0:T(8,128)(2,1)S(1)} %get-tuple-element.33), channel_id=1, source_target_pairs={{0,4},{1,5},{2,6},{3,7},{4,0},{5,1},{6,2},{7,3},{8,12},{9,13},{10,... | collective-permute-start | bytes 294920 | tf_op jit(solution)/shard_map/ppermute | solution.py:479
  29.3 0.2 collective-permute-start.8
  29.5 1.7 %collective-permute-start.7 = (bf16[384,128]{1,0:T(8,128)(2,1)S(1)}, bf16[384,128]{1,0:T(8,128)(2,1)S(1)}, u32[]{:S(2)}, u32[]{:S(2)}) collective-permute-start(bf16[384,128]{1,0:T(8,128)(2,1)S(1)} %get-tuple-element.35), channel_id=1, source_target_pairs={{0,5},{1,4},{2,7},{3,6},{4,1},{5,0},{6,3},{7,2},{8,13},{9,12},{10,... | collective-permute-start | bytes 294920 | tf_op jit(solution)/shard_map/ppermute | solution.py:479
  31.2 0.0 collective-permute-done.11.refs_8_
  31.2 2.3 %collective-permute-start.6 = (bf16[384,128]{1,0:T(8,128)(2,1)S(1)}, bf16[384,128]{1,0:T(8,128)(2,1)S(1)}, u32[]{:S(2)}, u32[]{:S(2)}) collective-permute-start(bf16[384,128]{1,0:T(8,128)(2,1)S(1)} %get-tuple-element.36), channel_id=1, source_target_pairs={{0,7},{1,6},{2,5},{3,4},{4,3},{5,2},{6,1},{7,0},{8,15},{9,14},{10,... | collective-permute-start | bytes 294920 | tf_op jit(solution)/shard_map/ppermute | solution.py:479
  33.5 0.0 collective-permute-done.10.refs_7_
  33.5 1.2 %collective-permute-start.5 = (bf16[384,128]{1,0:T(8,128)(2,1)S(1)}, bf16[384,128]{1,0:T(8,128)(2,1)S(1)}, u32[]{:S(2)}, u32[]{:S(2)}) collective-permute-start(bf16[384,128]{1,0:T(8,128)(2,1)S(1)} %get-tuple-element.37), channel_id=1, source_target_pairs={{0,3},{1,2},{2,1},{3,0},{4,7},{5,6},{6,5},{7,4},{8,11},{9,10},{10,... | collective-permute-start | bytes 294920 | tf_op jit(solution)/shard_map/ppermute | solution.py:479
  34.7 1.3 %shard_map.53 = (f32[1536,128]{1,0:T(8,128)}, f32[8,128]{1,0:T(8,128)S(1)}) custom-call(f32[768,128]{1,0:T(8,128)S(1)} %get-tuple-element.23.second_ref, f32[768,128]{1,0:T(8,128)S(1)} %get-tuple-element.24.beyond_ref), custom_call_target="tpu_custom_call" | custom-call | flops 1000000 | bytes 1000000 | tf_op jit(solution)/shard_map/pallas_call | solution.py:373
  36.0 5.6 %collective-permute-done.9.refs_6_ = bf16[384,128]{1,0:T(8,128)(2,1)S(1)} collective-permute-done((bf16[384,128]{1,0:T(8,128)(2,1)S(1)}, bf16[384,128]{1,0:T(8,128)(2,1)S(1)}, u32[]{:S(2)}, u32[]{:S(2)}) %collective-permute-start.9) | collective-permute-done | bytes 98336 | tf_op jit(solution)/shard_map/ppermute | solution.py:479
  41.6 0.0 collective-permute-done.8.refs_5_
  41.6 4.2 %collective-permute-done.7.refs_4_ = bf16[384,128]{1,0:T(8,128)(2,1)S(1)} collective-permute-done((bf16[384,128]{1,0:T(8,128)(2,1)S(1)}, bf16[384,128]{1,0:T(8,128)(2,1)S(1)}, u32[]{:S(2)}, u32[]{:S(2)}) %collective-permute-start.7) | collective-permute-done | bytes 98336 | tf_op jit(solution)/shard_map/ppermute | solution.py:479
  45.8 0.0 collective-permute-done.6.refs_3_
  45.8 0.0 collective-permute-done.5.refs_2_
  45.8 0.5 shard_map.57
  46.3 12.5 %all_to_all.5.in_ref = f32[32,8,128]{2,1,0:T(8,128)S(1)} all-to-all(f32[32,8,128]{2,1,0:T(8,128)S(1)} %shard_map.57), channel_id=1, replica_groups=mesh['space'=4,'band'=8] {'space','band'}, dimensions={0} | all-to-all | bytes 262144 | tf_op jit(solution)/shard_map/all_to_all | solution.py:489
  58.8 0.9 %shard_map.58 = (f32[8,64]{1,0:T(8,128)}, f32[8,64]{1,0:T(8,128)}) custom-call(f32[32,8,128]{2,1,0:T(8,128)S(1)} %all_to_all.5.in_ref), custom_call_target="tpu_custom_call" | custom-call | flops 1000000 | bytes 1000000 | tf_op jit(solution)/shard_map/pallas_call | solution.py:373
  (1 shorter events, 0.0 us)
Async XLA Ops:
  0.6 0.9 %copy-start = (f32[12,16,128]{2,1,0:T(8,128)S(1)}, f32[12,16,128]{2,1,0:T(8,128)}, u32[]{:S(2)}) copy-start(f32[12,16,128]{2,1,0:T(8,128)} %param.3) | copy-start | bytes 294916
  3.1 3.2 %collective-permute-start.2 = (bf16[1888,128]{1,0:T(8,128)(2,1)S(1)}, bf16[1888,128]{1,0:T(8,128)(2,1)S(1)}, u32[]{:S(2)}, u32[]{:S(2)}) collective-permute-start(bf16[1888,128]{1,0:T(8,128)(2,1)S(1)} %get-tuple-element.21), channel_id=1, source_target_pairs={{0,8},{8,0},{16,24},{24,16},{1,9},{9,1},{17,25},{25,17},{2,10},{10... | collective-permute-start | bytes 1449992 | tf_op jit(solution)/shard_map/ppermute | solution.py:427
  3.6 9.3 %collective-permute-start = (bf16[1024,128]{1,0:T(8,128)(2,1)S(1)}, bf16[1024,128]{1,0:T(8,128)(2,1)S(1)}, u32[]{:S(2)}, u32[]{:S(2)}) collective-permute-start(bf16[1024,128]{1,0:T(8,128)(2,1)S(1)} %get-tuple-element.19), channel_id=1, source_target_pairs={{0,24},{8,16},{16,8},{24,0},{1,25},{9,17},{17,9},{25,1},{2,26},{10... | collective-permute-start | bytes 786440 | tf_op jit(solution)/shard_map/ppermute | solution.py:426
  6.3 11.3 %collective-permute-start.1 = (bf16[864,128]{1,0:T(8,128)(2,1)S(1)}, bf16[864,128]{1,0:T(8,128)(2,1)S(1)}, u32[]{:S(2)}, u32[]{:S(2)}) collective-permute-start(bf16[864,128]{1,0:T(8,128)(2,1)S(1)} %get-tuple-element.20), channel_id=1, source_target_pairs={{0,24},{8,16},{16,8},{24,0},{1,25},{9,17},{17,9},{25,1},{2,26},{10... | collective-permute-start | bytes 663560 | tf_op jit(solution)/shard_map/ppermute | solution.py:428
  17.6 3.3 %collective-permute-start.3 = (bf16[864,128]{1,0:T(8,128)(2,1)S(1)}, bf16[864,128]{1,0:T(8,128)(2,1)S(1)}, u32[]{:S(2)}, u32[]{:S(2)}) collective-permute-start(bf16[864,128]{1,0:T(8,128)(2,1)S(1)} %shard_map.54), channel_id=1, source_target_pairs={{0,8},{8,0},{16,24},{24,16},{1,9},{9,1},{17,25},{25,17},{2,10},{10... | collective-permute-start | bytes 663560 | tf_op jit(solution)/shard_map/ppermute | solution.py:444
  17.8 2.2 %collective-permute-start.4 = (bf16[768,128]{1,0:T(8,128)(2,1)S(1)}, bf16[768,128]{1,0:T(8,128)(2,1)S(1)}, u32[]{:S(2)}, u32[]{:S(2)}) collective-permute-start(bf16[768,128]{1,0:T(8,128)(2,1)S(1)} %get-tuple-element.28), channel_id=1, source_target_pairs={{0,8},{8,0},{16,24},{24,16},{1,9},{9,1},{17,25},{25,17},{2,10},{10... | collective-permute-start | bytes 589832 | tf_op jit(solution)/shard_map/ppermute | solution.py:442
  23.7 7.5 %collective-permute-start.11 = (bf16[384,128]{1,0:T(8,128)(2,1)S(1)}, bf16[384,128]{1,0:T(8,128)(2,1)S(1)}, u32[]{:S(2)}, u32[]{:S(2)}) collective-permute-start(bf16[384,128]{1,0:T(8,128)(2,1)S(1)} %get-tuple-element.31), channel_id=1, source_target_pairs={{0,1},{1,0},{2,3},{3,2},{4,5},{5,4},{6,7},{7,6},{8,9},{9,8},{10,11... | collective-permute-start | bytes 294920 | tf_op jit(solution)/shard_map/ppermute | solution.py:479
  25.1 8.3 %collective-permute-start.10 = (bf16[384,128]{1,0:T(8,128)(2,1)S(1)}, bf16[384,128]{1,0:T(8,128)(2,1)S(1)}, u32[]{:S(2)}, u32[]{:S(2)}) collective-permute-start(bf16[384,128]{1,0:T(8,128)(2,1)S(1)} %get-tuple-element.32), channel_id=1, source_target_pairs={{0,2},{1,3},{2,0},{3,1},{4,6},{5,7},{6,4},{7,5},{8,10},{9,11},{10,... | collective-permute-start | bytes 294920 | tf_op jit(solution)/shard_map/ppermute | solution.py:479
  26.7 14.9 %collective-permute-start.9 = (bf16[384,128]{1,0:T(8,128)(2,1)S(1)}, bf16[384,128]{1,0:T(8,128)(2,1)S(1)}, u32[]{:S(2)}, u32[]{:S(2)}) collective-permute-start(bf16[384,128]{1,0:T(8,128)(2,1)S(1)} %get-tuple-element.33), channel_id=1, source_target_pairs={{0,4},{1,5},{2,6},{3,7},{4,0},{5,1},{6,2},{7,3},{8,12},{9,13},{10,... | collective-permute-start | bytes 294920 | tf_op jit(solution)/shard_map/ppermute | solution.py:479
  29.3 12.3 %collective-permute-start.8 = (bf16[384,128]{1,0:T(8,128)(2,1)S(1)}, bf16[384,128]{1,0:T(8,128)(2,1)S(1)}, u32[]{:S(2)}, u32[]{:S(2)}) collective-permute-start(bf16[384,128]{1,0:T(8,128)(2,1)S(1)} %get-tuple-element.34), channel_id=1, source_target_pairs={{0,6},{1,7},{2,4},{3,5},{4,2},{5,3},{6,0},{7,1},{8,14},{9,15},{10,... | collective-permute-start | bytes 294920 | tf_op jit(solution)/shard_map/ppermute | solution.py:479
  29.5 16.3 %collective-permute-start.7 = (bf16[384,128]{1,0:T(8,128)(2,1)S(1)}, bf16[384,128]{1,0:T(8,128)(2,1)S(1)}, u32[]{:S(2)}, u32[]{:S(2)}) collective-permute-start(bf16[384,128]{1,0:T(8,128)(2,1)S(1)} %get-tuple-element.35), channel_id=1, source_target_pairs={{0,5},{1,4},{2,7},{3,6},{4,1},{5,0},{6,3},{7,2},{8,13},{9,12},{10,... | collective-permute-start | bytes 294920 | tf_op jit(solution)/shard_map/ppermute | solution.py:479
  31.2 14.6 %collective-permute-start.6 = (bf16[384,128]{1,0:T(8,128)(2,1)S(1)}, bf16[384,128]{1,0:T(8,128)(2,1)S(1)}, u32[]{:S(2)}, u32[]{:S(2)}) collective-permute-start(bf16[384,128]{1,0:T(8,128)(2,1)S(1)} %get-tuple-element.36), channel_id=1, source_target_pairs={{0,7},{1,6},{2,5},{3,4},{4,3},{5,2},{6,1},{7,0},{8,15},{9,14},{10,... | collective-permute-start | bytes 294920 | tf_op jit(solution)/shard_map/ppermute | solution.py:479
  33.5 12.3 %collective-permute-start.5 = (bf16[384,128]{1,0:T(8,128)(2,1)S(1)}, bf16[384,128]{1,0:T(8,128)(2,1)S(1)}, u32[]{:S(2)}, u32[]{:S(2)}) collective-permute-start(bf16[384,128]{1,0:T(8,128)(2,1)S(1)} %get-tuple-element.37), channel_id=1, source_target_pairs={{0,3},{1,2},{2,1},{3,0},{4,7},{5,6},{6,5},{7,4},{8,11},{9,10},{10,... | collective-permute-start | bytes 294920 | tf_op jit(solution)/shard_map/ppermute | solution.py:479

commit v4 on v3

--- a/solution.py
+++ b/solution.py
@@ -203,96 +203,151 @@
 
 def pass_kernel(after_ref, in_ref, out_ref):
     del after_ref
-    out_ref[...] = in_ref[...]
+    out_ref[...] = in_ref[pl.ds(0, out_ref.shape[0]), :]
+
+
+def add_below(nx, below, factors, base, emit):
+    @pl.loop(0, nx)
+    def _(x):
+        low = [below[aligned((j * nx + x) * GROUP, GROUP), :] for j in range(WIDTH)]
+        for i in range(WIDTH):
+            total = base[aligned((i * nx + x) * GROUP, GROUP), :]
+            for j in range(i, WIDTH):
+                total = total + factors[WIDTH + i - j - 1] * low[j]
+            emit(i, x, total)
+
+
+def emit_rows(nx, ref):
+    def emit(i, x, value):
+        ref[aligned((i * nx + x) * GROUP, GROUP), :] = value
+
+    return emit
+
+
+def emit_pairs(nx, narrow, ref):
+    def emit(i, x, value):
+        row = i * nx + x
+        pair = jnp.concatenate([narrow[aligned(row * GROUP, GROUP), :], value], axis=0)
+        ref[aligned(row * 2 * GROUP, 2 * GROUP), :] = pair.astype(BF16)
+
+    return emit
+
+
+TWICE_L_FACTORS = tuple(2.0 * c for c in L_FACTORS)
+
+
+def first_ahead_kernel(
+    planes, nx, own_ref, level_ref, early_ref, first_part_ref, beyond_part_ref, values, y_ref,
+):
+    side = WIDTH * nx * GROUP
+    matrix = circulant(y_ref.shape[1])
+    values[pl.ds(0, side), :] = jnp.zeros((side, values.shape[1]), F32)
+    values[pl.ds(side, 2 * side), :] = own_ref[...]
+    apply_planes(
+        matrix, values, WIDTH, WIDTH, nx, y_ref, level_ref, 0, True,
+        store_planes(nx, (first_part_ref, 0)),
+    )
+    values[pl.ds(side, 2 * side), :] = early_ref[...]
+    apply_planes(
+        matrix, values, WIDTH, WIDTH, nx, y_ref, level_ref, WIDTH, True,
+        store_second(nx, own_ref, WIDTH, (beyond_part_ref, 0)),
+    )
 
 
 def near_kernel(
-    planes, nx, own_ref, level_ref, near_ref, early_ref, first_ref, second_ref, core_ref,
-    field, first, y_ref,
+    nx, near_ref, first_part_ref, beyond_part_ref, near_field_ref, first_ref, beyond_ref, core_ref
 ):
     plane_rows = nx * GROUP
+    place_planes(near_ref, WIDTH, near_field_ref, WIDTH - 1, -1, plane_rows)
+    add_low(near_ref, WIDTH, near_field_ref, WIDTH - 1, plane_rows)
+    add_below(nx, near_field_ref, L_FACTORS, first_part_ref, emit_rows(nx, first_ref))
+    add_below(nx, first_ref, TWICE_L_FACTORS, beyond_part_ref, emit_rows(nx, beyond_ref))
+    core_ref[...] = beyond_ref[...].astype(BF16)
+
+
+def ahead_kernel(
+    planes, nx, own_ref, level_ref, near_ref, near_field_ref, early_ref, first_ref,
+    first_part_ref, second_part_ref, values, levels, y_ref,
+):
+    plane_rows = nx * GROUP
     side = WIDTH * plane_rows
-    place_planes(near_ref, WIDTH, field, WIDTH - 1, -1, plane_rows)
-    add_low(near_ref, WIDTH, field, WIDTH - 1, plane_rows)
-    field[pl.ds(side, 2 * side), :] = own_ref[...]
-    first[pl.ds(side, 2 * side), :] = early_ref[...]
     matrix = circulant(y_ref.shape[1])
-    apply_planes(
-        matrix, field, WIDTH, WIDTH, nx, y_ref, level_ref, 0, True,
-        store_planes(nx, (first_ref, 0), (first, 0)),
-    )
-    apply_planes(
-        matrix, first, WIDTH, WIDTH, nx, y_ref, level_ref, WIDTH, True,
-        store_second(nx, own_ref, WIDTH, (second_ref, 0)),
-    )
-    core_ref[...] = second_ref[...].astype(BF16)
+    values[pl.ds(0, side), :] = jnp.zeros((side, values.shape[1]), F32)
+    values[pl.ds(side, side), :] = near_field_ref[...]
+    values[pl.ds(2 * side, side), :] = own_ref[pl.ds(0, side), :]
+    place_levels(near_ref, side + plane_rows, WIDTH, nx, levels, WIDTH - 1, 0)
+    apply_planes(
+        matrix, values, WIDTH, WIDTH, nx, y_ref, levels, 0, True, store_planes(nx, (first_part_ref, 0))
+    )
+    values[pl.ds(side, side), :] = first_ref[...]
+    values[pl.ds(2 * side, side), :] = early_ref[pl.ds(0, side), :]
+    apply_planes(
+        matrix, values, WIDTH, WIDTH, nx, y_ref, level_ref, 0, True,
+        store_second(nx, own_ref, 0, (second_part_ref, 0)),
+    )
+
+
+def right_ahead_kernel(nx, level_ref, beyond_ref, beside_ref, after_ref, right_part_ref, values, y_ref):
+    del after_ref
+    plane_rows = nx * GROUP
+    side = WIDTH * plane_rows
+    matrix = circulant(y_ref.shape[1])
+    values[pl.ds(0, side), :] = jnp.zeros((side, values.shape[1]), F32)
+    values[pl.ds(side, side), :] = beyond_ref[...]
+    place_planes(beside_ref, WIDTH, values, 3 * WIDTH - 1, -1, plane_rows)
+    apply_planes(
+        matrix, values, WIDTH, WIDTH, nx, y_ref, level_ref, WIDTH, False,
+        store_planes(nx, (right_part_ref, 0)),
+    )
 
 
 def middle_kernel(
-    planes, nx, own_ref, level_ref, near_ref, far_ref, early_ref, beside_first_ref,
-    first_ref, second_ref, field, levels, first, y_ref,
+    nx, far_ref, first_part_ref, second_part_ref, first_low_ref, second_ref, below
 ):
+    place_planes(far_ref, WIDTH, below, WIDTH - 1, -1, nx * GROUP)
+    add_below(nx, below, L_FACTORS, first_part_ref, emit_rows(nx, first_low_ref))
+    add_below(nx, first_low_ref, TWICE_L_FACTORS, second_part_ref, emit_rows(nx, second_ref))
+
+
+def behind_kernel(
+    planes, nx, level_ref, near_ref, near_field_ref, far_ref, first_low_ref, first_ref, second_ref,
+    beyond_ref, right_part_ref, first_part_ref, second_part_ref, left_part_ref, right_ref, values, levels, y_ref,
+):
     plane_rows = nx * GROUP
     side = WIDTH * plane_rows
-    place_planes(far_ref, WIDTH, field, WIDTH - 1, -1, plane_rows)
-    place_planes(near_ref, WIDTH, field, planes - 1, -1, plane_rows)
-    add_low(near_ref, WIDTH, field, planes - 1, plane_rows)
-    field[pl.ds(2 * side, side), :] = own_ref[pl.ds(0, side), :]
-    place_levels(near_ref, side + plane_rows, WIDTH, nx, levels, WIDTH - 1, 0)
-    first[pl.ds(side, side), :] = beside_first_ref[...]
-    first[pl.ds(2 * side, side), :] = early_ref[pl.ds(0, side), :]
+    add_below(nx, second_ref, H_FACTORS, right_part_ref, emit_pairs(nx, beyond_ref, right_ref))
     matrix = circulant(y_ref.shape[1])
-    apply_planes(
-        matrix, field, WIDTH, WIDTH, nx, y_ref, levels, 0, True,
-        store_planes(nx, (first_ref, 0), (first, 0)),
-    )
-    apply_planes(
-        matrix, first, WIDTH, WIDTH, nx, y_ref, level_ref, 0, True,
-        store_second(nx, own_ref, 0, (second_ref, 0)),
-    )
-
-
-def right_kernel(
-    planes, nx, level_ref, beside_ref, second_ref, beyond_ref, pairs_ref, second, y_ref,
-):
-    plane_rows = nx * GROUP
-    side = WIDTH * plane_rows
-    second[pl.ds(0, side), :] = second_ref[...]
-    second[pl.ds(side, side), :] = beyond_ref[...]
-    place_planes(beside_ref, WIDTH, second, 3 * WIDTH - 1, -1, plane_rows)
-    matrix = circulant(y_ref.shape[1])
-    apply_planes(
-        matrix, second, WIDTH, WIDTH, nx, y_ref, level_ref, WIDTH, False, store_pairs(pairs_ref, 0, nx)
-    )
-
-
-def left_kernel(
-    planes, nx, level_ref, near_ref, far_ref, relay_ref, first_low_ref, first_ref, second_ref,
-    beyond_ref, right_ref, out_ref, field, levels, first, second, y_ref, pairs,
-):
-    plane_rows = nx * GROUP
-    side = WIDTH * plane_rows
-    place_planes(relay_ref, WIDTH, field, 0, 1, plane_rows)
-    place_planes(far_ref, WIDTH, field, 2 * WIDTH - 1, -1, plane_rows)
-    place_planes(near_ref, WIDTH, field, 3 * WIDTH - 1, -1, plane_rows)
-    add_low(near_ref, WIDTH, field, 3 * WIDTH - 1, plane_rows)
+    values[pl.ds(0, side), :] = jnp.zeros((side, values.shape[1]), F32)
     place_levels(far_ref, side, WIDTH, nx, levels, WIDTH - 1, WIDTH)
     place_levels(near_ref, side + plane_rows, WIDTH, nx, levels, 2 * WIDTH - 1, 0)
-    first[pl.ds(side, side), :] = first_low_ref[...]
-    first[pl.ds(2 * side, side), :] = first_ref[...]
-    second[pl.ds(side, side), :] = second_ref[...]
-    second[pl.ds(2 * side, side), :] = beyond_ref[...]
-    matrix = circulant(y_ref.shape[1])
-    apply_planes(
-        matrix, field, WIDTH, WIDTH, nx, y_ref, levels, 0, True, store_planes(nx, (first, 0))
-    )
-    apply_planes(
-        matrix, first, WIDTH, WIDTH, nx, y_ref, levels, WIDTH, True,
-        store_second(nx, field, 2 * WIDTH, (second, 0)),
-    )
-    apply_planes(
-        matrix, second, WIDTH, WIDTH, nx, y_ref, level_ref, 0, False, store_pairs(pairs, 0, nx)
-    )
+
+    place_planes(far_ref, WIDTH, values, 2 * WIDTH - 1, -1, plane_rows)
+    values[pl.ds(2 * side, side), :] = near_field_ref[...]
+    apply_planes(
+        matrix, values, WIDTH, WIDTH, nx, y_ref, levels, 0, True, store_planes(nx, (first_part_ref, 0))
+    )
+    values[pl.ds(side, side), :] = first_low_ref[...]
+    values[pl.ds(2 * side, side), :] = first_ref[...]
+    apply_planes(
+        matrix, values, WIDTH, WIDTH, nx, y_ref, levels, WIDTH, True,
+        store_second(nx, near_field_ref, 0, (second_part_ref, 0)),
+    )
+    values[pl.ds(side, side), :] = second_ref[...]
+    values[pl.ds(2 * side, side), :] = beyond_ref[...]
+    apply_planes(
+        matrix, values, WIDTH, WIDTH, nx, y_ref, level_ref, 0, False,
+        store_planes(nx, (left_part_ref, 0)),
+    )
+
+
+def left_kernel(
+    nx, relay_ref, first_part_ref, second_part_ref, left_part_ref, second_ref, right_ref, out_ref,
+    below, lower, pairs,
+):
+    place_planes(relay_ref, WIDTH, below, 0, 1, nx * GROUP)
+    add_below(nx, below, L_FACTORS, first_part_ref, emit_rows(nx, lower))
+    add_below(nx, lower, TWICE_L_FACTORS, second_part_ref, emit_rows(nx, below))
+    add_below(nx, below, H_FACTORS, left_part_ref, emit_pairs(nx, second_ref, pairs))
     band, height, _ = out_ref.shape
     me = lax.axis_index("band")
     for i in range(band // 2):
@@ -314,15 +369,6 @@
             for x in range(nx):
                 value = ref[aligned((i * nx + x) * GROUP, GROUP), :]
                 filtered_ref[pl.ds(target + x, GROUP, stride=rows), :] = value
-
-
-def store_pairs(ref, first, nx):
-    def emit(i, values, center):
-        for x in range(nx):
-            pair = jnp.concatenate([center[x], values[x]], axis=0).astype(BF16)
-            ref[aligned(((first + i) * nx + x) * 2 * GROUP, 2 * GROUP), :] = pair
-
-    return emit
 
 
 def gram_kernel(space, steps, order, *refs):
@@ -433,41 +479,52 @@
         scratch=[f32_planes(2 * planes), f32_planes(2 * planes, nx), f32_planes(planes)],
     )
     wide = planes + WIDTH
-    first, beyond, to_beside = call(
-        functools.partial(near_kernel, planes, nx),
-        (half_slab, half_slab, bf16_rows(half)),
-        own, levels, near, early,
-        scratch=[f32_planes(wide), f32_planes(wide), f32_planes(WIDTH)],
+    part = [f32_planes(wide), f32_planes(planes, nx), f32_planes(WIDTH)]
+    first_part, beyond_part = call(
+        functools.partial(first_ahead_kernel, planes, nx),
+        (half_slab,) * 2,
+        own, levels, early,
+        scratch=[part[0], part[2]],
+    )
+    near_field, first, beyond, to_beside = call(
+        functools.partial(near_kernel, nx),
+        (half_slab,) * 3 + (bf16_rows(half),),
+        near, first_part, beyond_part,
     )
     beside = lax.ppermute(to_beside, "space", other_core)
-    (relay,) = call(pass_kernel, (bf16_rows(half + WIDTH * nx),), first, far, hbm_in=1)
+    first_part, second_part = call(
+        functools.partial(ahead_kernel, planes, nx),
+        (half_slab,) * 2,
+        own, levels, near, near_field, early, first,
+        scratch=part,
+    )
+    (right_part,) = call(
+        functools.partial(right_ahead_kernel, nx),
+        (half_slab,),
+        levels, beyond, beside, first_part,
+        scratch=[part[0], part[2]],
+    )
+    (relay,) = call(pass_kernel, (bf16_rows(half),), right_part, far, hbm_in=1)
     relay = lax.ppermute(relay, "space", other_core)
     first_low, second = call(
-        functools.partial(middle_kernel, planes, nx),
-        (half_slab, half_slab),
-        own, levels, near, far, early, first,
-        scratch=[f32_planes(wide), f32_planes(WIDTH, nx), f32_planes(wide), f32_planes(WIDTH)],
-    )
-    (right,) = call(
-        functools.partial(right_kernel, planes, nx),
-        (bf16_rows(WIDTH * nx * 2 * GROUP),),
-        levels, beside, second, beyond,
-        scratch=[f32_planes(wide), f32_planes(WIDTH)],
+        functools.partial(middle_kernel, nx),
+        (half_slab,) * 2,
+        far, first_part, second_part,
+        scratch=[f32_planes(WIDTH)],
+    )
+    first_part, second_part, left_part, right = call(
+        functools.partial(behind_kernel, planes, nx),
+        (half_slab,) * 3 + (bf16_rows(2 * half),),
+        levels, near, near_field, far, first_low, first, second, beyond, right_part,
+        scratch=part,
     )
     steps = rows // band
     block = (steps * 2 * GROUP, ny)
     (pairs,) = call(
-        functools.partial(left_kernel, planes, nx),
+        functools.partial(left_kernel, nx),
         (struct((band, *block), BF16),),
-        levels, near, far, relay, first_low, first, second, beyond, right,
-        scratch=[
-            f32_planes(wide),
-            f32_planes(planes, nx),
-            f32_planes(wide),
-            f32_planes(wide),
-            f32_planes(WIDTH),
-            pltpu.VMEM((WIDTH * nx * 2 * GROUP, ny), BF16),
-        ],
+        relay, first_part, second_part, left_part, second, right,
+        scratch=[f32_planes(WIDTH), f32_planes(WIDTH), pltpu.VMEM((2 * half, ny), BF16)],
     )
     filtered, written = call(
         functools.partial(write_kernel, planes, nx),

time: 59.8 us -> 57.9 us (0.968)
  waiting for transfers between devices: 17.8 us -> 13.9 us
  Pallas kernels: 12.9 us -> 14.5 us
    ppermute x1, waiting for transfers between devices: 2.85 us -> 0.95 us  [local_kernels(): far = lax.ppermute(to_far, 'space', other_chip)]
    ppermute x1, waiting for transfers between devices: 5.19 us -> 3.39 us  [local_kernels(): near = lax.ppermute(to_near, 'space', other_chip)]
    pallas_call x10 -> x13, Pallas kernels: 12.9 us -> 14.5 us  [call(): pl.pallas_call(kernel, out_shape=outs, in_specs=[anywhere] * hbm_in + [VM...]
  transfers between devices with their start and end apart: 12 -> 12, of which waited for: 4 -> 4; matrix products, arithmetic and copies ran while one was open for 0% -> 0% of each run, Pallas kernels for 12% -> 19%
where the time goes in v4:
time: 57.9 us; the launch traced here: 57.7 us
  starting transfers between devices  15.2 us (26%)
  Pallas kernels  14.5 us (25%)
  waiting for transfers between devices  13.9 us (24%)
  blocking collectives  12.4 us (21%)
  local copies, waits for them, and re-layouts  0.94 us (2%)
  between operations  0.75 us (1%)
    pallas_call x13, Pallas kernels, call(): pl.pallas_call(kernel, out_shape=outs, in_specs=[anywhere] * hbm_in + [VM...  14.5 us
    all_to_all x1, blocking collectives, local_kernels(): pieces = lax.all_to_all(pieces, ('space', 'band'), 0, 0, tiled=True)  12.4 us
    ppermute x7, starting transfers between devices, local_kernels(): lax.ppermute(pairs[k], 'band', [(i, i ^ k) for i in range(band)])  11.2 us
    ppermute x7, waiting for transfers between devices, local_kernels(): lax.ppermute(pairs[k], 'band', [(i, i ^ k) for i in range(band)])  9.53 us
    ppermute x1, waiting for transfers between devices, local_kernels(): near = lax.ppermute(to_near, 'space', other_chip)  3.39 us
    ppermute x1, starting transfers between devices, local_kernels(): near = lax.ppermute(to_near, 'space', other_chip)  2.64 us
  transfers between devices with their start and end apart: 12, of which 4 were waited for; matrix products, arithmetic and copies ran while one was open for 0% of the time, Pallas kernels for 19%

profile of v4, /device:TPU:0, one launch (start us, length us, event | category | flops | bytes accessed | tf_op | source)
XLA Modules:
  0.0 57.7 jit_solution(15309253522004211228)
XLA Ops:
  0.6 0.0 copy-start
  0.6 0.9 %copy-done = f32[12,16,128]{2,1,0:T(8,128)S(1)} copy-done((f32[12,16,128]{2,1,0:T(8,128)S(1)}, f32[12,16,128]{2,1,0:T(8,128)}, u32[]{:S(2)}) %copy-start) | copy-done | bytes 98328
  1.5 1.6 %shard_map.49 = (f32[1536,128]{1,0:T(8,128)S(1)}, f32[192,128]{1,0:T(8,128)S(1)}, bf16[1024,128]{1,0:T(8,128)(2,1)S(1)}, bf16[864,128]{1,0:T(8,128)(2,1)S(1)}, bf16[1888,128]{1,0:T(8,128)(2,1)S(1)}) custom-call(f32[8,12,16,128]{3,2,1,0:T(8,128)} %orbitals_hbm.1, f32[192,128]{1,0:T(8,128)S(1)} %bitcast.18), custom_call_target="tpu_custom_call" | custom-call | flops 1000000 | bytes 1000000 | tf_op jit(solution)/shard_map/pallas_call | solution.py:419
  3.1 0.5 collective-permute-start.2
  3.6 2.6 %collective-permute-start.1 = (bf16[1024,128]{1,0:T(8,128)(2,1)S(1)}, bf16[1024,128]{1,0:T(8,128)(2,1)S(1)}, u32[]{:S(2)}, u32[]{:S(2)}) collective-permute-start(bf16[1024,128]{1,0:T(8,128)(2,1)S(1)} %get-tuple-element.29), channel_id=1, source_target_pairs={{0,24},{8,16},{16,8},{24,0},{1,25},{9,17},{17,9},{25,1},{2,26},{10... | collective-permute-start | bytes 786440 | tf_op jit(solution)/shard_map/ppermute | solution.py:472
  6.3 0.0 collective-permute-start
  6.3 0.0 collective-permute-done.2.core_ref
  6.3 1.4 %shard_map.50.early_ref = f32[1536,128]{1,0:T(8,128)S(1)} custom-call(f32[1536,128]{1,0:T(8,128)S(1)} %get-tuple-element.27.own_ref, f32[192,128]{1,0:T(8,128)S(1)} %get-tuple-element.28.level_ref, bf16[1888,128]{1,0:T(8,128)(2,1)S(1)} %collective-permute-done.2.core_ref), custom_call_target="tpu_custom_call" | custom-call | flops 1000000 | bytes 1000000 | tf_op jit(solution)/shard_map/pallas_call | solution.py:419
  7.7 1.8 %shard_map.51 = (f32[768,128]{1,0:T(8,128)S(1)}, f32[768,128]{1,0:T(8,128)S(1)}) custom-call(f32[1536,128]{1,0:T(8,128)S(1)} %get-tuple-element.27.own_ref, f32[192,128]{1,0:T(8,128)S(1)} %get-tuple-element.28.level_ref, f32[1536,128]{1,0:T(8,128)S(1)} %shard_map.50.early_ref), custom_call_target="tpu_custom_call" | custom-call | flops 1000000 | bytes 1000000 | tf_op jit(solution)/shard_map/pallas_call | solution.py:419
  9.5 3.4 %collective-permute-done.1.near_ref = bf16[1024,128]{1,0:T(8,128)(2,1)S(1)} collective-permute-done((bf16[1024,128]{1,0:T(8,128)(2,1)S(1)}, bf16[1024,128]{1,0:T(8,128)(2,1)S(1)}, u32[]{:S(2)}, u32[]{:S(2)}) %collective-permute-start.1) | collective-permute-done | bytes 262176 | tf_op jit(solution)/shard_map/ppermute | solution.py:472
  12.9 0.4 shard_map.52
  13.4 0.6 %collective-permute-start.3 = (bf16[768,128]{1,0:T(8,128)(2,1)S(1)}, bf16[768,128]{1,0:T(8,128)(2,1)S(1)}, u32[]{:S(2)}, u32[]{:S(2)}) collective-permute-start(bf16[768,128]{1,0:T(8,128)(2,1)S(1)} %get-tuple-element.41), channel_id=1, source_target_pairs={{0,8},{8,0},{16,24},{24,16},{1,9},{9,1},{17,25},{25,17},{2,10},{10... | collective-permute-start | bytes 589832 | tf_op jit(solution)/shard_map/ppermute | solution.py:494
  14.0 1.8 %shard_map.53 = (f32[768,128]{1,0:T(8,128)S(1)}, f32[768,128]{1,0:T(8,128)S(1)}) custom-call(f32[1536,128]{1,0:T(8,128)S(1)} %get-tuple-element.27.own_ref, f32[192,128]{1,0:T(8,128)S(1)} %get-tuple-element.28.level_ref, bf16[1024,128]{1,0:T(8,128)(2,1)S(1)} %collective-permute-done.1.near_ref, f32[768,128]{1,0:T(8,128)S(1)} %get-tuple-element.33.near_field_ref, ...), custom_call_target="tpu_custom_call" | custom-call | flops 1000000 | bytes 1000000 | tf_op jit(solution)/shard_map/pallas_call | solution.py:419
  15.8 0.0 collective-permute-done.3.beside_ref
  15.8 0.8 %shard_map.56.after_ref.right_part_ref = f32[768,128]{1,0:T(8,128)S(1)} custom-call(f32[192,128]{1,0:T(8,128)S(1)} %get-tuple-element.28.level_ref, f32[768,128]{1,0:T(8,128)S(1)} %get-tuple-element.38.beyond_ref, bf16[768,128]{1,0:T(8,128)(2,1)S(1)} %collective-permute-done.3.beside_ref, f32[768,128]{1,0:T(8,128)S(1)} %get-tuple-element.35.first_part_ref.after_ref), custom_call_target="tpu_custom_call" | custom-call | flops 1000000 | bytes 1000000 | tf_op jit(solution)/shard_map/pallas_call | solution.py:419
  16.6 0.9 %collective-permute-done.far_ref.in_ref = bf16[864,128]{1,0:T(8,128)(2,1)S(1)} collective-permute-done((bf16[864,128]{1,0:T(8,128)(2,1)S(1)}, bf16[864,128]{1,0:T(8,128)(2,1)S(1)}, u32[]{:S(2)}, u32[]{:S(2)}) %collective-permute-start) | collective-permute-done | bytes 221216 | tf_op jit(solution)/shard_map/ppermute | solution.py:474
  17.6 0.2 collective-permute-start.4
  17.8 0.4 shard_map.54
  18.2 2.8 %shard_map.58 = (f32[768,128]{1,0:T(8,128)S(1)}, f32[768,128]{1,0:T(8,128)S(1)}, f32[768,128]{1,0:T(8,128)S(1)}, bf16[1536,128]{1,0:T(8,128)(2,1)S(1)}) custom-call(f32[192,128]{1,0:T(8,128)S(1)} %get-tuple-element.28.level_ref, bf16[1024,128]{1,0:T(8,128)(2,1)S(1)} %collective-permute-done.1.near_ref, f32[768,128]{1,0:T(8,128)S(1)} %get-tuple-element.33.near_field_ref, ...), custom_call_target="tpu_custom_call" | custom-call | flops 1000000 | bytes 1000000 | tf_op jit(solution)/shard_map/pallas_call | solution.py:419
  21.0 0.0 collective-permute-done.4.relay_ref
  21.0 0.7 %shard_map.59 = bf16[8,384,128]{2,1,0:T(8,128)(2,1)S(1)} custom-call(bf16[768,128]{1,0:T(8,128)(2,1)S(1)} %collective-permute-done.4.relay_ref, f32[768,128]{1,0:T(8,128)S(1)} %get-tuple-element.43.first_part_ref, f32[768,128]{1,0:T(8,128)S(1)} %get-tuple-element.44.second_part_ref, f32[768,128]{1,0:T(8,128)S(1)} %get-tuple-element.45.left_part_ref, ...), custom_call_target="tpu_custom_call" | custom-call | flops 1000000 | bytes 1000000 | tf_op jit(solution)/shard_map/pallas_call | solution.py:419
  21.8 0.1 slice_bitcast_fusion
  21.9 1.7 %collective-permute-start.11 = (bf16[384,128]{1,0:T(8,128)(2,1)S(1)}, bf16[384,128]{1,0:T(8,128)(2,1)S(1)}, u32[]{:S(2)}, u32[]{:S(2)}) collective-permute-start(bf16[384,128]{1,0:T(8,128)(2,1)S(1)} %get-tuple-element.49), channel_id=1, source_target_pairs={{0,1},{1,0},{2,3},{3,2},{4,5},{5,4},{6,7},{7,6},{8,9},{9,8},{10,11... | collective-permute-start | bytes 294920 | tf_op jit(solution)/shard_map/ppermute | solution.py:536
  23.6 1.6 %collective-permute-start.10 = (bf16[384,128]{1,0:T(8,128)(2,1)S(1)}, bf16[384,128]{1,0:T(8,128)(2,1)S(1)}, u32[]{:S(2)}, u32[]{:S(2)}) collective-permute-start(bf16[384,128]{1,0:T(8,128)(2,1)S(1)} %get-tuple-element.50), channel_id=1, source_target_pairs={{0,2},{1,3},{2,0},{3,1},{4,6},{5,7},{6,4},{7,5},{8,10},{9,11},{10,... | collective-permute-start | bytes 294920 | tf_op jit(solution)/shard_map/ppermute | solution.py:536
  25.1 2.6 %collective-permute-start.9 = (bf16[384,128]{1,0:T(8,128)(2,1)S(1)}, bf16[384,128]{1,0:T(8,128)(2,1)S(1)}, u32[]{:S(2)}, u32[]{:S(2)}) collective-permute-start(bf16[384,128]{1,0:T(8,128)(2,1)S(1)} %get-tuple-element.51), channel_id=1, source_target_pairs={{0,4},{1,5},{2,6},{3,7},{4,0},{5,1},{6,2},{7,3},{8,12},{9,13},{10,... | collective-permute-start | bytes 294920 | tf_op jit(solution)/shard_map/ppermute | solution.py:536
  27.7 0.2 collective-permute-start.8
  28.0 1.7 %collective-permute-start.7 = (bf16[384,128]{1,0:T(8,128)(2,1)S(1)}, bf16[384,128]{1,0:T(8,128)(2,1)S(1)}, u32[]{:S(2)}, u32[]{:S(2)}) collective-permute-start(bf16[384,128]{1,0:T(8,128)(2,1)S(1)} %get-tuple-element.53), channel_id=1, source_target_pairs={{0,5},{1,4},{2,7},{3,6},{4,1},{5,0},{6,3},{7,2},{8,13},{9,12},{10,... | collective-permute-start | bytes 294920 | tf_op jit(solution)/shard_map/ppermute | solution.py:536
  29.6 0.0 collective-permute-done.11.refs_8_
  29.6 2.3 %collective-permute-start.6 = (bf16[384,128]{1,0:T(8,128)(2,1)S(1)}, bf16[384,128]{1,0:T(8,128)(2,1)S(1)}, u32[]{:S(2)}, u32[]{:S(2)}) collective-permute-start(bf16[384,128]{1,0:T(8,128)(2,1)S(1)} %get-tuple-element.54), channel_id=1, source_target_pairs={{0,7},{1,6},{2,5},{3,4},{4,3},{5,2},{6,1},{7,0},{8,15},{9,14},{10,... | collective-permute-start | bytes 294920 | tf_op jit(solution)/shard_map/ppermute | solution.py:536
  31.9 0.0 collective-permute-done.10.refs_7_
  31.9 1.2 %collective-permute-start.5 = (bf16[384,128]{1,0:T(8,128)(2,1)S(1)}, bf16[384,128]{1,0:T(8,128)(2,1)S(1)}, u32[]{:S(2)}, u32[]{:S(2)}) collective-permute-start(bf16[384,128]{1,0:T(8,128)(2,1)S(1)} %get-tuple-element.55), channel_id=1, source_target_pairs={{0,3},{1,2},{2,1},{3,0},{4,7},{5,6},{6,5},{7,4},{8,11},{9,10},{10,... | collective-permute-start | bytes 294920 | tf_op jit(solution)/shard_map/ppermute | solution.py:536
  33.1 1.3 %shard_map.55 = (f32[1536,128]{1,0:T(8,128)}, f32[8,128]{1,0:T(8,128)S(1)}) custom-call(f32[768,128]{1,0:T(8,128)S(1)} %get-tuple-element.37.second_ref, f32[768,128]{1,0:T(8,128)S(1)} %get-tuple-element.38.beyond_ref), custom_call_target="tpu_custom_call" | custom-call | flops 1000000 | bytes 1000000 | tf_op jit(solution)/shard_map/pallas_call | solution.py:419
  34.4 5.4 %collective-permute-done.9.refs_6_ = bf16[384,128]{1,0:T(8,128)(2,1)S(1)} collective-permute-done((bf16[384,128]{1,0:T(8,128)(2,1)S(1)}, bf16[384,128]{1,0:T(8,128)(2,1)S(1)}, u32[]{:S(2)}, u32[]{:S(2)}) %collective-permute-start.9) | collective-permute-done | bytes 98336 | tf_op jit(solution)/shard_map/ppermute | solution.py:536
  39.9 0.0 collective-permute-done.8.refs_5_
  39.9 4.1 %collective-permute-done.7.refs_4_ = bf16[384,128]{1,0:T(8,128)(2,1)S(1)} collective-permute-done((bf16[384,128]{1,0:T(8,128)(2,1)S(1)}, bf16[384,128]{1,0:T(8,128)(2,1)S(1)}, u32[]{:S(2)}, u32[]{:S(2)}) %collective-permute-start.7) | collective-permute-done | bytes 98336 | tf_op jit(solution)/shard_map/ppermute | solution.py:536
  44.0 0.0 collective-permute-done.6.refs_3_
  44.0 0.0 collective-permute-done.5.refs_2_
  44.0 0.5 shard_map.60
  44.5 12.4 %all_to_all.5.in_ref = f32[32,8,128]{2,1,0:T(8,128)S(1)} all-to-all(f32[32,8,128]{2,1,0:T(8,128)S(1)} %shard_map.60), channel_id=1, replica_groups=mesh['space'=4,'band'=8] {'space','band'}, dimensions={0} | all-to-all | bytes 262144 | tf_op jit(solution)/shard_map/all_to_all | solution.py:546
  56.9 0.9 %shard_map.61 = (f32[8,64]{1,0:T(8,128)}, f32[8,64]{1,0:T(8,128)}) custom-call(f32[32,8,128]{2,1,0:T(8,128)S(1)} %all_to_all.5.in_ref), custom_call_target="tpu_custom_call" | custom-call | flops 1000000 | bytes 1000000 | tf_op jit(solution)/shard_map/pallas_call | solution.py:419
  (1 shorter events, 0.0 us)
Async XLA Ops:
  0.6 0.9 %copy-start = (f32[12,16,128]{2,1,0:T(8,128)S(1)}, f32[12,16,128]{2,1,0:T(8,128)}, u32[]{:S(2)}) copy-start(f32[12,16,128]{2,1,0:T(8,128)} %param.3) | copy-start | bytes 294916
  3.1 3.2 %collective-permute-start.2 = (bf16[1888,128]{1,0:T(8,128)(2,1)S(1)}, bf16[1888,128]{1,0:T(8,128)(2,1)S(1)}, u32[]{:S(2)}, u32[]{:S(2)}) collective-permute-start(bf16[1888,128]{1,0:T(8,128)(2,1)S(1)} %get-tuple-element.30), channel_id=1, source_target_pairs={{0,8},{8,0},{16,24},{24,16},{1,9},{9,1},{17,25},{25,17},{2,10},{10... | collective-permute-start | bytes 1449992 | tf_op jit(solution)/shard_map/ppermute | solution.py:473
  3.6 9.3 %collective-permute-start.1 = (bf16[1024,128]{1,0:T(8,128)(2,1)S(1)}, bf16[1024,128]{1,0:T(8,128)(2,1)S(1)}, u32[]{:S(2)}, u32[]{:S(2)}) collective-permute-start(bf16[1024,128]{1,0:T(8,128)(2,1)S(1)} %get-tuple-element.29), channel_id=1, source_target_pairs={{0,24},{8,16},{16,8},{24,0},{1,25},{9,17},{17,9},{25,1},{2,26},{10... | collective-permute-start | bytes 786440 | tf_op jit(solution)/shard_map/ppermute | solution.py:472
  6.3 11.3 %collective-permute-start = (bf16[864,128]{1,0:T(8,128)(2,1)S(1)}, bf16[864,128]{1,0:T(8,128)(2,1)S(1)}, u32[]{:S(2)}, u32[]{:S(2)}) collective-permute-start(bf16[864,128]{1,0:T(8,128)(2,1)S(1)} %get-tuple-element.26), channel_id=1, source_target_pairs={{0,24},{8,16},{16,8},{24,0},{1,25},{9,17},{17,9},{25,1},{2,26},{10... | collective-permute-start | bytes 663560 | tf_op jit(solution)/shard_map/ppermute | solution.py:474
  13.4 2.4 %collective-permute-start.3 = (bf16[768,128]{1,0:T(8,128)(2,1)S(1)}, bf16[768,128]{1,0:T(8,128)(2,1)S(1)}, u32[]{:S(2)}, u32[]{:S(2)}) collective-permute-start(bf16[768,128]{1,0:T(8,128)(2,1)S(1)} %get-tuple-element.41), channel_id=1, source_target_pairs={{0,8},{8,0},{16,24},{24,16},{1,9},{9,1},{17,25},{25,17},{2,10},{10... | collective-permute-start | bytes 589832 | tf_op jit(solution)/shard_map/ppermute | solution.py:494
  17.6 3.4 %collective-permute-start.4 = (bf16[768,128]{1,0:T(8,128)(2,1)S(1)}, bf16[768,128]{1,0:T(8,128)(2,1)S(1)}, u32[]{:S(2)}, u32[]{:S(2)}) collective-permute-start(bf16[768,128]{1,0:T(8,128)(2,1)S(1)} %shard_map.57), channel_id=1, source_target_pairs={{0,8},{8,0},{16,24},{24,16},{1,9},{9,1},{17,25},{25,17},{2,10},{10... | collective-permute-start | bytes 589832 | tf_op jit(solution)/shard_map/ppermute | solution.py:508
  21.9 7.8 %collective-permute-start.11 = (bf16[384,128]{1,0:T(8,128)(2,1)S(1)}, bf16[384,128]{1,0:T(8,128)(2,1)S(1)}, u32[]{:S(2)}, u32[]{:S(2)}) collective-permute-start(bf16[384,128]{1,0:T(8,128)(2,1)S(1)} %get-tuple-element.49), channel_id=1, source_target_pairs={{0,1},{1,0},{2,3},{3,2},{4,5},{5,4},{6,7},{7,6},{8,9},{9,8},{10,11... | collective-permute-start | bytes 294920 | tf_op jit(solution)/shard_map/ppermute | solution.py:536
  23.6 8.3 %collective-permute-start.10 = (bf16[384,128]{1,0:T(8,128)(2,1)S(1)}, bf16[384,128]{1,0:T(8,128)(2,1)S(1)}, u32[]{:S(2)}, u32[]{:S(2)}) collective-permute-start(bf16[384,128]{1,0:T(8,128)(2,1)S(1)} %get-tuple-element.50), channel_id=1, source_target_pairs={{0,2},{1,3},{2,0},{3,1},{4,6},{5,7},{6,4},{7,5},{8,10},{9,11},{10,... | collective-permute-start | bytes 294920 | tf_op jit(solution)/shard_map/ppermute | solution.py:536
  25.1 14.7 %collective-permute-start.9 = (bf16[384,128]{1,0:T(8,128)(2,1)S(1)}, bf16[384,128]{1,0:T(8,128)(2,1)S(1)}, u32[]{:S(2)}, u32[]{:S(2)}) collective-permute-start(bf16[384,128]{1,0:T(8,128)(2,1)S(1)} %get-tuple-element.51), channel_id=1, source_target_pairs={{0,4},{1,5},{2,6},{3,7},{4,0},{5,1},{6,2},{7,3},{8,12},{9,13},{10,... | collective-permute-start | bytes 294920 | tf_op jit(solution)/shard_map/ppermute | solution.py:536
  27.7 12.2 %collective-permute-start.8 = (bf16[384,128]{1,0:T(8,128)(2,1)S(1)}, bf16[384,128]{1,0:T(8,128)(2,1)S(1)}, u32[]{:S(2)}, u32[]{:S(2)}) collective-permute-start(bf16[384,128]{1,0:T(8,128)(2,1)S(1)} %get-tuple-element.52), channel_id=1, source_target_pairs={{0,6},{1,7},{2,4},{3,5},{4,2},{5,3},{6,0},{7,1},{8,14},{9,15},{10,... | collective-permute-start | bytes 294920 | tf_op jit(solution)/shard_map/ppermute | solution.py:536
  28.0 16.0 %collective-permute-start.7 = (bf16[384,128]{1,0:T(8,128)(2,1)S(1)}, bf16[384,128]{1,0:T(8,128)(2,1)S(1)}, u32[]{:S(2)}, u32[]{:S(2)}) collective-permute-start(bf16[384,128]{1,0:T(8,128)(2,1)S(1)} %get-tuple-element.53), channel_id=1, source_target_pairs={{0,5},{1,4},{2,7},{3,6},{4,1},{5,0},{6,3},{7,2},{8,13},{9,12},{10,... | collective-permute-start | bytes 294920 | tf_op jit(solution)/shard_map/ppermute | solution.py:536
  29.6 14.4 %collective-permute-start.6 = (bf16[384,128]{1,0:T(8,128)(2,1)S(1)}, bf16[384,128]{1,0:T(8,128)(2,1)S(1)}, u32[]{:S(2)}, u32[]{:S(2)}) collective-permute-start(bf16[384,128]{1,0:T(8,128)(2,1)S(1)} %get-tuple-element.54), channel_id=1, source_target_pairs={{0,7},{1,6},{2,5},{3,4},{4,3},{5,2},{6,1},{7,0},{8,15},{9,14},{10,... | collective-permute-start | bytes 294920 | tf_op jit(solution)/shard_map/ppermute | solution.py:536
  31.9 12.1 %collective-permute-start.5 = (bf16[384,128]{1,0:T(8,128)(2,1)S(1)}, bf16[384,128]{1,0:T(8,128)(2,1)S(1)}, u32[]{:S(2)}, u32[]{:S(2)}) collective-permute-start(bf16[384,128]{1,0:T(8,128)(2,1)S(1)} %get-tuple-element.55), channel_id=1, source_target_pairs={{0,3},{1,2},{2,1},{3,0},{4,7},{5,6},{6,5},{7,4},{8,11},{9,10},{10,... | collective-permute-start | bytes 294920 | tf_op jit(solution)/shard_map/ppermute | solution.py:536

commit v5 on v4

--- a/solution.py
+++ b/solution.py
@@ -71,28 +71,26 @@
     def _(i):
         where = (start + i) * plane_rows
         center = [load(where + x * GROUP) for x in range(nx)]
-        values = []
-        for x in range(nx):
-            row = levels[pl.ds((level + i) * nx + x, 1), :]
-            row = 0.125 * row + L_CENTER if linear else row + H_CENTER
-            total = jnp.broadcast_to(row, center[x].shape) * center[x]
-            total = total + factors[0] * y_ref[aligned(i * plane_rows + x * GROUP, GROUP), :]
-            for k in range(1, WIDTH + 1):
-                near = load(where + k * plane_rows + x * GROUP) + load(where - k * plane_rows + x * GROUP)
-                near = near + (center[(x + k) % nx] + center[(x - k) % nx])
-                total = total + factors[k - 1] * near
-            values.append(total)
+        values = [None] * nx
+        half = nx // 2
+        for x in range(half):
+            shared = {k: center[(x + k) % nx] + center[(x - k) % nx] for k in range(1, half)}
+            for at in (x, x + half):
+                row = levels[pl.ds((level + i) * nx + at, 1), :]
+                row = 0.125 * row + L_CENTER if linear else row + H_CENTER
+                total = jnp.broadcast_to(row, center[at].shape) * center[at]
+                total = total + factors[0] * y_ref[aligned(i * plane_rows + at * GROUP, GROUP), :]
+                for k in range(1, WIDTH + 1):
+                    up, down = where + k * plane_rows + at * GROUP, where - k * plane_rows + at * GROUP
+                    near = load(up) + load(down) + shared[k if at == x else half - k]
+                    total = total + factors[k - 1] * near
+                values[at] = total
         emit(i, values, center)
 
 
-def prepare_kernel(
-    planes, nx, orbitals_hbm, potential_hbm, own_ref, level_ref, near_ref, far_ref, core_ref,
-    orbitals, potential, semaphores,
-):
-    plane_rows = nx * GROUP
+def own_kernel(planes, nx, orbitals_hbm, own_ref, orbitals, semaphores):
     rows = planes * nx
-    side = WIDTH * plane_rows
-    parts = semaphores.shape[0] - 1
+    parts = semaphores.shape[0]
     each = planes // parts
     odd = lax.rem(lax.axis_index("space"), 2)
 
@@ -100,36 +98,34 @@
         at = pl.ds(i * each, each)
         return pltpu.make_async_copy(orbitals_hbm.at[:, at], orbitals.at[:, at], semaphores.at[i])
 
-    fetch_levels = pltpu.make_async_copy(potential_hbm, potential, semaphores.at[parts])
     for i in range(parts):
         fetch(i).start()
-    fetch_levels.start()
     cells = orbitals.reshape(GROUP * rows, orbitals.shape[-1])
     for i in range(parts):
         fetch(i).wait()
 
         @pl.loop(i * each, (i + 1) * each)
         def _(plane):
-            target = lax.select(odd == 1, planes - 1 - plane, plane) * plane_rows
-            for x in range(0, nx, 2):
-                row = plane * nx + x
-                both = jnp.concatenate(
-                    [cells[pl.ds(row + j, GROUP, stride=rows), :] for j in range(2)], axis=0
-                )
-                at = aligned(target + x * GROUP, 2 * GROUP)
-                own_ref[at, :] = both
-                core_ref[at, :] = both.astype(BF16)
-
-    near_ref[pl.ds(0, side), :] = core_ref[pl.ds(0, side), :]
-    far_ref[pl.ds(0, side), :] = core_ref[pl.ds(side, side), :]
-    size = planes * plane_rows
+            target = lax.select(odd == 1, planes - 1 - plane, plane) * nx
+            for x in range(nx):
+                value = cells[pl.ds(plane * nx + x, GROUP, stride=rows), :]
+                own_ref[aligned((target + x) * GROUP, GROUP), :] = value
+
+
+def messages_kernel(planes, nx, own_ref, potential_ref, level_ref, near_ref, far_ref, core_ref):
+    plane_rows = nx * GROUP
+    side, size = WIDTH * plane_rows, planes * plane_rows
+    odd = lax.rem(lax.axis_index("space"), 2)
+    for start, ref in ((0, near_ref), (side, far_ref)):
+        high = own_ref[pl.ds(start, side), :].astype(BF16)
+        ref[pl.ds(0, side), :] = high
+        core_ref[pl.ds(start, side), :] = high
     for out_ref, plane, at in ((near_ref, 0, side), (core_ref, planes - 1, size)):
         block = own_ref[pl.ds(plane * plane_rows, plane_rows), :]
         out_ref[pl.ds(at, plane_rows), :] = low_part(block).astype(BF16)
-    fetch_levels.wait()
     for plane in range(planes):
         source = lax.select(odd == 1, planes - 1 - plane, plane) * nx
-        block = potential[aligned(source, nx), :]
+        block = potential_ref[aligned(source, nx), :]
         level_ref[pl.ds(plane * nx, nx), :] = block
         core_ref[pl.ds(size + plane_rows + plane * nx, nx), :] = block.astype(BF16)
         if plane < WIDTH:
@@ -411,6 +407,8 @@
         ref[...] = jnp.dot(total, pick, precision=lax.Precision.HIGHEST, preferred_element_type=F32)
 
 
+VMEM_FIRST = 53
+
 ORDER = (1, 2, 4, 6, 5, 7, 3)
 
 
@@ -451,23 +449,22 @@
 
     half = WIDTH * plane_rows
     slab, half_slab = struct((size, ny), F32), struct((half, ny), F32)
-    parts = 4
-    own, levels, to_near, to_far, to_core = call(
-        functools.partial(prepare_kernel, planes, nx),
+    (own,) = call(
+        functools.partial(own_kernel, planes, nx),
+        (slab,),
+        orbitals,
+        hbm_in=1, vmem=VMEM_FIRST,
+        scratch=[pltpu.VMEM(orbitals.shape, F32), pltpu.SemaphoreType.DMA((4,))],
+    )
+    levels, to_near, to_far, to_core = call(
+        functools.partial(messages_kernel, planes, nx),
         (
-            slab,
             struct((rows, ny), F32),
             bf16_rows(half + plane_rows + (WIDTH + NEAR) * nx),
             bf16_rows(half + WIDTH * nx),
             bf16_rows(size + plane_rows + (planes + NEAR) * nx),
         ),
-        orbitals, potential.reshape(rows, ny),
-        hbm_in=2, vmem=52,
-        scratch=[
-            pltpu.VMEM(orbitals.shape, F32),
-            pltpu.VMEM((rows, ny), F32),
-            pltpu.SemaphoreType.DMA((parts + 1,)),
-        ],
+        own, potential.reshape(rows, ny),
     )
     near = lax.ppermute(to_near, "space", other_chip)
     core = lax.ppermute(to_core, "space", other_core)

time: 57.9 us -> 57 us (0.984)
  local copies, waits for them, and re-layouts: 0.94 us -> 0.06 us
    unnamed x2, local copies, waits for them, and re-layouts: 0.89 us -> 0.01 us
    pallas_call x13 -> x14, Pallas kernels: 14.5 us -> 14.5 us  [call(): pl.pallas_call(kernel, out_shape=outs, in_specs=[anywhere] * hbm_in + [VM...]
where the time goes in v5:
time: 57 us; the launch traced here: 56.9 us
  starting transfers between devices  15.2 us (27%)
  Pallas kernels  14.5 us (25%)
  waiting for transfers between devices  13.9 us (24%)
  blocking collectives  12.4 us (22%)
  between operations  0.76 us (1%)
    pallas_call x14, Pallas kernels, call(): pl.pallas_call(kernel, out_shape=outs, in_specs=[anywhere] * hbm_in + [VM...  14.5 us
    all_to_all x1, blocking collectives, local_kernels(): pieces = lax.all_to_all(pieces, ('space', 'band'), 0, 0, tiled=True)  12.4 us
    ppermute x7, starting transfers between devices, local_kernels(): lax.ppermute(pairs[k], 'band', [(i, i ^ k) for i in range(band)])  11.2 us
    ppermute x7, waiting for transfers between devices, local_kernels(): lax.ppermute(pairs[k], 'band', [(i, i ^ k) for i in range(band)])  9.52 us
    ppermute x1, waiting for transfers between devices, local_kernels(): near = lax.ppermute(to_near, 'space', other_chip)  3.4 us
    ppermute x1, starting transfers between devices, local_kernels(): near = lax.ppermute(to_near, 'space', other_chip)  2.64 us
  transfers between devices with their start and end apart: 12, of which 4 were waited for; matrix products, arithmetic and copies ran while one was open for 0% of the time, Pallas kernels for 19%

profile of v5, /device:TPU:0, one launch (start us, length us, event | category | flops | bytes accessed | tf_op | source)
XLA Modules:
  0.0 56.9 jit_solution(5057217645907321015)
XLA Ops:
  0.6 0.0 copy-start
  0.6 1.5 %shard_map.49.own_ref = f32[1536,128]{1,0:T(8,128)S(1)} custom-call(f32[8,12,16,128]{3,2,1,0:T(8,128)} %orbitals_hbm.1), custom_call_target="tpu_custom_call" | custom-call | flops 1000000 | bytes 1000000 | tf_op jit(solution)/shard_map/pallas_call | solution.py:417
  2.2 0.0 copy-done
  2.2 0.1 shard_map.50
  2.3 0.5 collective-permute-start.2
  2.8 2.6 %collective-permute-start.1 = (bf16[1024,128]{1,0:T(8,128)(2,1)S(1)}, bf16[1024,128]{1,0:T(8,128)(2,1)S(1)}, u32[]{:S(2)}, u32[]{:S(2)}) collective-permute-start(bf16[1024,128]{1,0:T(8,128)(2,1)S(1)} %get-tuple-element.27), channel_id=1, source_target_pairs={{0,24},{8,16},{16,8},{24,0},{1,25},{9,17},{17,9},{25,1},{2,26},{10... | collective-permute-start | bytes 786440 | tf_op jit(solution)/shard_map/ppermute | solution.py:469
  5.4 0.0 collective-permute-start
  5.4 0.0 collective-permute-done.2.core_ref
  5.4 1.4 %shard_map.51.early_ref = f32[1536,128]{1,0:T(8,128)S(1)} custom-call(f32[1536,128]{1,0:T(8,128)S(1)} %shard_map.49.own_ref, f32[192,128]{1,0:T(8,128)S(1)} %get-tuple-element.26.level_ref, bf16[1888,128]{1,0:T(8,128)(2,1)S(1)} %collective-permute-done.2.core_ref), custom_call_target="tpu_custom_call" | custom-call | flops 1000000 | bytes 1000000 | tf_op jit(solution)/shard_map/pallas_call | solution.py:417
  6.9 1.8 %shard_map.52 = (f32[768,128]{1,0:T(8,128)S(1)}, f32[768,128]{1,0:T(8,128)S(1)}) custom-call(f32[1536,128]{1,0:T(8,128)S(1)} %shard_map.49.own_ref, f32[192,128]{1,0:T(8,128)S(1)} %get-tuple-element.26.level_ref, f32[1536,128]{1,0:T(8,128)S(1)} %shard_map.51.early_ref), custom_call_target="tpu_custom_call" | custom-call | flops 1000000 | bytes 1000000 | tf_op jit(solution)/shard_map/pallas_call | solution.py:417
  8.7 3.4 %collective-permute-done.1.near_ref = bf16[1024,128]{1,0:T(8,128)(2,1)S(1)} collective-permute-done((bf16[1024,128]{1,0:T(8,128)(2,1)S(1)}, bf16[1024,128]{1,0:T(8,128)(2,1)S(1)}, u32[]{:S(2)}, u32[]{:S(2)}) %collective-permute-start.1) | collective-permute-done | bytes 262176 | tf_op jit(solution)/shard_map/ppermute | solution.py:469
  12.1 0.4 shard_map.53
  12.5 0.6 %collective-permute-start.3 = (bf16[768,128]{1,0:T(8,128)(2,1)S(1)}, bf16[768,128]{1,0:T(8,128)(2,1)S(1)}, u32[]{:S(2)}, u32[]{:S(2)}) collective-permute-start(bf16[768,128]{1,0:T(8,128)(2,1)S(1)} %get-tuple-element.39), channel_id=1, source_target_pairs={{0,8},{8,0},{16,24},{24,16},{1,9},{9,1},{17,25},{25,17},{2,10},{10... | collective-permute-start | bytes 589832 | tf_op jit(solution)/shard_map/ppermute | solution.py:491
  13.2 1.8 %shard_map.54 = (f32[768,128]{1,0:T(8,128)S(1)}, f32[768,128]{1,0:T(8,128)S(1)}) custom-call(f32[1536,128]{1,0:T(8,128)S(1)} %shard_map.49.own_ref, f32[192,128]{1,0:T(8,128)S(1)} %get-tuple-element.26.level_ref, bf16[1024,128]{1,0:T(8,128)(2,1)S(1)} %collective-permute-done.1.near_ref, f32[768,128]{1,0:T(8,128)S(1)} %get-tuple-element.31.near_field_ref, ...), custom_call_target="tpu_custom_call" | custom-call | flops 1000000 | bytes 1000000 | tf_op jit(solution)/shard_map/pallas_call | solution.py:417
  15.0 0.0 collective-permute-done.3.beside_ref
  15.0 0.8 %shard_map.57.after_ref.right_part_ref = f32[768,128]{1,0:T(8,128)S(1)} custom-call(f32[192,128]{1,0:T(8,128)S(1)} %get-tuple-element.26.level_ref, f32[768,128]{1,0:T(8,128)S(1)} %get-tuple-element.36.beyond_ref, bf16[768,128]{1,0:T(8,128)(2,1)S(1)} %collective-permute-done.3.beside_ref, f32[768,128]{1,0:T(8,128)S(1)} %get-tuple-element.33.first_part_ref.after_ref), custom_call_target="tpu_custom_call" | custom-call | flops 1000000 | bytes 1000000 | tf_op jit(solution)/shard_map/pallas_call | solution.py:417
  15.8 0.9 %collective-permute-done.far_ref.in_ref = bf16[864,128]{1,0:T(8,128)(2,1)S(1)} collective-permute-done((bf16[864,128]{1,0:T(8,128)(2,1)S(1)}, bf16[864,128]{1,0:T(8,128)(2,1)S(1)}, u32[]{:S(2)}, u32[]{:S(2)}) %collective-permute-start) | collective-permute-done | bytes 221216 | tf_op jit(solution)/shard_map/ppermute | solution.py:471
  16.8 0.2 collective-permute-start.4
  16.9 0.4 shard_map.55
  17.4 2.8 %shard_map.59 = (f32[768,128]{1,0:T(8,128)S(1)}, f32[768,128]{1,0:T(8,128)S(1)}, f32[768,128]{1,0:T(8,128)S(1)}, bf16[1536,128]{1,0:T(8,128)(2,1)S(1)}) custom-call(f32[192,128]{1,0:T(8,128)S(1)} %get-tuple-element.26.level_ref, bf16[1024,128]{1,0:T(8,128)(2,1)S(1)} %collective-permute-done.1.near_ref, f32[768,128]{1,0:T(8,128)S(1)} %get-tuple-element.31.near_field_ref, ...), custom_call_target="tpu_custom_call" | custom-call | flops 1000000 | bytes 1000000 | tf_op jit(solution)/shard_map/pallas_call | solution.py:417
  20.2 0.0 collective-permute-done.4.relay_ref
  20.2 0.7 %shard_map.60 = bf16[8,384,128]{2,1,0:T(8,128)(2,1)S(1)} custom-call(bf16[768,128]{1,0:T(8,128)(2,1)S(1)} %collective-permute-done.4.relay_ref, f32[768,128]{1,0:T(8,128)S(1)} %get-tuple-element.41.first_part_ref, f32[768,128]{1,0:T(8,128)S(1)} %get-tuple-element.42.second_part_ref, f32[768,128]{1,0:T(8,128)S(1)} %get-tuple-element.43.left_part_ref, ...), custom_call_target="tpu_custom_call" | custom-call | flops 1000000 | bytes 1000000 | tf_op jit(solution)/shard_map/pallas_call | solution.py:417
  20.9 0.1 slice_bitcast_fusion
  21.0 1.7 %collective-permute-start.11 = (bf16[384,128]{1,0:T(8,128)(2,1)S(1)}, bf16[384,128]{1,0:T(8,128)(2,1)S(1)}, u32[]{:S(2)}, u32[]{:S(2)}) collective-permute-start(bf16[384,128]{1,0:T(8,128)(2,1)S(1)} %get-tuple-element.47), channel_id=1, source_target_pairs={{0,1},{1,0},{2,3},{3,2},{4,5},{5,4},{6,7},{7,6},{8,9},{9,8},{10,11... | collective-permute-start | bytes 294920 | tf_op jit(solution)/shard_map/ppermute | solution.py:533
  22.7 1.6 %collective-permute-start.10 = (bf16[384,128]{1,0:T(8,128)(2,1)S(1)}, bf16[384,128]{1,0:T(8,128)(2,1)S(1)}, u32[]{:S(2)}, u32[]{:S(2)}) collective-permute-start(bf16[384,128]{1,0:T(8,128)(2,1)S(1)} %get-tuple-element.48), channel_id=1, source_target_pairs={{0,2},{1,3},{2,0},{3,1},{4,6},{5,7},{6,4},{7,5},{8,10},{9,11},{10,... | collective-permute-start | bytes 294920 | tf_op jit(solution)/shard_map/ppermute | solution.py:533
  24.3 2.6 %collective-permute-start.9 = (bf16[384,128]{1,0:T(8,128)(2,1)S(1)}, bf16[384,128]{1,0:T(8,128)(2,1)S(1)}, u32[]{:S(2)}, u32[]{:S(2)}) collective-permute-start(bf16[384,128]{1,0:T(8,128)(2,1)S(1)} %get-tuple-element.49), channel_id=1, source_target_pairs={{0,4},{1,5},{2,6},{3,7},{4,0},{5,1},{6,2},{7,3},{8,12},{9,13},{10,... | collective-permute-start | bytes 294920 | tf_op jit(solution)/shard_map/ppermute | solution.py:533
  26.9 0.2 collective-permute-start.8
  27.1 1.7 %collective-permute-start.7 = (bf16[384,128]{1,0:T(8,128)(2,1)S(1)}, bf16[384,128]{1,0:T(8,128)(2,1)S(1)}, u32[]{:S(2)}, u32[]{:S(2)}) collective-permute-start(bf16[384,128]{1,0:T(8,128)(2,1)S(1)} %get-tuple-element.51), channel_id=1, source_target_pairs={{0,5},{1,4},{2,7},{3,6},{4,1},{5,0},{6,3},{7,2},{8,13},{9,12},{10,... | collective-permute-start | bytes 294920 | tf_op jit(solution)/shard_map/ppermute | solution.py:533
  28.8 0.0 collective-permute-done.11.refs_8_
  28.8 2.3 %collective-permute-start.6 = (bf16[384,128]{1,0:T(8,128)(2,1)S(1)}, bf16[384,128]{1,0:T(8,128)(2,1)S(1)}, u32[]{:S(2)}, u32[]{:S(2)}) collective-permute-start(bf16[384,128]{1,0:T(8,128)(2,1)S(1)} %get-tuple-element.52), channel_id=1, source_target_pairs={{0,7},{1,6},{2,5},{3,4},{4,3},{5,2},{6,1},{7,0},{8,15},{9,14},{10,... | collective-permute-start | bytes 294920 | tf_op jit(solution)/shard_map/ppermute | solution.py:533
  31.0 0.0 collective-permute-done.10.refs_7_
  31.0 1.2 %collective-permute-start.5 = (bf16[384,128]{1,0:T(8,128)(2,1)S(1)}, bf16[384,128]{1,0:T(8,128)(2,1)S(1)}, u32[]{:S(2)}, u32[]{:S(2)}) collective-permute-start(bf16[384,128]{1,0:T(8,128)(2,1)S(1)} %get-tuple-element.53), channel_id=1, source_target_pairs={{0,3},{1,2},{2,1},{3,0},{4,7},{5,6},{6,5},{7,4},{8,11},{9,10},{10,... | collective-permute-start | bytes 294920 | tf_op jit(solution)/shard_map/ppermute | solution.py:533
  32.2 1.3 %shard_map.56 = (f32[1536,128]{1,0:T(8,128)}, f32[8,128]{1,0:T(8,128)S(1)}) custom-call(f32[768,128]{1,0:T(8,128)S(1)} %get-tuple-element.35.second_ref, f32[768,128]{1,0:T(8,128)S(1)} %get-tuple-element.36.beyond_ref), custom_call_target="tpu_custom_call" | custom-call | flops 1000000 | bytes 1000000 | tf_op jit(solution)/shard_map/pallas_call | solution.py:417
  33.6 5.4 %collective-permute-done.9.refs_6_ = bf16[384,128]{1,0:T(8,128)(2,1)S(1)} collective-permute-done((bf16[384,128]{1,0:T(8,128)(2,1)S(1)}, bf16[384,128]{1,0:T(8,128)(2,1)S(1)}, u32[]{:S(2)}, u32[]{:S(2)}) %collective-permute-start.9) | collective-permute-done | bytes 98336 | tf_op jit(solution)/shard_map/ppermute | solution.py:533
  39.0 0.0 collective-permute-done.8.refs_5_
  39.0 4.1 %collective-permute-done.7.refs_4_ = bf16[384,128]{1,0:T(8,128)(2,1)S(1)} collective-permute-done((bf16[384,128]{1,0:T(8,128)(2,1)S(1)}, bf16[384,128]{1,0:T(8,128)(2,1)S(1)}, u32[]{:S(2)}, u32[]{:S(2)}) %collective-permute-start.7) | collective-permute-done | bytes 98336 | tf_op jit(solution)/shard_map/ppermute | solution.py:533
  43.1 0.0 collective-permute-done.6.refs_3_
  43.1 0.0 collective-permute-done.5.refs_2_
  43.1 0.5 shard_map.61
  43.6 12.4 %all_to_all.5.in_ref = f32[32,8,128]{2,1,0:T(8,128)S(1)} all-to-all(f32[32,8,128]{2,1,0:T(8,128)S(1)} %shard_map.61), channel_id=1, replica_groups=mesh['space'=4,'band'=8] {'space','band'}, dimensions={0} | all-to-all | bytes 262144 | tf_op jit(solution)/shard_map/all_to_all | solution.py:543
  56.0 0.9 %shard_map.62 = (f32[8,64]{1,0:T(8,128)}, f32[8,64]{1,0:T(8,128)}) custom-call(f32[32,8,128]{2,1,0:T(8,128)S(1)} %all_to_all.5.in_ref), custom_call_target="tpu_custom_call" | custom-call | flops 1000000 | bytes 1000000 | tf_op jit(solution)/shard_map/pallas_call | solution.py:417
  (1 shorter events, 0.0 us)
Async XLA Ops:
  0.6 1.5 %copy-start = (f32[12,16,128]{2,1,0:T(8,128)S(1)}, f32[12,16,128]{2,1,0:T(8,128)}, u32[]{:S(2)}) copy-start(f32[12,16,128]{2,1,0:T(8,128)} %param.3) | copy-start | bytes 294916
  2.3 3.2 %collective-permute-start.2 = (bf16[1888,128]{1,0:T(8,128)(2,1)S(1)}, bf16[1888,128]{1,0:T(8,128)(2,1)S(1)}, u32[]{:S(2)}, u32[]{:S(2)}) collective-permute-start(bf16[1888,128]{1,0:T(8,128)(2,1)S(1)} %get-tuple-element.28), channel_id=1, source_target_pairs={{0,8},{8,0},{16,24},{24,16},{1,9},{9,1},{17,25},{25,17},{2,10},{10... | collective-permute-start | bytes 1449992 | tf_op jit(solution)/shard_map/ppermute | solution.py:470
  2.8 9.3 %collective-permute-start.1 = (bf16[1024,128]{1,0:T(8,128)(2,1)S(1)}, bf16[1024,128]{1,0:T(8,128)(2,1)S(1)}, u32[]{:S(2)}, u32[]{:S(2)}) collective-permute-start(bf16[1024,128]{1,0:T(8,128)(2,1)S(1)} %get-tuple-element.27), channel_id=1, source_target_pairs={{0,24},{8,16},{16,8},{24,0},{1,25},{9,17},{17,9},{25,1},{2,26},{10... | collective-permute-start | bytes 786440 | tf_op jit(solution)/shard_map/ppermute | solution.py:469
  5.4 11.3 %collective-permute-start = (bf16[864,128]{1,0:T(8,128)(2,1)S(1)}, bf16[864,128]{1,0:T(8,128)(2,1)S(1)}, u32[]{:S(2)}, u32[]{:S(2)}) collective-permute-start(bf16[864,128]{1,0:T(8,128)(2,1)S(1)} %get-tuple-element.25), channel_id=1, source_target_pairs={{0,24},{8,16},{16,8},{24,0},{1,25},{9,17},{17,9},{25,1},{2,26},{10... | collective-permute-start | bytes 663560 | tf_op jit(solution)/shard_map/ppermute | solution.py:471
  12.5 2.4 %collective-permute-start.3 = (bf16[768,128]{1,0:T(8,128)(2,1)S(1)}, bf16[768,128]{1,0:T(8,128)(2,1)S(1)}, u32[]{:S(2)}, u32[]{:S(2)}) collective-permute-start(bf16[768,128]{1,0:T(8,128)(2,1)S(1)} %get-tuple-element.39), channel_id=1, source_target_pairs={{0,8},{8,0},{16,24},{24,16},{1,9},{9,1},{17,25},{25,17},{2,10},{10... | collective-permute-start | bytes 589832 | tf_op jit(solution)/shard_map/ppermute | solution.py:491
  16.8 3.4 %collective-permute-start.4 = (bf16[768,128]{1,0:T(8,128)(2,1)S(1)}, bf16[768,128]{1,0:T(8,128)(2,1)S(1)}, u32[]{:S(2)}, u32[]{:S(2)}) collective-permute-start(bf16[768,128]{1,0:T(8,128)(2,1)S(1)} %shard_map.58), channel_id=1, source_target_pairs={{0,8},{8,0},{16,24},{24,16},{1,9},{9,1},{17,25},{25,17},{2,10},{10... | collective-permute-start | bytes 589832 | tf_op jit(solution)/shard_map/ppermute | solution.py:505
  21.0 7.8 %collective-permute-start.11 = (bf16[384,128]{1,0:T(8,128)(2,1)S(1)}, bf16[384,128]{1,0:T(8,128)(2,1)S(1)}, u32[]{:S(2)}, u32[]{:S(2)}) collective-permute-start(bf16[384,128]{1,0:T(8,128)(2,1)S(1)} %get-tuple-element.47), channel_id=1, source_target_pairs={{0,1},{1,0},{2,3},{3,2},{4,5},{5,4},{6,7},{7,6},{8,9},{9,8},{10,11... | collective-permute-start | bytes 294920 | tf_op jit(solution)/shard_map/ppermute | solution.py:533
  22.7 8.3 %collective-permute-start.10 = (bf16[384,128]{1,0:T(8,128)(2,1)S(1)}, bf16[384,128]{1,0:T(8,128)(2,1)S(1)}, u32[]{:S(2)}, u32[]{:S(2)}) collective-permute-start(bf16[384,128]{1,0:T(8,128)(2,1)S(1)} %get-tuple-element.48), channel_id=1, source_target_pairs={{0,2},{1,3},{2,0},{3,1},{4,6},{5,7},{6,4},{7,5},{8,10},{9,11},{10,... | collective-permute-start | bytes 294920 | tf_op jit(solution)/shard_map/ppermute | solution.py:533
  24.3 14.7 %collective-permute-start.9 = (bf16[384,128]{1,0:T(8,128)(2,1)S(1)}, bf16[384,128]{1,0:T(8,128)(2,1)S(1)}, u32[]{:S(2)}, u32[]{:S(2)}) collective-permute-start(bf16[384,128]{1,0:T(8,128)(2,1)S(1)} %get-tuple-element.49), channel_id=1, source_target_pairs={{0,4},{1,5},{2,6},{3,7},{4,0},{5,1},{6,2},{7,3},{8,12},{9,13},{10,... | collective-permute-start | bytes 294920 | tf_op jit(solution)/shard_map/ppermute | solution.py:533
  26.9 12.1 %collective-permute-start.8 = (bf16[384,128]{1,0:T(8,128)(2,1)S(1)}, bf16[384,128]{1,0:T(8,128)(2,1)S(1)}, u32[]{:S(2)}, u32[]{:S(2)}) collective-permute-start(bf16[384,128]{1,0:T(8,128)(2,1)S(1)} %get-tuple-element.50), channel_id=1, source_target_pairs={{0,6},{1,7},{2,4},{3,5},{4,2},{5,3},{6,0},{7,1},{8,14},{9,15},{10,... | collective-permute-start | bytes 294920 | tf_op jit(solution)/shard_map/ppermute | solution.py:533
  27.1 16.0 %collective-permute-start.7 = (bf16[384,128]{1,0:T(8,128)(2,1)S(1)}, bf16[384,128]{1,0:T(8,128)(2,1)S(1)}, u32[]{:S(2)}, u32[]{:S(2)}) collective-permute-start(bf16[384,128]{1,0:T(8,128)(2,1)S(1)} %get-tuple-element.51), channel_id=1, source_target_pairs={{0,5},{1,4},{2,7},{3,6},{4,1},{5,0},{6,3},{7,2},{8,13},{9,12},{10,... | collective-permute-start | bytes 294920 | tf_op jit(solution)/shard_map/ppermute | solution.py:533
  28.8 14.3 %collective-permute-start.6 = (bf16[384,128]{1,0:T(8,128)(2,1)S(1)}, bf16[384,128]{1,0:T(8,128)(2,1)S(1)}, u32[]{:S(2)}, u32[]{:S(2)}) collective-permute-start(bf16[384,128]{1,0:T(8,128)(2,1)S(1)} %get-tuple-element.52), channel_id=1, source_target_pairs={{0,7},{1,6},{2,5},{3,4},{4,3},{5,2},{6,1},{7,0},{8,15},{9,14},{10,... | collective-permute-start | bytes 294920 | tf_op jit(solution)/shard_map/ppermute | solution.py:533
  31.0 12.1 %collective-permute-start.5 = (bf16[384,128]{1,0:T(8,128)(2,1)S(1)}, bf16[384,128]{1,0:T(8,128)(2,1)S(1)}, u32[]{:S(2)}, u32[]{:S(2)}) collective-permute-start(bf16[384,128]{1,0:T(8,128)(2,1)S(1)} %get-tuple-element.53), channel_id=1, source_target_pairs={{0,3},{1,2},{2,1},{3,0},{4,7},{5,6},{6,5},{7,4},{8,11},{9,10},{10,... | collective-permute-start | bytes 294920 | tf_op jit(solution)/shard_map/ppermute | solution.py:533

commit v6 on v5

--- a/solution.py
+++ b/solution.py
@@ -337,19 +337,32 @@
 
 
 def left_kernel(
-    nx, relay_ref, first_part_ref, second_part_ref, left_part_ref, second_ref, right_ref, out_ref,
-    below, lower, pairs,
+    nx, relay_ref, first_part_ref, second_part_ref, left_part_ref, second_ref, beyond_ref, right_ref,
+    within_ref, across_ref, below, lower, pairs,
 ):
     place_planes(relay_ref, WIDTH, below, 0, 1, nx * GROUP)
     add_below(nx, below, L_FACTORS, first_part_ref, emit_rows(nx, lower))
     add_below(nx, lower, TWICE_L_FACTORS, second_part_ref, emit_rows(nx, below))
     add_below(nx, below, H_FACTORS, left_part_ref, emit_pairs(nx, second_ref, pairs))
-    band, height, _ = out_ref.shape
     me = lax.axis_index("band")
-    for i in range(band // 2):
-        at = pl.ds(i * height, height)
-        out_ref[i ^ me] = pairs[at, :]
-        out_ref[(band // 2 + i) ^ me] = right_ref[at, :]
+    group = within_ref.shape[0]
+    place, upper = lax.rem(me, group), me >= group
+    plane = nx * 2 * GROUP
+    for j in range(group):
+        k = j ^ place
+        ref, at = (pairs, 2 * j) if 2 * j < WIDTH else (right_ref, 2 * j - WIDTH)
+        within_ref[k, pl.ds(0, 2 * plane), :] = ref[pl.ds(at * plane, 2 * plane), :]
+        last = right_ref[pl.ds((2 * group + j - WIDTH) * plane, plane), :]
+        within_ref[k, pl.ds(2 * plane, plane), :] = last
+        ref, at = (second_ref, 2 * j) if 2 * j < WIDTH else (beyond_ref, 2 * j - WIDTH)
+
+        @pl.when(upper)
+        def _():
+            across_ref[k] = ref[pl.ds(at * nx * GROUP, plane), :].astype(BF16)
+
+        @pl.when(jnp.logical_not(upper))
+        def _():
+            across_ref[k] = last
 
 
 def write_kernel(planes, nx, second_ref, beyond_ref, filtered_ref, done_ref):
@@ -367,30 +380,81 @@
                 filtered_ref[pl.ds(target + x, GROUP, stride=rows), :] = value
 
 
-def gram_kernel(space, steps, order, *refs):
-    after_ref, *blocks, out_ref, held = refs
+def gram_kernel(space, nx, order, *refs):
+    after_ref, own_ref, *blocks, out_ref, held = refs
     del after_ref
-    band = len(blocks)
+    band, rows, ny = held.shape
     width = 2 * GROUP
+    group = band // 2
+    shared, plane = 2 * nx, nx * width
     me = lax.axis_index("band")
+    place, upper = lax.rem(me, group), me >= group
+    base = me - place
+    other = group - base
+    held[base + place] = own_ref[...]
     for k, block in zip(order, blocks):
-        held[k ^ me] = block[...]
-    total = jnp.zeros((band * width, band * width), F32)
-    for step in range(0, steps, 2):
-        block = jnp.concatenate(
-            [held[:, pl.ds((step + i) * width, width), :].reshape(band * width, -1) for i in range(2)],
-            axis=1,
-        )
-        total = total + lax.dot_general(
-            block, block, (((1,), (1,)), ((), ())), preferred_element_type=F32
-        )
+        if k < group:
+            held[base + (k ^ place)] = block[...]
+            continue
+        target = other + ((k - group) ^ place)
+
+        @pl.when(upper)
+        def _():
+            held[target, pl.ds(0, 2 * plane), :] = jnp.zeros((2 * plane, ny), BF16)
+            held[target, pl.ds(2 * plane, plane), :] = block[...]
+
+        @pl.when(jnp.logical_not(upper))
+        def _():
+            for u in range(nx):
+                tile = block[pl.ds(u * width, width), :]
+                held[target, pl.ds(2 * u * width, width), :] = tile
+                held[target, pl.ds((2 * u + 1) * width, width), :] = tile
+            held[target, pl.ds(2 * plane, plane), :] = jnp.zeros((plane, ny), BF16)
+
+    def products(steps):
+        total = jnp.zeros((band * width, band * width), F32)
+        for i in range(0, len(steps), 2):
+            block = jnp.concatenate(
+                [held[:, pl.ds(q * width, width), :].reshape(band * width, ny) for q in steps[i : i + 2]],
+                axis=1,
+            )
+            total = total + lax.dot_general(
+                block, block, (((1,), (1,)), ((), ())), preferred_element_type=F32
+            )
+        return total
+
+    even = products(range(0, shared, 2))
+    odd = products(range(1, shared, 2))
+    total = even + odd + products(range(shared, rows // width))
     lanes = lax.broadcasted_iota(jnp.int32, (GROUP, band * width), 1)
-    for b in range(band):
-        narrow = total[b * width : b * width + GROUP]
-        applied = pltpu.roll(total[b * width + GROUP : (b + 1) * width], GROUP, 1)
-        piece = jnp.where(lanes % width < GROUP, narrow, applied)
+    filtered, lower_lanes = lanes % width < GROUP, lanes < group * width
+    crossed = even + pltpu.roll(odd, band * width - GROUP, 1)
+
+    def rows_of(matrix, b):
+        return matrix[b * width : b * width + GROUP], matrix[b * width + GROUP : (b + 1) * width]
+
+    def both(matrix, b):
+        narrow, applied = rows_of(matrix, b)
+        return jnp.where(filtered, narrow, pltpu.roll(applied, GROUP, 1))
+
+    def store(b, piece):
         for s in range(space):
             out_ref[s * band + b] = piece
+
+    zero = jnp.zeros((GROUP, band * width), F32)
+
+    @pl.when(upper)
+    def _():
+        for b in range(group):
+            store(b, jnp.where(lower_lanes, zero, both(total, b)))
+            store(group + b, jnp.where(lower_lanes, rows_of(total, group + b)[0], both(total, group + b)))
+
+    @pl.when(jnp.logical_not(upper))
+    def _():
+        for b in range(group):
+            store(b, jnp.where(lower_lanes, both(total, b), both(crossed, b)))
+            piece = rows_of(even, group + b)[0] + rows_of(odd, group + b)[1]
+            store(group + b, jnp.where(lower_lanes, piece, zero))
 
 
 def sum_kernel(scale, in_ref, intersection_ref, projected_ref):
@@ -409,10 +473,10 @@
 
 VMEM_FIRST = 53
 
-ORDER = (1, 2, 4, 6, 5, 7, 3)
-
-
-def call(kernel, outs, *args, scratch=(), hbm_in=0, hbm_out=(), vmem=40, flops=1000000):
+ORDER = (4, 6, 5, 7, 2, 3, 1)
+
+
+def call(kernel, outs, *args, scratch=(), hbm_in=0, hbm_out=(), vmem=40, cost=1000000):
     anywhere = pl.BlockSpec(memory_space=pl.ANY)
     return pl.pallas_call(
         kernel,
@@ -421,7 +485,7 @@
         out_specs=tuple(anywhere if i in hbm_out else VMEM for i in range(len(outs))),
         scratch_shapes=list(scratch),
         compiler_params=pltpu.CompilerParams(vmem_limit_bytes=int(vmem * 2**20)),
-        cost_estimate=pl.CostEstimate(flops=flops, bytes_accessed=1000000, transcendentals=0),
+        cost_estimate=pl.CostEstimate(flops=cost, bytes_accessed=cost, transcendentals=0),
     )(*args)
 
 
@@ -515,30 +579,32 @@
         levels, near, near_field, far, first_low, first, second, beyond, right_part,
         scratch=part,
     )
-    steps = rows // band
-    block = (steps * 2 * GROUP, ny)
-    (pairs,) = call(
+    group, plane = band // 2, (nx * 2 * GROUP, ny)
+    within, across = call(
         functools.partial(left_kernel, nx),
-        (struct((band, *block), BF16),),
-        relay, first_part, second_part, left_part, second, right,
+        (struct((group, 3 * plane[0], ny), BF16), struct((group, *plane), BF16)),
+        relay, first_part, second_part, left_part, second, beyond, right,
         scratch=[f32_planes(WIDTH), f32_planes(WIDTH), pltpu.VMEM((2 * half, ny), BF16)],
     )
     filtered, written = call(
         functools.partial(write_kernel, planes, nx),
         (struct((count * rows, ny), F32), struct((GROUP, ny), F32)),
         second, beyond,
-    )
-    order = (0,) + ORDER[::-1]
+        cost=4000000000,
+    )
+    order = ORDER[::-1]
     blocks = [
-        lax.ppermute(pairs[k], "band", [(i, i ^ k) for i in range(band)]) if k else pairs[k]
+        lax.ppermute(
+            within[k] if k < group else across[k - group], "band", [(i, i ^ k) for i in range(band)]
+        )
         for k in order
     ]
     (pieces,) = call(
-        functools.partial(gram_kernel, space, steps, order),
+        functools.partial(gram_kernel, space, nx, order),
         (struct((space * band, GROUP, band * 2 * GROUP), F32),),
-        written, *blocks,
+        written, within[0], *blocks,
         hbm_in=1,
-        scratch=[pltpu.VMEM((band, *block), BF16)],
+        scratch=[pltpu.VMEM((band, 3 * plane[0], ny), BF16)],
     )
     pieces = lax.all_to_all(pieces, ("space", "band"), 0, 0, tiled=True)
     rows_out = struct((count, count * band), F32)
@@ -599,7 +665,7 @@
         and nx == 16
         and ny == 128
         and band * 2 * GROUP == 128
-        and (planes * nx) % (2 * band) == 0
+        and 2 * planes == 3 * band
     )
     return (local_kernels if fits else local_plain)(orbitals, potential)
 

time: 57 us -> 55.2 us (0.968)
  waiting for transfers between devices: 13.9 us -> 11.7 us
  blocking collectives: 12.4 us -> 11.1 us
  starting transfers between devices: 15.2 us -> 16.5 us
    ppermute x7, waiting for transfers between devices: 9.52 us -> 7.33 us  [local_kernels(): lax.ppermute(within[k] if k < group else across[k - group], 'band', [(i,...]
    all_to_all x1, blocking collectives: 12.4 us -> 11.1 us  [local_kernels(): pieces = lax.all_to_all(pieces, ('space', 'band'), 0, 0, tiled=True)]
    ppermute x7, starting transfers between devices: 11.2 us -> 12.4 us  [local_kernels(): lax.ppermute(within[k] if k < group else across[k - group], 'band', [(i,...]
  transfers between devices with their start and end apart: 12 -> 12, of which waited for: 4 -> 5; matrix products, arithmetic and copies ran while one was open for 0% -> 0% of each run, Pallas kernels for 19% -> 20%
where the time goes in v6:
time: 55.2 us; the launch traced here: 55.1 us
  starting transfers between devices  16.5 us (30%)
  Pallas kernels  14.9 us (27%)
  waiting for transfers between devices  11.7 us (21%)
  blocking collectives  11.1 us (20%)
  between operations  0.77 us (1%)
    pallas_call x14, Pallas kernels, call(): pl.pallas_call(kernel, out_shape=outs, in_specs=[anywhere] * hbm_in + [VM...  14.9 us
    ppermute x7, starting transfers between devices, local_kernels(): lax.ppermute(within[k] if k < group else across[k - group], 'band', [(i,...  12.4 us
    all_to_all x1, blocking collectives, local_kernels(): pieces = lax.all_to_all(pieces, ('space', 'band'), 0, 0, tiled=True)  11.1 us
    ppermute x7, waiting for transfers between devices, local_kernels(): lax.ppermute(within[k] if k < group else across[k - group], 'band', [(i,...  7.33 us
    ppermute x1, waiting for transfers between devices, local_kernels(): near = lax.ppermute(to_near, 'space', other_chip)  3.4 us
    ppermute x1, starting transfers between devices, local_kernels(): near = lax.ppermute(to_near, 'space', other_chip)  2.64 us
  transfers between devices with their start and end apart: 12, of which 5 were waited for; matrix products, arithmetic and copies ran while one was open for 0% of the time, Pallas kernels for 20%

profile of v6, /device:TPU:0, one launch (start us, length us, event | category | flops | bytes accessed | tf_op | source)
XLA Modules:
  0.0 55.1 jit_solution(15169870954681004209)
XLA Ops:
  0.6 0.0 copy-start
  0.6 1.5 %shard_map.49.own_ref = f32[1536,128]{1,0:T(8,128)S(1)} custom-call(f32[8,12,16,128]{3,2,1,0:T(8,128)} %orbitals_hbm.1), custom_call_target="tpu_custom_call" | custom-call | flops 1000000 | bytes 1000000 | tf_op jit(solution)/shard_map/pallas_call | solution.py:481
  2.2 0.0 copy-done
  2.2 0.1 shard_map.50
  2.3 0.5 collective-permute-start.2
  2.8 2.6 %collective-permute-start.1 = (bf16[1024,128]{1,0:T(8,128)(2,1)S(1)}, bf16[1024,128]{1,0:T(8,128)(2,1)S(1)}, u32[]{:S(2)}, u32[]{:S(2)}) collective-permute-start(bf16[1024,128]{1,0:T(8,128)(2,1)S(1)} %get-tuple-element.29), channel_id=1, source_target_pairs={{0,24},{8,16},{16,8},{24,0},{1,25},{9,17},{17,9},{25,1},{2,26},{10... | collective-permute-start | bytes 786440 | tf_op jit(solution)/shard_map/ppermute | solution.py:533
  5.4 0.0 collective-permute-start
  5.4 0.0 collective-permute-done.2.core_ref
  5.4 1.4 %shard_map.51.early_ref = f32[1536,128]{1,0:T(8,128)S(1)} custom-call(f32[1536,128]{1,0:T(8,128)S(1)} %shard_map.49.own_ref, f32[192,128]{1,0:T(8,128)S(1)} %get-tuple-element.28.level_ref, bf16[1888,128]{1,0:T(8,128)(2,1)S(1)} %collective-permute-done.2.core_ref), custom_call_target="tpu_custom_call" | custom-call | flops 1000000 | bytes 1000000 | tf_op jit(solution)/shard_map/pallas_call | solution.py:481
  6.9 1.8 %shard_map.52 = (f32[768,128]{1,0:T(8,128)S(1)}, f32[768,128]{1,0:T(8,128)S(1)}) custom-call(f32[1536,128]{1,0:T(8,128)S(1)} %shard_map.49.own_ref, f32[192,128]{1,0:T(8,128)S(1)} %get-tuple-element.28.level_ref, f32[1536,128]{1,0:T(8,128)S(1)} %shard_map.51.early_ref), custom_call_target="tpu_custom_call" | custom-call | flops 1000000 | bytes 1000000 | tf_op jit(solution)/shard_map/pallas_call | solution.py:481
  8.7 3.4 %collective-permute-done.1.near_ref = bf16[1024,128]{1,0:T(8,128)(2,1)S(1)} collective-permute-done((bf16[1024,128]{1,0:T(8,128)(2,1)S(1)}, bf16[1024,128]{1,0:T(8,128)(2,1)S(1)}, u32[]{:S(2)}, u32[]{:S(2)}) %collective-permute-start.1) | collective-permute-done | bytes 262176 | tf_op jit(solution)/shard_map/ppermute | solution.py:533
  12.1 0.4 shard_map.53
  12.5 0.6 %collective-permute-start.3 = (bf16[768,128]{1,0:T(8,128)(2,1)S(1)}, bf16[768,128]{1,0:T(8,128)(2,1)S(1)}, u32[]{:S(2)}, u32[]{:S(2)}) collective-permute-start(bf16[768,128]{1,0:T(8,128)(2,1)S(1)} %get-tuple-element.41), channel_id=1, source_target_pairs={{0,8},{8,0},{16,24},{24,16},{1,9},{9,1},{17,25},{25,17},{2,10},{10... | collective-permute-start | bytes 589832 | tf_op jit(solution)/shard_map/ppermute | solution.py:555
  13.2 1.8 %shard_map.54 = (f32[768,128]{1,0:T(8,128)S(1)}, f32[768,128]{1,0:T(8,128)S(1)}) custom-call(f32[1536,128]{1,0:T(8,128)S(1)} %shard_map.49.own_ref, f32[192,128]{1,0:T(8,128)S(1)} %get-tuple-element.28.level_ref, bf16[1024,128]{1,0:T(8,128)(2,1)S(1)} %collective-permute-done.1.near_ref, f32[768,128]{1,0:T(8,128)S(1)} %get-tuple-element.33.near_field_ref, ...), custom_call_target="tpu_custom_call" | custom-call | flops 1000000 | bytes 1000000 | tf_op jit(solution)/shard_map/pallas_call | solution.py:481
  15.0 0.0 collective-permute-done.3.beside_ref
  15.0 0.8 %shard_map.57.after_ref.right_part_ref = f32[768,128]{1,0:T(8,128)S(1)} custom-call(f32[192,128]{1,0:T(8,128)S(1)} %get-tuple-element.28.level_ref, f32[768,128]{1,0:T(8,128)S(1)} %get-tuple-element.38.beyond_ref, bf16[768,128]{1,0:T(8,128)(2,1)S(1)} %collective-permute-done.3.beside_ref, f32[768,128]{1,0:T(8,128)S(1)} %get-tuple-element.35.first_part_ref.after_ref), custom_call_target="tpu_custom_call" | custom-call | flops 1000000 | bytes 1000000 | tf_op jit(solution)/shard_map/pallas_call | solution.py:481
  15.8 0.9 %collective-permute-done.far_ref.in_ref = bf16[864,128]{1,0:T(8,128)(2,1)S(1)} collective-permute-done((bf16[864,128]{1,0:T(8,128)(2,1)S(1)}, bf16[864,128]{1,0:T(8,128)(2,1)S(1)}, u32[]{:S(2)}, u32[]{:S(2)}) %collective-permute-start) | collective-permute-done | bytes 221216 | tf_op jit(solution)/shard_map/ppermute | solution.py:535
  16.8 0.2 collective-permute-start.4
  16.9 0.4 shard_map.55
  17.4 2.8 %shard_map.59 = (f32[768,128]{1,0:T(8,128)S(1)}, f32[768,128]{1,0:T(8,128)S(1)}, f32[768,128]{1,0:T(8,128)S(1)}, bf16[1536,128]{1,0:T(8,128)(2,1)S(1)}) custom-call(f32[192,128]{1,0:T(8,128)S(1)} %get-tuple-element.28.level_ref, bf16[1024,128]{1,0:T(8,128)(2,1)S(1)} %collective-permute-done.1.near_ref, f32[768,128]{1,0:T(8,128)S(1)} %get-tuple-element.33.near_field_ref, ...), custom_call_target="tpu_custom_call" | custom-call | flops 1000000 | bytes 1000000 | tf_op jit(solution)/shard_map/pallas_call | solution.py:481
  20.2 0.0 collective-permute-done.4.relay_ref
  20.2 0.8 %shard_map.60 = (bf16[4,768,128]{2,1,0:T(8,128)(2,1)S(1)}, bf16[4,256,128]{2,1,0:T(8,128)(2,1)S(1)}) custom-call(bf16[768,128]{1,0:T(8,128)(2,1)S(1)} %collective-permute-done.4.relay_ref, f32[768,128]{1,0:T(8,128)S(1)} %get-tuple-element.43.first_part_ref, f32[768,128]{1,0:T(8,128)S(1)} %get-tuple-element.44.second_part_ref, ...), custom_call_target="tpu_custom_call" | custom-call | flops 1000000 | bytes 1000000 | tf_op jit(solution)/shard_map/pallas_call | solution.py:481
  21.0 2.8 %collective-permute-start.11 = (bf16[256,128]{1,0:T(8,128)(2,1)S(1)}, bf16[256,128]{1,0:T(8,128)(2,1)S(1)}, u32[]{:S(2)}, u32[]{:S(2)}) collective-permute-start(bf16[256,128]{1,0:T(8,128)(2,1)S(1)} %get-tuple-element.55), channel_id=1, source_target_pairs={{0,4},{1,5},{2,6},{3,7},{4,0},{5,1},{6,2},{7,3},{8,12},{9,13},{10,... | collective-permute-start | bytes 196616 | tf_op jit(solution)/shard_map/ppermute | solution.py:597
  23.8 1.4 %collective-permute-start.10 = (bf16[256,128]{1,0:T(8,128)(2,1)S(1)}, bf16[256,128]{1,0:T(8,128)(2,1)S(1)}, u32[]{:S(2)}, u32[]{:S(2)}) collective-permute-start(bf16[256,128]{1,0:T(8,128)(2,1)S(1)} %get-tuple-element.56), channel_id=1, source_target_pairs={{0,6},{1,7},{2,4},{3,5},{4,2},{5,3},{6,0},{7,1},{8,14},{9,15},{10,... | collective-permute-start | bytes 196616 | tf_op jit(solution)/shard_map/ppermute | solution.py:597
  25.2 0.1 slice_bitcast_fusion
  25.3 0.3 collective-permute-start.7
  25.5 2.7 %collective-permute-start.6 = (bf16[768,128]{1,0:T(8,128)(2,1)S(1)}, bf16[768,128]{1,0:T(8,128)(2,1)S(1)}, u32[]{:S(2)}, u32[]{:S(2)}) collective-permute-start(bf16[768,128]{1,0:T(8,128)(2,1)S(1)} %get-tuple-element.52), channel_id=1, source_target_pairs={{0,3},{1,2},{2,1},{3,0},{4,7},{5,6},{6,5},{7,4},{8,11},{9,10},{10,... | collective-permute-start | bytes 589832 | tf_op jit(solution)/shard_map/ppermute | solution.py:597
  28.3 0.5 collective-permute-start.5
  28.8 0.2 collective-permute-done.11.refs_8_
  29.0 2.5 %collective-permute-start.9 = (bf16[256,128]{1,0:T(8,128)(2,1)S(1)}, bf16[256,128]{1,0:T(8,128)(2,1)S(1)}, u32[]{:S(2)}, u32[]{:S(2)}) collective-permute-start(bf16[256,128]{1,0:T(8,128)(2,1)S(1)} %get-tuple-element.57), channel_id=1, source_target_pairs={{0,5},{1,4},{2,7},{3,6},{4,1},{5,0},{6,3},{7,2},{8,13},{9,12},{10,... | collective-permute-start | bytes 196616 | tf_op jit(solution)/shard_map/ppermute | solution.py:597
  31.4 0.0 collective-permute-done.10.refs_7_
  31.4 2.3 %collective-permute-start.8 = (bf16[256,128]{1,0:T(8,128)(2,1)S(1)}, bf16[256,128]{1,0:T(8,128)(2,1)S(1)}, u32[]{:S(2)}, u32[]{:S(2)}) collective-permute-start(bf16[256,128]{1,0:T(8,128)(2,1)S(1)} %get-tuple-element.58), channel_id=1, source_target_pairs={{0,7},{1,6},{2,5},{3,4},{4,3},{5,2},{6,1},{7,0},{8,15},{9,14},{10,... | collective-permute-start | bytes 196616 | tf_op jit(solution)/shard_map/ppermute | solution.py:597
  33.7 1.3 %shard_map.56 = (f32[1536,128]{1,0:T(8,128)}, f32[8,128]{1,0:T(8,128)S(1)}) custom-call(f32[768,128]{1,0:T(8,128)S(1)} %get-tuple-element.37.second_ref, f32[768,128]{1,0:T(8,128)S(1)} %get-tuple-element.38.beyond_ref), custom_call_target="tpu_custom_call" | custom-call | flops 4000000000 | bytes 4000000000 | tf_op jit(solution)/shard_map/pallas_call | solution.py:481
  35.0 2.8 %collective-permute-done.9.refs_6_ = bf16[256,128]{1,0:T(8,128)(2,1)S(1)} collective-permute-done((bf16[256,128]{1,0:T(8,128)(2,1)S(1)}, bf16[256,128]{1,0:T(8,128)(2,1)S(1)}, u32[]{:S(2)}, u32[]{:S(2)}) %collective-permute-start.9) | collective-permute-done | bytes 65568 | tf_op jit(solution)/shard_map/ppermute | solution.py:597
  37.8 4.4 %collective-permute-done.8.refs_5_ = bf16[256,128]{1,0:T(8,128)(2,1)S(1)} collective-permute-done((bf16[256,128]{1,0:T(8,128)(2,1)S(1)}, bf16[256,128]{1,0:T(8,128)(2,1)S(1)}, u32[]{:S(2)}, u32[]{:S(2)}) %collective-permute-start.8) | collective-permute-done | bytes 65568 | tf_op jit(solution)/shard_map/ppermute | solution.py:597
  42.2 0.0 collective-permute-done.7.refs_4_
  42.2 0.0 collective-permute-done.6.refs_3_
  42.2 0.0 collective-permute-done.5.refs_2_
  42.2 0.8 %shard_map.61 = f32[32,8,128]{2,1,0:T(8,128)S(1)} custom-call(f32[8,128]{1,0:T(8,128)S(1)} %get-tuple-element.40.refs_0_, bf16[768,128]{1,0:T(8,128)(2,1)S(1)} %get-tuple-element.54.refs_1_, bf16[768,128]{1,0:T(8,128)(2,1)S(1)} %collective-permute-done.5.refs_2_, bf16[768,128]{1,0:T(8,128)(2,1)S(1)} %collective-permute-done.6.refs_3_, ...), custom_call_target="tpu_custom_call" | custom-call | flops 1000000 | bytes 1000000 | tf_op jit(solution)/shard_map/pallas_call | solution.py:481
  43.1 11.1 %all_to_all.5.in_ref = f32[32,8,128]{2,1,0:T(8,128)S(1)} all-to-all(f32[32,8,128]{2,1,0:T(8,128)S(1)} %shard_map.61), channel_id=1, replica_groups=mesh['space'=4,'band'=8] {'space','band'}, dimensions={0} | all-to-all | bytes 262144 | tf_op jit(solution)/shard_map/all_to_all | solution.py:609
  54.2 0.9 %shard_map.62 = (f32[8,64]{1,0:T(8,128)}, f32[8,64]{1,0:T(8,128)}) custom-call(f32[32,8,128]{2,1,0:T(8,128)S(1)} %all_to_all.5.in_ref), custom_call_target="tpu_custom_call" | custom-call | flops 1000000 | bytes 1000000 | tf_op jit(solution)/shard_map/pallas_call | solution.py:481
  (2 shorter events, 0.0 us)
Async XLA Ops:
  0.6 1.5 %copy-start = (f32[12,16,128]{2,1,0:T(8,128)S(1)}, f32[12,16,128]{2,1,0:T(8,128)}, u32[]{:S(2)}) copy-start(f32[12,16,128]{2,1,0:T(8,128)} %param.3) | copy-start | bytes 294916
  2.3 3.2 %collective-permute-start.2 = (bf16[1888,128]{1,0:T(8,128)(2,1)S(1)}, bf16[1888,128]{1,0:T(8,128)(2,1)S(1)}, u32[]{:S(2)}, u32[]{:S(2)}) collective-permute-start(bf16[1888,128]{1,0:T(8,128)(2,1)S(1)} %get-tuple-element.30), channel_id=1, source_target_pairs={{0,8},{8,0},{16,24},{24,16},{1,9},{9,1},{17,25},{25,17},{2,10},{10... | collective-permute-start | bytes 1449992 | tf_op jit(solution)/shard_map/ppermute | solution.py:534
  2.8 9.3 %collective-permute-start.1 = (bf16[1024,128]{1,0:T(8,128)(2,1)S(1)}, bf16[1024,128]{1,0:T(8,128)(2,1)S(1)}, u32[]{:S(2)}, u32[]{:S(2)}) collective-permute-start(bf16[1024,128]{1,0:T(8,128)(2,1)S(1)} %get-tuple-element.29), channel_id=1, source_target_pairs={{0,24},{8,16},{16,8},{24,0},{1,25},{9,17},{17,9},{25,1},{2,26},{10... | collective-permute-start | bytes 786440 | tf_op jit(solution)/shard_map/ppermute | solution.py:533
  5.4 11.3 %collective-permute-start = (bf16[864,128]{1,0:T(8,128)(2,1)S(1)}, bf16[864,128]{1,0:T(8,128)(2,1)S(1)}, u32[]{:S(2)}, u32[]{:S(2)}) collective-permute-start(bf16[864,128]{1,0:T(8,128)(2,1)S(1)} %get-tuple-element.27), channel_id=1, source_target_pairs={{0,24},{8,16},{16,8},{24,0},{1,25},{9,17},{17,9},{25,1},{2,26},{10... | collective-permute-start | bytes 663560 | tf_op jit(solution)/shard_map/ppermute | solution.py:535
  12.5 2.4 %collective-permute-start.3 = (bf16[768,128]{1,0:T(8,128)(2,1)S(1)}, bf16[768,128]{1,0:T(8,128)(2,1)S(1)}, u32[]{:S(2)}, u32[]{:S(2)}) collective-permute-start(bf16[768,128]{1,0:T(8,128)(2,1)S(1)} %get-tuple-element.41), channel_id=1, source_target_pairs={{0,8},{8,0},{16,24},{24,16},{1,9},{9,1},{17,25},{25,17},{2,10},{10... | collective-permute-start | bytes 589832 | tf_op jit(solution)/shard_map/ppermute | solution.py:555
  16.8 3.4 %collective-permute-start.4 = (bf16[768,128]{1,0:T(8,128)(2,1)S(1)}, bf16[768,128]{1,0:T(8,128)(2,1)S(1)}, u32[]{:S(2)}, u32[]{:S(2)}) collective-permute-start(bf16[768,128]{1,0:T(8,128)(2,1)S(1)} %shard_map.58), channel_id=1, source_target_pairs={{0,8},{8,0},{16,24},{24,16},{1,9},{9,1},{17,25},{25,17},{2,10},{10... | collective-permute-start | bytes 589832 | tf_op jit(solution)/shard_map/ppermute | solution.py:569
  21.0 7.9 %collective-permute-start.11 = (bf16[256,128]{1,0:T(8,128)(2,1)S(1)}, bf16[256,128]{1,0:T(8,128)(2,1)S(1)}, u32[]{:S(2)}, u32[]{:S(2)}) collective-permute-start(bf16[256,128]{1,0:T(8,128)(2,1)S(1)} %get-tuple-element.55), channel_id=1, source_target_pairs={{0,4},{1,5},{2,6},{3,7},{4,0},{5,1},{6,2},{7,3},{8,12},{9,13},{10,... | collective-permute-start | bytes 196616 | tf_op jit(solution)/shard_map/ppermute | solution.py:597
  23.8 7.6 %collective-permute-start.10 = (bf16[256,128]{1,0:T(8,128)(2,1)S(1)}, bf16[256,128]{1,0:T(8,128)(2,1)S(1)}, u32[]{:S(2)}, u32[]{:S(2)}) collective-permute-start(bf16[256,128]{1,0:T(8,128)(2,1)S(1)} %get-tuple-element.56), channel_id=1, source_target_pairs={{0,6},{1,7},{2,4},{3,5},{4,2},{5,3},{6,0},{7,1},{8,14},{9,15},{10,... | collective-permute-start | bytes 196616 | tf_op jit(solution)/shard_map/ppermute | solution.py:597
  25.3 17.0 %collective-permute-start.7 = (bf16[768,128]{1,0:T(8,128)(2,1)S(1)}, bf16[768,128]{1,0:T(8,128)(2,1)S(1)}, u32[]{:S(2)}, u32[]{:S(2)}) collective-permute-start(bf16[768,128]{1,0:T(8,128)(2,1)S(1)} %get-tuple-element.51), channel_id=1, source_target_pairs={{0,2},{1,3},{2,0},{3,1},{4,6},{5,7},{6,4},{7,5},{8,10},{9,11},{10,... | collective-permute-start | bytes 589832 | tf_op jit(solution)/shard_map/ppermute | solution.py:597
  25.5 16.7 %collective-permute-start.6 = (bf16[768,128]{1,0:T(8,128)(2,1)S(1)}, bf16[768,128]{1,0:T(8,128)(2,1)S(1)}, u32[]{:S(2)}, u32[]{:S(2)}) collective-permute-start(bf16[768,128]{1,0:T(8,128)(2,1)S(1)} %get-tuple-element.52), channel_id=1, source_target_pairs={{0,3},{1,2},{2,1},{3,0},{4,7},{5,6},{6,5},{7,4},{8,11},{9,10},{10,... | collective-permute-start | bytes 589832 | tf_op jit(solution)/shard_map/ppermute | solution.py:597
  28.3 14.0 %collective-permute-start.5 = (bf16[768,128]{1,0:T(8,128)(2,1)S(1)}, bf16[768,128]{1,0:T(8,128)(2,1)S(1)}, u32[]{:S(2)}, u32[]{:S(2)}) collective-permute-start(bf16[768,128]{1,0:T(8,128)(2,1)S(1)} %get-tuple-element.53), channel_id=1, source_target_pairs={{0,1},{1,0},{2,3},{3,2},{4,5},{5,4},{6,7},{7,6},{8,9},{9,8},{10,11... | collective-permute-start | bytes 589832 | tf_op jit(solution)/shard_map/ppermute | solution.py:597
  29.0 8.9 %collective-permute-start.9 = (bf16[256,128]{1,0:T(8,128)(2,1)S(1)}, bf16[256,128]{1,0:T(8,128)(2,1)S(1)}, u32[]{:S(2)}, u32[]{:S(2)}) collective-permute-start(bf16[256,128]{1,0:T(8,128)(2,1)S(1)} %get-tuple-element.57), channel_id=1, source_target_pairs={{0,5},{1,4},{2,7},{3,6},{4,1},{5,0},{6,3},{7,2},{8,13},{9,12},{10,... | collective-permute-start | bytes 196616 | tf_op jit(solution)/shard_map/ppermute | solution.py:597
  31.4 10.8 %collective-permute-start.8 = (bf16[256,128]{1,0:T(8,128)(2,1)S(1)}, bf16[256,128]{1,0:T(8,128)(2,1)S(1)}, u32[]{:S(2)}, u32[]{:S(2)}) collective-permute-start(bf16[256,128]{1,0:T(8,128)(2,1)S(1)} %get-tuple-element.58), channel_id=1, source_target_pairs={{0,7},{1,6},{2,5},{3,4},{4,3},{5,2},{6,1},{7,0},{8,15},{9,14},{10,... | collective-permute-start | bytes 196616 | tf_op jit(solution)/shard_map/ppermute | solution.py:597

commit v7 on v6

--- a/solution.py
+++ b/solution.py
@@ -473,7 +473,7 @@
 
 VMEM_FIRST = 53
 
-ORDER = (4, 6, 5, 7, 2, 3, 1)
+ORDER = (6, 4, 7, 5, 2, 3, 1)
 
 
 def call(kernel, outs, *args, scratch=(), hbm_in=0, hbm_out=(), vmem=40, cost=1000000):

time: 55.2 us -> 54.8 us (level)
  blocking collectives: 11.1 us -> 11.8 us
  waiting for transfers between devices: 11.7 us -> 11.1 us
    all_to_all x1, blocking collectives: 11.1 us -> 11.8 us  [local_kernels(): pieces = lax.all_to_all(pieces, ('space', 'band'), 0, 0, tiled=True)]
    ppermute x7, waiting for transfers between devices: 7.33 us -> 6.77 us  [local_kernels(): lax.ppermute(within[k] if k < group else across[k - group], 'band', [(i,...]
  transfers between devices with their start and end apart: 12 -> 12, of which waited for: 5 -> 3; matrix products, arithmetic and copies ran while one was open for 0% -> 0% of each run, Pallas kernels for 20% -> 20%
where the time goes in v7:
time: 54.8 us; the launch traced here: 54.7 us
  starting transfers between devices  16 us (29%)
  Pallas kernels  14.9 us (27%)
  blocking collectives  11.8 us (22%)
  waiting for transfers between devices  11.1 us (20%)
  between operations  0.77 us (1%)
    pallas_call x14, Pallas kernels, call(): pl.pallas_call(kernel, out_shape=outs, in_specs=[anywhere] * hbm_in + [VM...  14.9 us
    ppermute x7, starting transfers between devices, local_kernels(): lax.ppermute(within[k] if k < group else across[k - group], 'band', [(i,...  12 us
    all_to_all x1, blocking collectives, local_kernels(): pieces = lax.all_to_all(pieces, ('space', 'band'), 0, 0, tiled=True)  11.8 us
    ppermute x7, waiting for transfers between devices, local_kernels(): lax.ppermute(within[k] if k < group else across[k - group], 'band', [(i,...  6.77 us
    ppermute x1, waiting for transfers between devices, local_kernels(): near = lax.ppermute(to_near, 'space', other_chip)  3.4 us
    ppermute x1, starting transfers between devices, local_kernels(): near = lax.ppermute(to_near, 'space', other_chip)  2.64 us
  transfers between devices with their start and end apart: 12, of which 3 were waited for; matrix products, arithmetic and copies ran while one was open for 0% of the time, Pallas kernels for 20%

profile of v7, /device:TPU:0, one launch (start us, length us, event | category | flops | bytes accessed | tf_op | source)
XLA Modules:
  0.0 54.7 jit_solution(1989498640645209693)
XLA Ops:
  0.6 0.0 copy-start
  0.6 1.5 %shard_map.49.own_ref = f32[1536,128]{1,0:T(8,128)S(1)} custom-call(f32[8,12,16,128]{3,2,1,0:T(8,128)} %orbitals_hbm.1), custom_call_target="tpu_custom_call" | custom-call | flops 1000000 | bytes 1000000 | tf_op jit(solution)/shard_map/pallas_call | solution.py:481
  2.2 0.0 copy-done
  2.2 0.1 shard_map.50
  2.3 0.5 collective-permute-start.2
  2.8 2.6 %collective-permute-start.1 = (bf16[1024,128]{1,0:T(8,128)(2,1)S(1)}, bf16[1024,128]{1,0:T(8,128)(2,1)S(1)}, u32[]{:S(2)}, u32[]{:S(2)}) collective-permute-start(bf16[1024,128]{1,0:T(8,128)(2,1)S(1)} %get-tuple-element.29), channel_id=1, source_target_pairs={{0,24},{8,16},{16,8},{24,0},{1,25},{9,17},{17,9},{25,1},{2,26},{10... | collective-permute-start | bytes 786440 | tf_op jit(solution)/shard_map/ppermute | solution.py:533
  5.4 0.0 collective-permute-start
  5.4 0.0 collective-permute-done.2.core_ref
  5.4 1.4 %shard_map.51.early_ref = f32[1536,128]{1,0:T(8,128)S(1)} custom-call(f32[1536,128]{1,0:T(8,128)S(1)} %shard_map.49.own_ref, f32[192,128]{1,0:T(8,128)S(1)} %get-tuple-element.28.level_ref, bf16[1888,128]{1,0:T(8,128)(2,1)S(1)} %collective-permute-done.2.core_ref), custom_call_target="tpu_custom_call" | custom-call | flops 1000000 | bytes 1000000 | tf_op jit(solution)/shard_map/pallas_call | solution.py:481
  6.9 1.8 %shard_map.52 = (f32[768,128]{1,0:T(8,128)S(1)}, f32[768,128]{1,0:T(8,128)S(1)}) custom-call(f32[1536,128]{1,0:T(8,128)S(1)} %shard_map.49.own_ref, f32[192,128]{1,0:T(8,128)S(1)} %get-tuple-element.28.level_ref, f32[1536,128]{1,0:T(8,128)S(1)} %shard_map.51.early_ref), custom_call_target="tpu_custom_call" | custom-call | flops 1000000 | bytes 1000000 | tf_op jit(solution)/shard_map/pallas_call | solution.py:481
  8.7 3.4 %collective-permute-done.1.near_ref = bf16[1024,128]{1,0:T(8,128)(2,1)S(1)} collective-permute-done((bf16[1024,128]{1,0:T(8,128)(2,1)S(1)}, bf16[1024,128]{1,0:T(8,128)(2,1)S(1)}, u32[]{:S(2)}, u32[]{:S(2)}) %collective-permute-start.1) | collective-permute-done | bytes 262176 | tf_op jit(solution)/shard_map/ppermute | solution.py:533
  12.1 0.4 shard_map.53
  12.5 0.6 %collective-permute-start.3 = (bf16[768,128]{1,0:T(8,128)(2,1)S(1)}, bf16[768,128]{1,0:T(8,128)(2,1)S(1)}, u32[]{:S(2)}, u32[]{:S(2)}) collective-permute-start(bf16[768,128]{1,0:T(8,128)(2,1)S(1)} %get-tuple-element.41), channel_id=1, source_target_pairs={{0,8},{8,0},{16,24},{24,16},{1,9},{9,1},{17,25},{25,17},{2,10},{10... | collective-permute-start | bytes 589832 | tf_op jit(solution)/shard_map/ppermute | solution.py:555
  13.2 1.8 %shard_map.54 = (f32[768,128]{1,0:T(8,128)S(1)}, f32[768,128]{1,0:T(8,128)S(1)}) custom-call(f32[1536,128]{1,0:T(8,128)S(1)} %shard_map.49.own_ref, f32[192,128]{1,0:T(8,128)S(1)} %get-tuple-element.28.level_ref, bf16[1024,128]{1,0:T(8,128)(2,1)S(1)} %collective-permute-done.1.near_ref, f32[768,128]{1,0:T(8,128)S(1)} %get-tuple-element.33.near_field_ref, ...), custom_call_target="tpu_custom_call" | custom-call | flops 1000000 | bytes 1000000 | tf_op jit(solution)/shard_map/pallas_call | solution.py:481
  15.0 0.0 collective-permute-done.3.beside_ref
  15.0 0.8 %shard_map.57.after_ref.right_part_ref = f32[768,128]{1,0:T(8,128)S(1)} custom-call(f32[192,128]{1,0:T(8,128)S(1)} %get-tuple-element.28.level_ref, f32[768,128]{1,0:T(8,128)S(1)} %get-tuple-element.38.beyond_ref, bf16[768,128]{1,0:T(8,128)(2,1)S(1)} %collective-permute-done.3.beside_ref, f32[768,128]{1,0:T(8,128)S(1)} %get-tuple-element.35.first_part_ref.after_ref), custom_call_target="tpu_custom_call" | custom-call | flops 1000000 | bytes 1000000 | tf_op jit(solution)/shard_map/pallas_call | solution.py:481
  15.8 0.9 %collective-permute-done.far_ref.in_ref = bf16[864,128]{1,0:T(8,128)(2,1)S(1)} collective-permute-done((bf16[864,128]{1,0:T(8,128)(2,1)S(1)}, bf16[864,128]{1,0:T(8,128)(2,1)S(1)}, u32[]{:S(2)}, u32[]{:S(2)}) %collective-permute-start) | collective-permute-done | bytes 221216 | tf_op jit(solution)/shard_map/ppermute | solution.py:535
  16.8 0.2 collective-permute-start.4
  16.9 0.4 shard_map.55
  17.4 2.8 %shard_map.59 = (f32[768,128]{1,0:T(8,128)S(1)}, f32[768,128]{1,0:T(8,128)S(1)}, f32[768,128]{1,0:T(8,128)S(1)}, bf16[1536,128]{1,0:T(8,128)(2,1)S(1)}) custom-call(f32[192,128]{1,0:T(8,128)S(1)} %get-tuple-element.28.level_ref, bf16[1024,128]{1,0:T(8,128)(2,1)S(1)} %collective-permute-done.1.near_ref, f32[768,128]{1,0:T(8,128)S(1)} %get-tuple-element.33.near_field_ref, ...), custom_call_target="tpu_custom_call" | custom-call | flops 1000000 | bytes 1000000 | tf_op jit(solution)/shard_map/pallas_call | solution.py:481
  20.2 0.0 collective-permute-done.4.relay_ref
  20.2 0.8 %shard_map.60 = (bf16[4,768,128]{2,1,0:T(8,128)(2,1)S(1)}, bf16[4,256,128]{2,1,0:T(8,128)(2,1)S(1)}) custom-call(bf16[768,128]{1,0:T(8,128)(2,1)S(1)} %collective-permute-done.4.relay_ref, f32[768,128]{1,0:T(8,128)S(1)} %get-tuple-element.43.first_part_ref, f32[768,128]{1,0:T(8,128)S(1)} %get-tuple-element.44.second_part_ref, ...), custom_call_target="tpu_custom_call" | custom-call | flops 1000000 | bytes 1000000 | tf_op jit(solution)/shard_map/pallas_call | solution.py:481
  21.0 3.8 %collective-permute-start.11 = (bf16[256,128]{1,0:T(8,128)(2,1)S(1)}, bf16[256,128]{1,0:T(8,128)(2,1)S(1)}, u32[]{:S(2)}, u32[]{:S(2)}) collective-permute-start(bf16[256,128]{1,0:T(8,128)(2,1)S(1)} %get-tuple-element.55), channel_id=1, source_target_pairs={{0,6},{1,7},{2,4},{3,5},{4,2},{5,3},{6,0},{7,1},{8,14},{9,15},{10,... | collective-permute-start | bytes 196616 | tf_op jit(solution)/shard_map/ppermute | solution.py:597
  24.9 0.0 collective-permute-start.10
  24.9 0.1 slice_bitcast_fusion
  24.9 0.7 %collective-permute-start.7 = (bf16[768,128]{1,0:T(8,128)(2,1)S(1)}, bf16[768,128]{1,0:T(8,128)(2,1)S(1)}, u32[]{:S(2)}, u32[]{:S(2)}) collective-permute-start(bf16[768,128]{1,0:T(8,128)(2,1)S(1)} %get-tuple-element.51), channel_id=1, source_target_pairs={{0,2},{1,3},{2,0},{3,1},{4,6},{5,7},{6,4},{7,5},{8,10},{9,11},{10,... | collective-permute-start | bytes 589832 | tf_op jit(solution)/shard_map/ppermute | solution.py:597
  25.6 2.3 %collective-permute-start.6 = (bf16[768,128]{1,0:T(8,128)(2,1)S(1)}, bf16[768,128]{1,0:T(8,128)(2,1)S(1)}, u32[]{:S(2)}, u32[]{:S(2)}) collective-permute-start(bf16[768,128]{1,0:T(8,128)(2,1)S(1)} %get-tuple-element.52), channel_id=1, source_target_pairs={{0,3},{1,2},{2,1},{3,0},{4,7},{5,6},{6,5},{7,4},{8,11},{9,10},{10,... | collective-permute-start | bytes 589832 | tf_op jit(solution)/shard_map/ppermute | solution.py:597
  27.9 0.5 collective-permute-start.5
  28.5 0.0 collective-permute-done.11.refs_8_
  28.5 4.1 %collective-permute-start.9 = (bf16[256,128]{1,0:T(8,128)(2,1)S(1)}, bf16[256,128]{1,0:T(8,128)(2,1)S(1)}, u32[]{:S(2)}, u32[]{:S(2)}) collective-permute-start(bf16[256,128]{1,0:T(8,128)(2,1)S(1)} %get-tuple-element.57), channel_id=1, source_target_pairs={{0,7},{1,6},{2,5},{3,4},{4,3},{5,2},{6,1},{7,0},{8,15},{9,14},{10,... | collective-permute-start | bytes 196616 | tf_op jit(solution)/shard_map/ppermute | solution.py:597
  32.6 0.0 collective-permute-done.10.refs_7_
  32.6 0.5 collective-permute-start.8
  33.1 1.3 %shard_map.56 = (f32[1536,128]{1,0:T(8,128)}, f32[8,128]{1,0:T(8,128)S(1)}) custom-call(f32[768,128]{1,0:T(8,128)S(1)} %get-tuple-element.37.second_ref, f32[768,128]{1,0:T(8,128)S(1)} %get-tuple-element.38.beyond_ref), custom_call_target="tpu_custom_call" | custom-call | flops 4000000000 | bytes 4000000000 | tf_op jit(solution)/shard_map/pallas_call | solution.py:481
  34.4 6.8 %collective-permute-done.9.refs_6_ = bf16[256,128]{1,0:T(8,128)(2,1)S(1)} collective-permute-done((bf16[256,128]{1,0:T(8,128)(2,1)S(1)}, bf16[256,128]{1,0:T(8,128)(2,1)S(1)}, u32[]{:S(2)}, u32[]{:S(2)}) %collective-permute-start.9) | collective-permute-done | bytes 65568 | tf_op jit(solution)/shard_map/ppermute | solution.py:597
  41.2 0.0 collective-permute-done.8.refs_5_
  41.2 0.0 collective-permute-done.7.refs_4_
  41.2 0.0 collective-permute-done.6.refs_3_
  41.2 0.0 collective-permute-done.5.refs_2_
  41.2 0.8 %shard_map.61 = f32[32,8,128]{2,1,0:T(8,128)S(1)} custom-call(f32[8,128]{1,0:T(8,128)S(1)} %get-tuple-element.40.refs_0_, bf16[768,128]{1,0:T(8,128)(2,1)S(1)} %get-tuple-element.54.refs_1_, bf16[768,128]{1,0:T(8,128)(2,1)S(1)} %collective-permute-done.5.refs_2_, bf16[768,128]{1,0:T(8,128)(2,1)S(1)} %collective-permute-done.6.refs_3_, ...), custom_call_target="tpu_custom_call" | custom-call | flops 1000000 | bytes 1000000 | tf_op jit(solution)/shard_map/pallas_call | solution.py:481
  42.0 11.8 %all_to_all.5.in_ref = f32[32,8,128]{2,1,0:T(8,128)S(1)} all-to-all(f32[32,8,128]{2,1,0:T(8,128)S(1)} %shard_map.61), channel_id=1, replica_groups=mesh['space'=4,'band'=8] {'space','band'}, dimensions={0} | all-to-all | bytes 262144 | tf_op jit(solution)/shard_map/all_to_all | solution.py:609
  53.8 0.9 %shard_map.62 = (f32[8,64]{1,0:T(8,128)}, f32[8,64]{1,0:T(8,128)}) custom-call(f32[32,8,128]{2,1,0:T(8,128)S(1)} %all_to_all.5.in_ref), custom_call_target="tpu_custom_call" | custom-call | flops 1000000 | bytes 1000000 | tf_op jit(solution)/shard_map/pallas_call | solution.py:481
  (2 shorter events, 0.0 us)
Async XLA Ops:
  0.6 1.5 %copy-start = (f32[12,16,128]{2,1,0:T(8,128)S(1)}, f32[12,16,128]{2,1,0:T(8,128)}, u32[]{:S(2)}) copy-start(f32[12,16,128]{2,1,0:T(8,128)} %param.3) | copy-start | bytes 294916
  2.3 3.2 %collective-permute-start.2 = (bf16[1888,128]{1,0:T(8,128)(2,1)S(1)}, bf16[1888,128]{1,0:T(8,128)(2,1)S(1)}, u32[]{:S(2)}, u32[]{:S(2)}) collective-permute-start(bf16[1888,128]{1,0:T(8,128)(2,1)S(1)} %get-tuple-element.30), channel_id=1, source_target_pairs={{0,8},{8,0},{16,24},{24,16},{1,9},{9,1},{17,25},{25,17},{2,10},{10... | collective-permute-start | bytes 1449992 | tf_op jit(solution)/shard_map/ppermute | solution.py:534
  2.8 9.3 %collective-permute-start.1 = (bf16[1024,128]{1,0:T(8,128)(2,1)S(1)}, bf16[1024,128]{1,0:T(8,128)(2,1)S(1)}, u32[]{:S(2)}, u32[]{:S(2)}) collective-permute-start(bf16[1024,128]{1,0:T(8,128)(2,1)S(1)} %get-tuple-element.29), channel_id=1, source_target_pairs={{0,24},{8,16},{16,8},{24,0},{1,25},{9,17},{17,9},{25,1},{2,26},{10... | collective-permute-start | bytes 786440 | tf_op jit(solution)/shard_map/ppermute | solution.py:533
  5.4 11.3 %collective-permute-start = (bf16[864,128]{1,0:T(8,128)(2,1)S(1)}, bf16[864,128]{1,0:T(8,128)(2,1)S(1)}, u32[]{:S(2)}, u32[]{:S(2)}) collective-permute-start(bf16[864,128]{1,0:T(8,128)(2,1)S(1)} %get-tuple-element.27), channel_id=1, source_target_pairs={{0,24},{8,16},{16,8},{24,0},{1,25},{9,17},{17,9},{25,1},{2,26},{10... | collective-permute-start | bytes 663560 | tf_op jit(solution)/shard_map/ppermute | solution.py:535
  12.5 2.4 %collective-permute-start.3 = (bf16[768,128]{1,0:T(8,128)(2,1)S(1)}, bf16[768,128]{1,0:T(8,128)(2,1)S(1)}, u32[]{:S(2)}, u32[]{:S(2)}) collective-permute-start(bf16[768,128]{1,0:T(8,128)(2,1)S(1)} %get-tuple-element.41), channel_id=1, source_target_pairs={{0,8},{8,0},{16,24},{24,16},{1,9},{9,1},{17,25},{25,17},{2,10},{10... | collective-permute-start | bytes 589832 | tf_op jit(solution)/shard_map/ppermute | solution.py:555
  16.8 3.4 %collective-permute-start.4 = (bf16[768,128]{1,0:T(8,128)(2,1)S(1)}, bf16[768,128]{1,0:T(8,128)(2,1)S(1)}, u32[]{:S(2)}, u32[]{:S(2)}) collective-permute-start(bf16[768,128]{1,0:T(8,128)(2,1)S(1)} %shard_map.58), channel_id=1, source_target_pairs={{0,8},{8,0},{16,24},{24,16},{1,9},{9,1},{17,25},{25,17},{2,10},{10... | collective-permute-start | bytes 589832 | tf_op jit(solution)/shard_map/ppermute | solution.py:569
  21.0 7.4 %collective-permute-start.11 = (bf16[256,128]{1,0:T(8,128)(2,1)S(1)}, bf16[256,128]{1,0:T(8,128)(2,1)S(1)}, u32[]{:S(2)}, u32[]{:S(2)}) collective-permute-start(bf16[256,128]{1,0:T(8,128)(2,1)S(1)} %get-tuple-element.55), channel_id=1, source_target_pairs={{0,6},{1,7},{2,4},{3,5},{4,2},{5,3},{6,0},{7,1},{8,14},{9,15},{10,... | collective-permute-start | bytes 196616 | tf_op jit(solution)/shard_map/ppermute | solution.py:597
  24.9 7.7 %collective-permute-start.10 = (bf16[256,128]{1,0:T(8,128)(2,1)S(1)}, bf16[256,128]{1,0:T(8,128)(2,1)S(1)}, u32[]{:S(2)}, u32[]{:S(2)}) collective-permute-start(bf16[256,128]{1,0:T(8,128)(2,1)S(1)} %get-tuple-element.56), channel_id=1, source_target_pairs={{0,4},{1,5},{2,6},{3,7},{4,0},{5,1},{6,2},{7,3},{8,12},{9,13},{10,... | collective-permute-start | bytes 196616 | tf_op jit(solution)/shard_map/ppermute | solution.py:597
  24.9 16.3 %collective-permute-start.7 = (bf16[768,128]{1,0:T(8,128)(2,1)S(1)}, bf16[768,128]{1,0:T(8,128)(2,1)S(1)}, u32[]{:S(2)}, u32[]{:S(2)}) collective-permute-start(bf16[768,128]{1,0:T(8,128)(2,1)S(1)} %get-tuple-element.51), channel_id=1, source_target_pairs={{0,2},{1,3},{2,0},{3,1},{4,6},{5,7},{6,4},{7,5},{8,10},{9,11},{10,... | collective-permute-start | bytes 589832 | tf_op jit(solution)/shard_map/ppermute | solution.py:597
  25.6 15.6 %collective-permute-start.6 = (bf16[768,128]{1,0:T(8,128)(2,1)S(1)}, bf16[768,128]{1,0:T(8,128)(2,1)S(1)}, u32[]{:S(2)}, u32[]{:S(2)}) collective-permute-start(bf16[768,128]{1,0:T(8,128)(2,1)S(1)} %get-tuple-element.52), channel_id=1, source_target_pairs={{0,3},{1,2},{2,1},{3,0},{4,7},{5,6},{6,5},{7,4},{8,11},{9,10},{10,... | collective-permute-start | bytes 589832 | tf_op jit(solution)/shard_map/ppermute | solution.py:597
  27.9 13.3 %collective-permute-start.5 = (bf16[768,128]{1,0:T(8,128)(2,1)S(1)}, bf16[768,128]{1,0:T(8,128)(2,1)S(1)}, u32[]{:S(2)}, u32[]{:S(2)}) collective-permute-start(bf16[768,128]{1,0:T(8,128)(2,1)S(1)} %get-tuple-element.53), channel_id=1, source_target_pairs={{0,1},{1,0},{2,3},{3,2},{4,5},{5,4},{6,7},{7,6},{8,9},{9,8},{10,11... | collective-permute-start | bytes 589832 | tf_op jit(solution)/shard_map/ppermute | solution.py:597
  28.5 12.7 %collective-permute-start.9 = (bf16[256,128]{1,0:T(8,128)(2,1)S(1)}, bf16[256,128]{1,0:T(8,128)(2,1)S(1)}, u32[]{:S(2)}, u32[]{:S(2)}) collective-permute-start(bf16[256,128]{1,0:T(8,128)(2,1)S(1)} %get-tuple-element.57), channel_id=1, source_target_pairs={{0,7},{1,6},{2,5},{3,4},{4,3},{5,2},{6,1},{7,0},{8,15},{9,14},{10,... | collective-permute-start | bytes 196616 | tf_op jit(solution)/shard_map/ppermute | solution.py:597
  32.6 8.6 %collective-permute-start.8 = (bf16[256,128]{1,0:T(8,128)(2,1)S(1)}, bf16[256,128]{1,0:T(8,128)(2,1)S(1)}, u32[]{:S(2)}, u32[]{:S(2)}) collective-permute-start(bf16[256,128]{1,0:T(8,128)(2,1)S(1)} %get-tuple-element.58), channel_id=1, source_target_pairs={{0,5},{1,4},{2,7},{3,6},{4,1},{5,0},{6,3},{7,2},{8,13},{9,12},{10,... | collective-permute-start | bytes 196616 | tf_op jit(solution)/shard_map/ppermute | solution.py:597

commit v8 on v7

--- a/solution.py
+++ b/solution.py
@@ -463,12 +463,14 @@
         total = total + in_ref[i]
     total = total * scale
     lanes, columns = total.shape[1], intersection_ref.shape[1]
-    source = lax.broadcasted_iota(jnp.int32, (lanes, columns), 0)
-    target = lax.broadcasted_iota(jnp.int32, (lanes, columns), 1)
-    place = (target // GROUP) * (2 * GROUP) + target % GROUP
-    for offset, ref in ((0, intersection_ref), (GROUP, projected_ref)):
-        pick = jnp.where(source == place + offset, 1.0, 0.0).astype(F32)
-        ref[...] = jnp.dot(total, pick, precision=lax.Precision.HIGHEST, preferred_element_type=F32)
+    source = lax.broadcasted_iota(jnp.int32, (lanes, 2 * columns), 0)
+    target = lax.broadcasted_iota(jnp.int32, (lanes, 2 * columns), 1)
+    column = target % columns
+    place = (column // GROUP) * (2 * GROUP) + column % GROUP + (target // columns) * GROUP
+    pick = jnp.where(source == place, 1.0, 0.0).astype(F32)
+    both = jnp.dot(total, pick, precision=lax.Precision.HIGHEST, preferred_element_type=F32)
+    intersection_ref[...] = both[:, :columns]
+    projected_ref[...] = both[:, columns:]
 
 
 VMEM_FIRST = 53

time: 54.8 us -> 54.8 us (level)
  no operation moved by 1% of the time
where the time goes in v8:
time: 54.8 us; the launch traced here: 54.7 us
  starting transfers between devices  16 us (29%)
  Pallas kernels  14.9 us (27%)
  blocking collectives  11.8 us (22%)
  waiting for transfers between devices  11.1 us (20%)
  between operations  0.77 us (1%)
    pallas_call x14, Pallas kernels, call(): pl.pallas_call(kernel, out_shape=outs, in_specs=[anywhere] * hbm_in + [VM...  14.9 us
    ppermute x7, starting transfers between devices, local_kernels(): lax.ppermute(within[k] if k < group else across[k - group], 'band', [(i,...  12 us
    all_to_all x1, blocking collectives, local_kernels(): pieces = lax.all_to_all(pieces, ('space', 'band'), 0, 0, tiled=True)  11.8 us
    ppermute x7, waiting for transfers between devices, local_kernels(): lax.ppermute(within[k] if k < group else across[k - group], 'band', [(i,...  6.77 us
    ppermute x1, waiting for transfers between devices, local_kernels(): near = lax.ppermute(to_near, 'space', other_chip)  3.4 us
    ppermute x1, starting transfers between devices, local_kernels(): near = lax.ppermute(to_near, 'space', other_chip)  2.64 us
  transfers between devices with their start and end apart: 12, of which 3 were waited for; matrix products, arithmetic and copies ran while one was open for 0% of the time, Pallas kernels for 20%

profile of v8, /device:TPU:0, one launch (start us, length us, event | category | flops | bytes accessed | tf_op | source)
XLA Modules:
  0.0 54.7 jit_solution(6424486052964870302)
XLA Ops:
  0.6 0.0 copy-start
  0.6 1.5 %shard_map.49.own_ref = f32[1536,128]{1,0:T(8,128)S(1)} custom-call(f32[8,12,16,128]{3,2,1,0:T(8,128)} %orbitals_hbm.1), custom_call_target="tpu_custom_call" | custom-call | flops 1000000 | bytes 1000000 | tf_op jit(solution)/shard_map/pallas_call | solution.py:483
  2.2 0.0 copy-done
  2.2 0.1 shard_map.50
  2.3 0.5 collective-permute-start.2
  2.8 2.6 %collective-permute-start.1 = (bf16[1024,128]{1,0:T(8,128)(2,1)S(1)}, bf16[1024,128]{1,0:T(8,128)(2,1)S(1)}, u32[]{:S(2)}, u32[]{:S(2)}) collective-permute-start(bf16[1024,128]{1,0:T(8,128)(2,1)S(1)} %get-tuple-element.29), channel_id=1, source_target_pairs={{0,24},{8,16},{16,8},{24,0},{1,25},{9,17},{17,9},{25,1},{2,26},{10... | collective-permute-start | bytes 786440 | tf_op jit(solution)/shard_map/ppermute | solution.py:535
  5.4 0.0 collective-permute-start
  5.4 0.0 collective-permute-done.2.core_ref
  5.4 1.4 %shard_map.51.early_ref = f32[1536,128]{1,0:T(8,128)S(1)} custom-call(f32[1536,128]{1,0:T(8,128)S(1)} %shard_map.49.own_ref, f32[192,128]{1,0:T(8,128)S(1)} %get-tuple-element.28.level_ref, bf16[1888,128]{1,0:T(8,128)(2,1)S(1)} %collective-permute-done.2.core_ref), custom_call_target="tpu_custom_call" | custom-call | flops 1000000 | bytes 1000000 | tf_op jit(solution)/shard_map/pallas_call | solution.py:483
  6.9 1.8 %shard_map.52 = (f32[768,128]{1,0:T(8,128)S(1)}, f32[768,128]{1,0:T(8,128)S(1)}) custom-call(f32[1536,128]{1,0:T(8,128)S(1)} %shard_map.49.own_ref, f32[192,128]{1,0:T(8,128)S(1)} %get-tuple-element.28.level_ref, f32[1536,128]{1,0:T(8,128)S(1)} %shard_map.51.early_ref), custom_call_target="tpu_custom_call" | custom-call | flops 1000000 | bytes 1000000 | tf_op jit(solution)/shard_map/pallas_call | solution.py:483
  8.7 3.4 %collective-permute-done.1.near_ref = bf16[1024,128]{1,0:T(8,128)(2,1)S(1)} collective-permute-done((bf16[1024,128]{1,0:T(8,128)(2,1)S(1)}, bf16[1024,128]{1,0:T(8,128)(2,1)S(1)}, u32[]{:S(2)}, u32[]{:S(2)}) %collective-permute-start.1) | collective-permute-done | bytes 262176 | tf_op jit(solution)/shard_map/ppermute | solution.py:535
  12.1 0.4 shard_map.53
  12.5 0.6 %collective-permute-start.3 = (bf16[768,128]{1,0:T(8,128)(2,1)S(1)}, bf16[768,128]{1,0:T(8,128)(2,1)S(1)}, u32[]{:S(2)}, u32[]{:S(2)}) collective-permute-start(bf16[768,128]{1,0:T(8,128)(2,1)S(1)} %get-tuple-element.41), channel_id=1, source_target_pairs={{0,8},{8,0},{16,24},{24,16},{1,9},{9,1},{17,25},{25,17},{2,10},{10... | collective-permute-start | bytes 589832 | tf_op jit(solution)/shard_map/ppermute | solution.py:557
  13.2 1.8 %shard_map.54 = (f32[768,128]{1,0:T(8,128)S(1)}, f32[768,128]{1,0:T(8,128)S(1)}) custom-call(f32[1536,128]{1,0:T(8,128)S(1)} %shard_map.49.own_ref, f32[192,128]{1,0:T(8,128)S(1)} %get-tuple-element.28.level_ref, bf16[1024,128]{1,0:T(8,128)(2,1)S(1)} %collective-permute-done.1.near_ref, f32[768,128]{1,0:T(8,128)S(1)} %get-tuple-element.33.near_field_ref, ...), custom_call_target="tpu_custom_call" | custom-call | flops 1000000 | bytes 1000000 | tf_op jit(solution)/shard_map/pallas_call | solution.py:483
  15.0 0.0 collective-permute-done.3.beside_ref
  15.0 0.8 %shard_map.57.after_ref.right_part_ref = f32[768,128]{1,0:T(8,128)S(1)} custom-call(f32[192,128]{1,0:T(8,128)S(1)} %get-tuple-element.28.level_ref, f32[768,128]{1,0:T(8,128)S(1)} %get-tuple-element.38.beyond_ref, bf16[768,128]{1,0:T(8,128)(2,1)S(1)} %collective-permute-done.3.beside_ref, f32[768,128]{1,0:T(8,128)S(1)} %get-tuple-element.35.first_part_ref.after_ref), custom_call_target="tpu_custom_call" | custom-call | flops 1000000 | bytes 1000000 | tf_op jit(solution)/shard_map/pallas_call | solution.py:483
  15.8 0.9 %collective-permute-done.far_ref.in_ref = bf16[864,128]{1,0:T(8,128)(2,1)S(1)} collective-permute-done((bf16[864,128]{1,0:T(8,128)(2,1)S(1)}, bf16[864,128]{1,0:T(8,128)(2,1)S(1)}, u32[]{:S(2)}, u32[]{:S(2)}) %collective-permute-start) | collective-permute-done | bytes 221216 | tf_op jit(solution)/shard_map/ppermute | solution.py:537
  16.8 0.2 collective-permute-start.4
  16.9 0.4 shard_map.55
  17.4 2.8 %shard_map.59 = (f32[768,128]{1,0:T(8,128)S(1)}, f32[768,128]{1,0:T(8,128)S(1)}, f32[768,128]{1,0:T(8,128)S(1)}, bf16[1536,128]{1,0:T(8,128)(2,1)S(1)}) custom-call(f32[192,128]{1,0:T(8,128)S(1)} %get-tuple-element.28.level_ref, bf16[1024,128]{1,0:T(8,128)(2,1)S(1)} %collective-permute-done.1.near_ref, f32[768,128]{1,0:T(8,128)S(1)} %get-tuple-element.33.near_field_ref, ...), custom_call_target="tpu_custom_call" | custom-call | flops 1000000 | bytes 1000000 | tf_op jit(solution)/shard_map/pallas_call | solution.py:483
  20.2 0.0 collective-permute-done.4.relay_ref
  20.2 0.8 %shard_map.60 = (bf16[4,768,128]{2,1,0:T(8,128)(2,1)S(1)}, bf16[4,256,128]{2,1,0:T(8,128)(2,1)S(1)}) custom-call(bf16[768,128]{1,0:T(8,128)(2,1)S(1)} %collective-permute-done.4.relay_ref, f32[768,128]{1,0:T(8,128)S(1)} %get-tuple-element.43.first_part_ref, f32[768,128]{1,0:T(8,128)S(1)} %get-tuple-element.44.second_part_ref, ...), custom_call_target="tpu_custom_call" | custom-call | flops 1000000 | bytes 1000000 | tf_op jit(solution)/shard_map/pallas_call | solution.py:483
  21.0 3.8 %collective-permute-start.11 = (bf16[256,128]{1,0:T(8,128)(2,1)S(1)}, bf16[256,128]{1,0:T(8,128)(2,1)S(1)}, u32[]{:S(2)}, u32[]{:S(2)}) collective-permute-start(bf16[256,128]{1,0:T(8,128)(2,1)S(1)} %get-tuple-element.55), channel_id=1, source_target_pairs={{0,6},{1,7},{2,4},{3,5},{4,2},{5,3},{6,0},{7,1},{8,14},{9,15},{10,... | collective-permute-start | bytes 196616 | tf_op jit(solution)/shard_map/ppermute | solution.py:599
  24.9 0.0 collective-permute-start.10
  24.9 0.1 slice_bitcast_fusion
  24.9 0.7 %collective-permute-start.7 = (bf16[768,128]{1,0:T(8,128)(2,1)S(1)}, bf16[768,128]{1,0:T(8,128)(2,1)S(1)}, u32[]{:S(2)}, u32[]{:S(2)}) collective-permute-start(bf16[768,128]{1,0:T(8,128)(2,1)S(1)} %get-tuple-element.51), channel_id=1, source_target_pairs={{0,2},{1,3},{2,0},{3,1},{4,6},{5,7},{6,4},{7,5},{8,10},{9,11},{10,... | collective-permute-start | bytes 589832 | tf_op jit(solution)/shard_map/ppermute | solution.py:599
  25.6 2.3 %collective-permute-start.6 = (bf16[768,128]{1,0:T(8,128)(2,1)S(1)}, bf16[768,128]{1,0:T(8,128)(2,1)S(1)}, u32[]{:S(2)}, u32[]{:S(2)}) collective-permute-start(bf16[768,128]{1,0:T(8,128)(2,1)S(1)} %get-tuple-element.52), channel_id=1, source_target_pairs={{0,3},{1,2},{2,1},{3,0},{4,7},{5,6},{6,5},{7,4},{8,11},{9,10},{10,... | collective-permute-start | bytes 589832 | tf_op jit(solution)/shard_map/ppermute | solution.py:599
  27.9 0.5 collective-permute-start.5
  28.5 0.0 collective-permute-done.11.refs_8_
  28.5 4.1 %collective-permute-start.9 = (bf16[256,128]{1,0:T(8,128)(2,1)S(1)}, bf16[256,128]{1,0:T(8,128)(2,1)S(1)}, u32[]{:S(2)}, u32[]{:S(2)}) collective-permute-start(bf16[256,128]{1,0:T(8,128)(2,1)S(1)} %get-tuple-element.57), channel_id=1, source_target_pairs={{0,7},{1,6},{2,5},{3,4},{4,3},{5,2},{6,1},{7,0},{8,15},{9,14},{10,... | collective-permute-start | bytes 196616 | tf_op jit(solution)/shard_map/ppermute | solution.py:599
  32.6 0.0 collective-permute-done.10.refs_7_
  32.6 0.5 collective-permute-start.8
  33.1 1.3 %shard_map.56 = (f32[1536,128]{1,0:T(8,128)}, f32[8,128]{1,0:T(8,128)S(1)}) custom-call(f32[768,128]{1,0:T(8,128)S(1)} %get-tuple-element.37.second_ref, f32[768,128]{1,0:T(8,128)S(1)} %get-tuple-element.38.beyond_ref), custom_call_target="tpu_custom_call" | custom-call | flops 4000000000 | bytes 4000000000 | tf_op jit(solution)/shard_map/pallas_call | solution.py:483
  34.4 6.8 %collective-permute-done.9.refs_6_ = bf16[256,128]{1,0:T(8,128)(2,1)S(1)} collective-permute-done((bf16[256,128]{1,0:T(8,128)(2,1)S(1)}, bf16[256,128]{1,0:T(8,128)(2,1)S(1)}, u32[]{:S(2)}, u32[]{:S(2)}) %collective-permute-start.9) | collective-permute-done | bytes 65568 | tf_op jit(solution)/shard_map/ppermute | solution.py:599
  41.2 0.0 collective-permute-done.8.refs_5_
  41.2 0.0 collective-permute-done.7.refs_4_
  41.2 0.0 collective-permute-done.6.refs_3_
  41.2 0.0 collective-permute-done.5.refs_2_
  41.2 0.8 %shard_map.61 = f32[32,8,128]{2,1,0:T(8,128)S(1)} custom-call(f32[8,128]{1,0:T(8,128)S(1)} %get-tuple-element.40.refs_0_, bf16[768,128]{1,0:T(8,128)(2,1)S(1)} %get-tuple-element.54.refs_1_, bf16[768,128]{1,0:T(8,128)(2,1)S(1)} %collective-permute-done.5.refs_2_, bf16[768,128]{1,0:T(8,128)(2,1)S(1)} %collective-permute-done.6.refs_3_, ...), custom_call_target="tpu_custom_call" | custom-call | flops 1000000 | bytes 1000000 | tf_op jit(solution)/shard_map/pallas_call | solution.py:483
  42.0 11.8 %all_to_all.5.in_ref = f32[32,8,128]{2,1,0:T(8,128)S(1)} all-to-all(f32[32,8,128]{2,1,0:T(8,128)S(1)} %shard_map.61), channel_id=1, replica_groups=mesh['space'=4,'band'=8] {'space','band'}, dimensions={0} | all-to-all | bytes 262144 | tf_op jit(solution)/shard_map/all_to_all | solution.py:611
  53.8 0.9 %shard_map.62 = (f32[8,64]{1,0:T(8,128)}, f32[8,64]{1,0:T(8,128)}) custom-call(f32[32,8,128]{2,1,0:T(8,128)S(1)} %all_to_all.5.in_ref), custom_call_target="tpu_custom_call" | custom-call | flops 1000000 | bytes 1000000 | tf_op jit(solution)/shard_map/pallas_call | solution.py:483
  (2 shorter events, 0.0 us)
Async XLA Ops:
  0.6 1.5 %copy-start = (f32[12,16,128]{2,1,0:T(8,128)S(1)}, f32[12,16,128]{2,1,0:T(8,128)}, u32[]{:S(2)}) copy-start(f32[12,16,128]{2,1,0:T(8,128)} %param.3) | copy-start | bytes 294916
  2.3 3.2 %collective-permute-start.2 = (bf16[1888,128]{1,0:T(8,128)(2,1)S(1)}, bf16[1888,128]{1,0:T(8,128)(2,1)S(1)}, u32[]{:S(2)}, u32[]{:S(2)}) collective-permute-start(bf16[1888,128]{1,0:T(8,128)(2,1)S(1)} %get-tuple-element.30), channel_id=1, source_target_pairs={{0,8},{8,0},{16,24},{24,16},{1,9},{9,1},{17,25},{25,17},{2,10},{10... | collective-permute-start | bytes 1449992 | tf_op jit(solution)/shard_map/ppermute | solution.py:536
  2.8 9.3 %collective-permute-start.1 = (bf16[1024,128]{1,0:T(8,128)(2,1)S(1)}, bf16[1024,128]{1,0:T(8,128)(2,1)S(1)}, u32[]{:S(2)}, u32[]{:S(2)}) collective-permute-start(bf16[1024,128]{1,0:T(8,128)(2,1)S(1)} %get-tuple-element.29), channel_id=1, source_target_pairs={{0,24},{8,16},{16,8},{24,0},{1,25},{9,17},{17,9},{25,1},{2,26},{10... | collective-permute-start | bytes 786440 | tf_op jit(solution)/shard_map/ppermute | solution.py:535
  5.4 11.3 %collective-permute-start = (bf16[864,128]{1,0:T(8,128)(2,1)S(1)}, bf16[864,128]{1,0:T(8,128)(2,1)S(1)}, u32[]{:S(2)}, u32[]{:S(2)}) collective-permute-start(bf16[864,128]{1,0:T(8,128)(2,1)S(1)} %get-tuple-element.27), channel_id=1, source_target_pairs={{0,24},{8,16},{16,8},{24,0},{1,25},{9,17},{17,9},{25,1},{2,26},{10... | collective-permute-start | bytes 663560 | tf_op jit(solution)/shard_map/ppermute | solution.py:537
  12.5 2.4 %collective-permute-start.3 = (bf16[768,128]{1,0:T(8,128)(2,1)S(1)}, bf16[768,128]{1,0:T(8,128)(2,1)S(1)}, u32[]{:S(2)}, u32[]{:S(2)}) collective-permute-start(bf16[768,128]{1,0:T(8,128)(2,1)S(1)} %get-tuple-element.41), channel_id=1, source_target_pairs={{0,8},{8,0},{16,24},{24,16},{1,9},{9,1},{17,25},{25,17},{2,10},{10... | collective-permute-start | bytes 589832 | tf_op jit(solution)/shard_map/ppermute | solution.py:557
  16.8 3.4 %collective-permute-start.4 = (bf16[768,128]{1,0:T(8,128)(2,1)S(1)}, bf16[768,128]{1,0:T(8,128)(2,1)S(1)}, u32[]{:S(2)}, u32[]{:S(2)}) collective-permute-start(bf16[768,128]{1,0:T(8,128)(2,1)S(1)} %shard_map.58), channel_id=1, source_target_pairs={{0,8},{8,0},{16,24},{24,16},{1,9},{9,1},{17,25},{25,17},{2,10},{10... | collective-permute-start | bytes 589832 | tf_op jit(solution)/shard_map/ppermute | solution.py:571
  21.0 7.4 %collective-permute-start.11 = (bf16[256,128]{1,0:T(8,128)(2,1)S(1)}, bf16[256,128]{1,0:T(8,128)(2,1)S(1)}, u32[]{:S(2)}, u32[]{:S(2)}) collective-permute-start(bf16[256,128]{1,0:T(8,128)(2,1)S(1)} %get-tuple-element.55), channel_id=1, source_target_pairs={{0,6},{1,7},{2,4},{3,5},{4,2},{5,3},{6,0},{7,1},{8,14},{9,15},{10,... | collective-permute-start | bytes 196616 | tf_op jit(solution)/shard_map/ppermute | solution.py:599
  24.9 7.7 %collective-permute-start.10 = (bf16[256,128]{1,0:T(8,128)(2,1)S(1)}, bf16[256,128]{1,0:T(8,128)(2,1)S(1)}, u32[]{:S(2)}, u32[]{:S(2)}) collective-permute-start(bf16[256,128]{1,0:T(8,128)(2,1)S(1)} %get-tuple-element.56), channel_id=1, source_target_pairs={{0,4},{1,5},{2,6},{3,7},{4,0},{5,1},{6,2},{7,3},{8,12},{9,13},{10,... | collective-permute-start | bytes 196616 | tf_op jit(solution)/shard_map/ppermute | solution.py:599
  24.9 16.3 %collective-permute-start.7 = (bf16[768,128]{1,0:T(8,128)(2,1)S(1)}, bf16[768,128]{1,0:T(8,128)(2,1)S(1)}, u32[]{:S(2)}, u32[]{:S(2)}) collective-permute-start(bf16[768,128]{1,0:T(8,128)(2,1)S(1)} %get-tuple-element.51), channel_id=1, source_target_pairs={{0,2},{1,3},{2,0},{3,1},{4,6},{5,7},{6,4},{7,5},{8,10},{9,11},{10,... | collective-permute-start | bytes 589832 | tf_op jit(solution)/shard_map/ppermute | solution.py:599
  25.6 15.6 %collective-permute-start.6 = (bf16[768,128]{1,0:T(8,128)(2,1)S(1)}, bf16[768,128]{1,0:T(8,128)(2,1)S(1)}, u32[]{:S(2)}, u32[]{:S(2)}) collective-permute-start(bf16[768,128]{1,0:T(8,128)(2,1)S(1)} %get-tuple-element.52), channel_id=1, source_target_pairs={{0,3},{1,2},{2,1},{3,0},{4,7},{5,6},{6,5},{7,4},{8,11},{9,10},{10,... | collective-permute-start | bytes 589832 | tf_op jit(solution)/shard_map/ppermute | solution.py:599
  27.9 13.3 %collective-permute-start.5 = (bf16[768,128]{1,0:T(8,128)(2,1)S(1)}, bf16[768,128]{1,0:T(8,128)(2,1)S(1)}, u32[]{:S(2)}, u32[]{:S(2)}) collective-permute-start(bf16[768,128]{1,0:T(8,128)(2,1)S(1)} %get-tuple-element.53), channel_id=1, source_target_pairs={{0,1},{1,0},{2,3},{3,2},{4,5},{5,4},{6,7},{7,6},{8,9},{9,8},{10,11... | collective-permute-start | bytes 589832 | tf_op jit(solution)/shard_map/ppermute | solution.py:599
  28.5 12.7 %collective-permute-start.9 = (bf16[256,128]{1,0:T(8,128)(2,1)S(1)}, bf16[256,128]{1,0:T(8,128)(2,1)S(1)}, u32[]{:S(2)}, u32[]{:S(2)}) collective-permute-start(bf16[256,128]{1,0:T(8,128)(2,1)S(1)} %get-tuple-element.57), channel_id=1, source_target_pairs={{0,7},{1,6},{2,5},{3,4},{4,3},{5,2},{6,1},{7,0},{8,15},{9,14},{10,... | collective-permute-start | bytes 196616 | tf_op jit(solution)/shard_map/ppermute | solution.py:599
  32.6 8.6 %collective-permute-start.8 = (bf16[256,128]{1,0:T(8,128)(2,1)S(1)}, bf16[256,128]{1,0:T(8,128)(2,1)S(1)}, u32[]{:S(2)}, u32[]{:S(2)}) collective-permute-start(bf16[256,128]{1,0:T(8,128)(2,1)S(1)} %get-tuple-element.58), channel_id=1, source_target_pairs={{0,5},{1,4},{2,7},{3,6},{4,1},{5,0},{6,3},{7,2},{8,13},{9,12},{10,... | collective-permute-start | bytes 196616 | tf_op jit(solution)/shard_map/ppermute | solution.py:599
